TPU v7x, 256 devices: a whole 4x4x8 slice. The times are simulated.
256 devices in a mesh: band: 4 (over y), gx: 16 (over z, core), gy: 4 (over x).
Axes of the slice: x: 4, y: 4, z: 8, core: 2. Of those that a mesh axis runs over, the one named last changes fastest.
Arguments:
- ensemble: bfloat16 [4, 16, 1408, 2560], P('band', None, ('gx', 'gy')), may hold values from -6 to 6
- spectral: bfloat16 [4, 2, 1024, 16, 256], P('band', None, 'gx', 'gy'), may hold values from -6 to 6
- band_cut: int32 [4], replicated, may hold values from 1 to 327680, as said below
Outputs:
- increment: float32 [1408, 2560], P(('gx', 'gy'), 'band')
Inputs may be any that keep to these rules, and one draw needn't show every extreme that they name: band_cut rises strictly from band to band, and the last band's value exceeds (j - 512)^2 + ky^2 for every wavenumber pair of the control fields.
All inputs are finite; a program needn't handle non-finite values.
Results may differ from a plain program's by a relative error of at most 0.0044.
Values may be sent and summed in bfloat16 or wider, within the bound.
No kernel may reach another device: no remote copies, remote signals or barrier semaphores. Data moves between devices by JAX's collectives and lax.ppermute only.
A program may use at most 64 MiB of HBM per device.

v0:
```python
import math

import jax
import jax.numpy as jnp
from jax import lax
from jax.sharding import PartitionSpec as P

NX = 2560
NY = 1408
KX = 1024
KY = 256
M = 16


def table_along_y():
    wave_y = jnp.arange(KY, dtype=jnp.int32)[:, None]
    positions = jnp.arange(NY, dtype=jnp.int32)[None, :]
    phase_angle = jnp.mod(wave_y * positions, NY).astype(jnp.float32) * (2.0 * math.pi / NY)
    return jnp.concatenate([jnp.cos(phase_angle), jnp.sin(phase_angle)], axis=1).astype(
        jnp.bfloat16
    )


def table_along_x():
    wave_x = (jnp.arange(KX, dtype=jnp.int32) - KX // 2)[:, None]
    positions = jnp.arange(NX, dtype=jnp.int32)[None, :]
    phase_angle = jnp.mod(wave_x * positions, NX).astype(jnp.float32) * (2.0 * math.pi / NX)
    return jnp.concatenate([jnp.cos(phase_angle), -jnp.sin(phase_angle)], axis=0).astype(
        jnp.bfloat16
    )


def wave_mask(first_row, wave_rows, band_limit):
    wave_x = first_row + jnp.arange(wave_rows, dtype=jnp.int32) - KX // 2
    wave_y = jnp.arange(KY, dtype=jnp.int32)
    return wave_x[:, None] ** 2 + wave_y[None, :] ** 2 < band_limit


def along_y(masked, table_y):
    product = jnp.dot(masked.reshape(-1, KY), table_y, preferred_element_type=jnp.float32)
    product = product.reshape(2, -1, 2, NY)
    real_part = product[0, :, 0] - product[1, :, 1]
    imag_part = product[0, :, 1] + product[1, :, 0]
    return jnp.stack([real_part, imag_part]).astype(jnp.bfloat16)


def body(ensemble, spectral, band_cut):
    wave_rows = spectral.shape[2]
    member_rows = spectral.shape[3]
    local_rows = ensemble.shape[2]
    band_limit = lax.dynamic_index_in_dim(band_cut, lax.axis_index("band"), 0, keepdims=False)
    whole_mask = wave_mask(0, KX, band_limit)
    norm_scale = lax.rsqrt(jnp.sum(whole_mask.astype(jnp.int32)).astype(jnp.float32))
    local_mask = wave_mask(lax.axis_index("gx") * wave_rows, wave_rows, band_limit).astype(
        jnp.bfloat16
    )
    masked = spectral[0] * local_mask[None, :, None, :]
    spectra = along_y(masked, table_along_y()).reshape(2, wave_rows, member_rows, NY)
    across_x = lax.axis_size("gx")
    across_y = lax.axis_size("gy")
    received = lax.all_to_all(
        spectra[:, None], ("gx", "gy"), split_axis=4, concat_axis=1, tiled=True
    )
    received = received.reshape(2, across_x, across_y, wave_rows, member_rows, local_rows)
    transposed = received.transpose(0, 1, 3, 2, 4, 5).reshape(2, KX, M, local_rows)
    alpha_field = (
        lax.dot_general(
            transposed.reshape(2 * KX, M * local_rows),
            table_along_x(),
            (((0,), (0,)), ((), ())),
            preferred_element_type=jnp.float32,
        )
        * norm_scale
    )
    weighted = jnp.sum(
        alpha_field.reshape(M, local_rows, NX) * ensemble[0].astype(jnp.float32), axis=0
    )
    increment = lax.psum_scatter(weighted, "band", scatter_dimension=1, tiled=True)
    return increment * (1.0 / math.sqrt(M * lax.axis_size("band")))


def solution(mesh):
    placed = (P("band", None, ("gx", "gy"), None), P("band", None, "gx", "gy", None), P())
    return jax.shard_map(
        body, mesh=mesh, in_specs=placed, out_specs=P(("gx", "gy"), "band"), check_vma=False
    )
```

profile of v0, /device:TPU:2, one launch (start us, length us, event | category | flops | bytes accessed | tf_op | source)
XLA Modules:
  0.0 149.6 jit_solution(9783943985705602236)
XLA Ops:
  6.5 6.1 %sine_convert_fusion = (bf16[256,1408]{0,1:T(8,128)(2,1)S(1)}, bf16[256,1408]{0,1:T(8,128)(2,1)S(1)}) fusion(), kind=kLoop, calls=%fused_computation.26 | loop fusion | flops 3964928 | bytes 1441792 | tf_op jit(solution)/shard_map/convert.8
  12.6 1.2 dynamic_slice.4
  13.9 0.7 fusion.22
  14.6 1.1 broadcast_multiply_fusion
  15.7 0.1 reshape.152
  15.8 0.1 pad_maximum_fusion.1
  15.9 0.9 fusion.20
  16.8 0.3 fusion.16
  17.1 0.2 stack.9
  17.3 2.3 %copy.14 = bf16[1,1,64,4,1408]{2,3,0,1,4:T(4,128)(2,1)} copy(bf16[1,1,64,4,1408]{4,3,2,1,0:T(4,128)(2,1)S(1)} %stack.9) | data formatting | bytes 1441792 | tf_op jit(solution)/shard_map/stack | solution.py:44
  19.6 0.2 stack.10
  19.7 2.3 %copy.15 = bf16[1,1,64,4,1408]{2,3,0,1,4:T(4,128)(2,1)} copy(bf16[1,1,64,4,1408]{4,3,2,1,0:T(4,128)(2,1)S(1)} %stack.10) | data formatting | bytes 1441792 | tf_op jit(solution)/shard_map/stack | solution.py:44
  22.0 4.0 %fusion.25 = bf16[1408,1,2,4,64]{4,3,2,1,0:T(4,128)(2,1)S(1)} fusion(bf16[1,1,64,4,1408]{2,3,0,1,4:T(4,128)(2,1)} %copy.15, bf16[1,1,64,4,1408]{2,3,0,1,4:T(4,128)(2,1)} %copy.14), kind=kLoop, calls=%fused_computation.45 | loop fusion | flops 720896 | bytes 2883584
  26.0 3.0 %reshape.155 = bf16[64,2,5632]{2,1,0:T(2,128)(2,1)} reshape(bf16[1408,1,2,4,64]{4,3,2,1,0:T(4,128)(2,1)S(1)} %fusion.25) | data formatting | bytes 2883584
  29.0 12.2 %all-to-all-start = ((bf16[64,2,5632]{2,1,0:T(2,128)(2,1)}), bf16[64,2,5632]{2,1,0:T(2,128)(2,1)}, u32[]{:S(2)}, u32[]{:S(2)}) async-start(bf16[64,2,5632]{2,1,0:T(2,128)(2,1)} %reshape.155), calls=%async_computation | async-start | bytes 2883584 | tf_op jit(solution)/shard_map/all_to_all | solution.py:61
  41.2 0.2 reduce-scatter.2.cloned.1.call-start
  41.4 1.5 convert_reduce_fusion
  43.5 46.6 %cosine_convert_fusion = (bf16[1024,2560]{1,0:T(8,128)(2,1)}, bf16[1024,2560]{1,0:T(8,128)(2,1)}) fusion(s32[1024]{0:T(1024)S(1)} %iota_add_fusion), kind=kLoop, calls=%fused_computation.8 | loop fusion | flops 31457280 | bytes 10489856 | tf_op jit(solution)/shard_map/convert.1
  90.1 0.0 all-to-all-done
  90.1 3.5 %reshape.156 = bf16[1408,1,2,4,64]{4,3,2,1,0:T(4,128)(2,1)S(1)} reshape(bf16[64,2,5632]{2,1,0:T(2,128)(2,1)} %all-to-all-done) | data formatting | bytes 2883584
  93.6 3.5 %copy.23 = bf16[2,16,4,64,4,22]{3,1,0,5,4,2:T(8,128)(2,1)} copy(bf16[2,16,4,64,4,22]{3,4,0,5,2,1:T(4,128)(2,1)S(1)} %bitcast.36) | data formatting | bytes 2883584 | tf_op jit(solution)/shard_map/reshape | solution.py:64
  97.1 4.1 %reshape_reshape.3 = bf16[2048,352]{0,1:T(8,128)(2,1)S(1)} reshape(bf16[2,16,64,4,4,22]{2,1,0,5,4,3:T(8,128)(2,1)} %bitcast.37) | data formatting | bytes 2883584 | tf_op jit(solution)/shard_map/reshape;reshape | solution.py:68
  101.1 7.9 %fusion.9 = f32[352,2560]{1,0:T(8,128)} fusion(bf16[2048,352]{0,1:T(8,128)(2,1)S(1)} %reshape_reshape.3, bf16[1024,2560]{1,0:T(8,128)(2,1)} %get-tuple-element.8, bf16[1024,2560]{1,0:T(8,128)(2,1)} %get-tuple-element.7, f32[]{:T(128)S(6)} %rsqrt.3), kind=kOutput, calls=%fused_computation.13 | convolution fusion | flops 3712860160 | bytes 15532036 | tf_op jit(solution)/shard_map/dot_general | solution.py:67
  109.1 0.0 copy-start
  109.1 3.7 %reshape.150 = f32[16,22,2560]{2,1,0:T(8,128)} reshape(f32[352,2560]{1,0:T(8,128)} %fusion.9) | data formatting | bytes 7208960 | tf_op jit(solution)/shard_map/reshape | solution.py:76
  112.8 0.0 copy-done
  112.8 4.0 %fusion.12 = f32[22,2560]{1,0:T(8,128)} fusion(f32[16,22,2560]{2,1,0:T(8,128)} %reshape.150, bf16[1,16,22,2560]{3,1,2,0:T(8,128)(2,1)S(1)} %copy-done), kind=kLoop, calls=%fused_computation.15 | loop fusion | flops 2647040 | bytes 5632000 | tf_op jit(solution)/shard_map/reduce_sum | solution.py:75
  116.7 0.0 reduce-scatter.2.cloned.1.call-update
  116.8 24.5 %reduce-scatter.2.cloned.1.call-done = f32[22,640]{1,0:T(8,128)} async-done(((f32[22,2560]{1,0:T(8,128)}), f32[22,640]{1,0:T(8,128)}) %reduce-scatter.2.cloned.1.call-update) | async-done | bytes 56336 | tf_op jit(solution)/shard_map/reduce_scatter | solution.py:78
  141.3 1.5 broadcast_multiply_fusion.1
  (4 shorter events, 0.0 us)
Async XLA Ops:
  29.0 61.1 %all-to-all-start = ((bf16[64,2,5632]{2,1,0:T(2,128)(2,1)}), bf16[64,2,5632]{2,1,0:T(2,128)(2,1)}, u32[]{:S(2)}, u32[]{:S(2)}) async-start(bf16[64,2,5632]{2,1,0:T(2,128)(2,1)} %reshape.155), calls=%async_computation | async-start | bytes 2883584 | tf_op jit(solution)/shard_map/all_to_all | solution.py:61
  41.2 100.1 %reduce-scatter.2.cloned.1.call-start = ((), (), s32[]{:S(2)}) async-start(), calls=%async_computation.2 | async-start | bytes 307200 | tf_op jit(solution)/shard_map/reduce_scatter | solution.py:78
  109.1 3.7 %copy-start = (bf16[1,16,22,2560]{3,1,2,0:T(8,128)(2,1)S(1)}, bf16[1,16,22,2560]{3,1,2,0:T(8,128)(2,1)}, u32[]{:S(2)}) copy-start(bf16[1,16,22,2560]{3,1,2,0:T(8,128)(2,1)} %param.3) | copy-start | bytes 5406724
Sparse Core Ops, SparseCore 0:
  116.9 24.3 reduce-scatter.1
where the time goes:
time: 150 us
  other arithmetic  65.7 us (44%)
  waiting for transfers between devices  24.6 us (16%)
  local copies, waits for them, and re-layouts  23.9 us (16%)
  between operations  14.1 us (9%)
  starting transfers between devices  12.4 us (8%)
  matrix products  8.86 us (6%)
    another operation x3, other arithmetic  52.9 us
    reduce_scatter x1, waiting for transfers between devices, body(): lax.psum_scatter(weighted, 'band', scatter_dimension=1, tiled=True)  24.5 us
    all_to_all x1, starting transfers between devices, body(): lax.all_to_all(spectra[:, None], ('gx', 'gy'), split_axis=4, concat_axis=...  12.2 us
    dot_general x1, matrix products, body(): lax.dot_general(transposed.reshape(2 * KX, M * local_rows), table_along_x...  7.91 us
    unnamed x4, local copies, waits for them, and re-layouts  6.43 us
    another operation x4, local copies, waits for them, and re-layouts, along_y(): return jnp.stack([real_part, imag_part]).astype(jnp.bfloat16)  4.91 us
    another operation x1, local copies, waits for them, and re-layouts, body(): transposed.reshape(2 * KX, M * local_rows)  4.06 us
    unnamed x1, other arithmetic  3.99 us
  transfers between devices with their start and end apart: 2, of which 1 were waited for; matrix products, arithmetic and copies ran while one was open for 32% of the time, Pallas kernels for 0%

commit v1 on v0

v1 whole, which is shorter than its diff:
```python
import functools
import math

import jax
import jax.numpy as jnp
import ml_dtypes
import numpy as np
from jax import lax
from jax.experimental import pallas as pl
from jax.experimental.pallas import tpu as pltpu
from jax.sharding import PartitionSpec as P

NX = 2560
NY = 1408
KX = 1024
KY = 256
M = 16
BANDS = 4
GX = 16
GY = 4
DESTS = GX * GY
ROWS = NY // DESTS
PAD = 24
WAVES = KX // GX
HALF = WAVES // 2
MEMBERS = M // GY
CHUNK = NX // BANDS
SCRATCH = 16 * 1024 * 1024
OWN_FLOPS = 10 ** 10
ROWS_FLOPS = 2 * 10 ** 10


def low(array):
    return np.asarray(array, dtype=np.float64).astype(ml_dtypes.bfloat16)


def trig(wave, position, period):
    angle = np.mod(np.multiply.outer(wave, position), period) * (2.0 * math.pi / period)
    return np.cos(angle), np.sin(angle)


def first_wave(block):
    return WAVES * (block - GX // 2) if block >= GX // 2 else WAVES * (GX // 2 - 1 - block) + HALF


@functools.lru_cache(None)
def fold_tables():
    fold = np.zeros((2, 2, MEMBERS, HALF, (WAVES + HALF) * MEMBERS))
    for member in range(MEMBERS):
        for pair in range(HALF):
            own = MEMBERS * pair + member
            for part, sign in ((0, 1.0), (1, -1.0)):
                fold[0, part, member, pair, own] = 1.0
                if pair > 0:
                    fold[0, part, member, pair, MEMBERS * (WAVES + HALF - pair) + member] = sign
                fold[1, part, member, pair, MEMBERS * WAVES + own] = 1.0
                fold[1, part, member, pair, MEMBERS * (HALF - pair) + member] = sign
    return low(fold.reshape(2, 2 * MEMBERS * HALF, (WAVES + HALF) * MEMBERS))


@functools.lru_cache(None)
def row_tables():
    cosine, sine = trig(np.arange(NY), np.arange(KY), NY)
    table = np.zeros((DESTS, PAD, 2 * KY + 128))
    table[:, :ROWS, :KY] = cosine.reshape(DESTS, ROWS, KY)
    table[:, :ROWS, KY : 2 * KY] = sine.reshape(DESTS, ROWS, KY)
    table[np.arange(DESTS), ROWS, 2 * KY + np.arange(DESTS)] = 1.0
    coarse = np.zeros((128, 2 * KY))
    coarse[:DESTS] = np.concatenate(trig(np.arange(DESTS) * ROWS, np.arange(KY), NY), axis=1)
    fine = np.stack(trig(np.arange(32), np.arange(KY), NY)).astype(np.float32)
    return low(table.reshape(DESTS * PAD, -1)), low(coarse), fine


@functools.lru_cache(None)
def column_tables():
    waves = np.concatenate([first_wave(block) + np.arange(HALF) for block in range(GX)])
    cosine, sine = trig(waves, np.arange(NX), NX)
    extra = np.repeat(KX // 2 - WAVES * np.arange(GX // 2), GY)
    extra_cosine, extra_sine = trig(extra, np.arange(NX), NX)
    return low(np.concatenate([cosine, -sine, extra_cosine, extra_sine, np.zeros((64, NX))]))


@functools.lru_cache(None)
def order_tables():
    lanes = np.arange(512)
    lane_order = np.zeros((512, 512))
    block, member, pair = lanes // 128, lanes // 32 % 4, lanes % 32
    lane_order[lanes, member * 128 + block * 32 + pair] = 1.0
    row_order = np.zeros((ROWS, GY, MEMBERS, MEMBERS, GY, PAD))
    pick = np.zeros((ROWS, GY, MEMBERS, 2, MEMBERS, 32))
    same = np.zeros((ROWS, GY, MEMBERS, 128))
    for row in range(ROWS):
        for column in range(GY):
            for member in range(MEMBERS):
                row_order[row, column, member, member, column, row] = 1.0
                pick[row, column, member, :, member, row] = 1.0
                same[row, column, member, column:64:GY] = 1.0
    gather = np.zeros((128, DESTS // 2, PAD))
    lane_part = np.zeros((128, 256))
    for slot in range(64):
        gather[slot, slot % 32, ROWS] = 1.0
        lane_part[slot, slot // 32 * 128 : slot // 32 * 128 + 128] = 1.0
    return (
        low(lane_order),
        low(row_order.reshape(ROWS * M, MEMBERS * GY * PAD)),
        low(pick.reshape(ROWS * M, 256)),
        same.reshape(ROWS * M, 128).astype(np.float32),
        low(gather.reshape(128, DESTS // 2 * PAD)),
        lane_part.astype(np.float32),
    )


def nn(a, b):
    return jnp.dot(a, b, preferred_element_type=jnp.float32)


def nt(a, b):
    return lax.dot_general(a, b, (((1,), (1,)), ((), ())), preferred_element_type=jnp.float32)


def place(block, rows):
    negative = (block < GX // 2).astype(jnp.int32)
    return negative, jnp.where(negative == 1, WAVES * (GX // 2 - 1 - block), WAVES * (block - GX // 2))


def pair_mask(base, negative, cut):
    shape = (2 * MEMBERS * HALF, KY)
    wave = base + HALF * negative + (lax.broadcasted_iota(jnp.int32, shape, 0) & (HALF - 1))
    wave_y = lax.broadcasted_iota(jnp.int32, shape, 1)
    return wave * wave + wave_y * wave_y < cut


def own_kernel(cut_ref, own_ref, fold_ref, coarse_ref, fine_ref, folded_ref, extra_ref, scale_ref):
    block = lax.axis_index("gx")
    cut = cut_ref[lax.axis_index("band")]
    negative, base = place(block, WAVES)
    fold = fold_ref[negative, :, : WAVES * MEMBERS]
    inside = pair_mask(base, negative, cut)
    for part in range(2):
        folded_ref[part] = jnp.where(inside, nn(fold, own_ref[part]), 0.0)

    wave_y = lax.broadcasted_iota(jnp.int32, (MEMBERS, KY), 1)
    last = base + WAVES
    edge = last * last + wave_y * wave_y < cut
    edge_real = jnp.where(edge, own_ref[0, :16].astype(jnp.float32)[:MEMBERS], 0.0)
    edge_imag = jnp.where(edge, own_ref[1, :16].astype(jnp.float32)[:MEMBERS], 0.0)
    cosine, sine = fine_ref[0], fine_ref[1]
    even = jnp.concatenate(
        [edge_real[m : m + 1] * cosine - edge_imag[m : m + 1] * sine for m in range(MEMBERS)], axis=0
    )
    odd = jnp.concatenate(
        [edge_real[m : m + 1] * sine + edge_imag[m : m + 1] * cosine for m in range(MEMBERS)], axis=0
    )
    turned = jnp.concatenate(
        [jnp.concatenate([even, -odd], axis=1), jnp.concatenate([odd, even], axis=1)], axis=0
    ).astype(jnp.bfloat16)
    extra_ref[...] = nt(turned, coarse_ref[...]).astype(jnp.bfloat16)

    shape = (KX, KY)
    wave_x = lax.broadcasted_iota(jnp.int32, shape, 0) - KX // 2
    wave_y = lax.broadcasted_iota(jnp.int32, shape, 1)
    inside = (wave_x * wave_x + wave_y * wave_y < cut).astype(jnp.float32)
    count = jnp.sum(jnp.sum(inside.reshape(KX // 8, 8, KY), axis=0))
    scale_ref[...] = lax.rsqrt(jnp.full((8, 128), count)) * (1.0 / math.sqrt(M * BANDS))


def rows_kernel(cut_ref, folded_ref, extra_ref, mirror_ref, fold_ref, table_ref, out_ref):
    cut = cut_ref[lax.axis_index("band")]
    negative, base = place(lax.axis_index("gx"), WAVES)
    fold = fold_ref[negative, :, WAVES * MEMBERS :]
    inside = pair_mask(base, negative, cut)
    real = folded_ref[0] + jnp.where(inside, nn(fold, mirror_ref[0]), 0.0)
    imag = folded_ref[1] + jnp.where(inside, nn(fold, mirror_ref[1]), 0.0)
    half = MEMBERS * HALF
    with_cosine = jnp.concatenate([real[:half], imag[half:]], axis=0)
    with_sine = jnp.concatenate([-imag[:half], real[half:]], axis=0)
    weights = jnp.concatenate([with_cosine, with_sine], axis=1).astype(jnp.bfloat16)
    weights = jnp.concatenate([weights, extra_ref[...]], axis=1)
    for part in range(4):
        rows = pl.ds(part * 384, 384)
        out_ref[rows, :] = nt(table_ref[rows, :], weights).astype(jnp.bfloat16)


def field_kernel(
    scale_ref, got_ref, ensemble_ref, table_ref, lane_ref, row_ref, pick_ref, same_ref, gather_ref, part_ref, *rest
):
    outs, joined = rest[:BANDS], rest[BANDS]
    span = GY * PAD
    groups = []
    for part in range(2):
        for high in range(4):
            groups.append(
                jnp.concatenate(
                    [
                        got_ref[(4 * high + least) * span : (4 * high + least + 1) * span, part * 128 : part * 128 + 128]
                        for least in range(4)
                    ],
                    axis=1,
                )
            )
    ordered = nn(jnp.concatenate(groups, axis=0), lane_ref[...]).astype(jnp.bfloat16)
    members = [
        jnp.concatenate(
            [ordered[group * span : (group + 1) * span, m * 128 : m * 128 + 128] for group in range(8)], axis=1
        )
        for m in range(MEMBERS)
    ]
    joined[:, : 2 * KX // 2] = nn(row_ref[...], jnp.concatenate(members, axis=0)).astype(jnp.bfloat16)
    edge = nn(gather_ref[...], got_ref[: DESTS // 2 * PAD, :]) * part_ref[...]
    joined[:, KX:] = (nt(pick_ref[...], edge.astype(jnp.bfloat16)) * same_ref[...]).astype(jnp.bfloat16)
    scale = scale_ref[:1, :1]
    band = lax.axis_index("band")
    for step in range(BANDS):
        start = pl.multiple_of(lax.rem(band + step, BANDS) * CHUNK, CHUNK)
        columns = pl.ds(start, CHUNK)
        alpha = nn(joined[...], table_ref[:, columns]).reshape(ROWS, M, CHUNK)
        weighted = alpha * ensemble_ref[:, :, columns].astype(jnp.float32)
        outs[step][...] = jnp.sum(weighted, axis=1) * scale


def whole(count):
    return [pl.BlockSpec(memory_space=pltpu.VMEM) for _ in range(count)]


def body(ensemble, spectral, band_cut):
    own = spectral[0].reshape(2, WAVES * MEMBERS, KY)
    mirror = lax.ppermute(own[:, HALF * MEMBERS :], "gx", [(i, GX - 1 - i) for i in range(GX)])
    table_y, coarse, fine = row_tables()
    smem = pl.BlockSpec(memory_space=pltpu.SMEM)
    folded, extra, scale = pl.pallas_call(
        own_kernel,
        out_shape=[
            jax.ShapeDtypeStruct((2, 256, KY), jnp.float32),
            jax.ShapeDtypeStruct((256, 128), jnp.bfloat16),
            jax.ShapeDtypeStruct((8, 128), jnp.float32),
        ],
        in_specs=[smem] + whole(4),
        out_specs=whole(3),
        compiler_params=pltpu.CompilerParams(vmem_limit_bytes=SCRATCH),
        cost_estimate=pl.CostEstimate(flops=OWN_FLOPS, bytes_accessed=1 << 20, transcendentals=0),
        name="own_kernel",
    )(band_cut, own, fold_tables(), coarse, fine)
    rows = pl.pallas_call(
        rows_kernel,
        out_shape=jax.ShapeDtypeStruct((DESTS * PAD, 256), jnp.bfloat16),
        in_specs=[smem] + whole(5),
        out_specs=pl.BlockSpec(memory_space=pltpu.VMEM),
        compiler_params=pltpu.CompilerParams(vmem_limit_bytes=SCRATCH),
        cost_estimate=pl.CostEstimate(flops=ROWS_FLOPS, bytes_accessed=4 << 20, transcendentals=0),
        name="rows_kernel",
    )(band_cut, folded, extra, mirror, fold_tables(), table_y)
    got = lax.all_to_all(rows, ("gx", "gy"), split_axis=0, concat_axis=0, tiled=True)
    pieces = pl.pallas_call(
        field_kernel,
        out_shape=[jax.ShapeDtypeStruct((ROWS, CHUNK), jnp.float32)] * BANDS,
        in_specs=whole(10),
        out_specs=whole(BANDS),
        scratch_shapes=[pltpu.VMEM((ROWS * M, KX + 128), jnp.bfloat16)],
        compiler_params=pltpu.CompilerParams(vmem_limit_bytes=SCRATCH),
        cost_estimate=pl.CostEstimate(flops=3 << 30, bytes_accessed=16 << 20, transcendentals=0),
        name="field_kernel",
    )(scale, got, ensemble[0].transpose(1, 0, 2), column_tables(), *order_tables())
    total = pieces[0]
    for step in range(1, BANDS):
        total = total + lax.ppermute(pieces[step], "band", [(i, (i + step) % BANDS) for i in range(BANDS)])
    return total


def solution(mesh):
    placed = (P("band", None, ("gx", "gy"), None), P("band", None, "gx", "gy", None), P())
    return jax.shard_map(
        body, mesh=mesh, in_specs=placed, out_specs=P(("gx", "gy"), "band"), check_vma=False
    )
```

time: 150 us -> 61.3 us (0.41)
  other arithmetic: 65.7 us -> 0.64 us
  blocking collectives: 0 us -> 32.8 us
  waiting for transfers between devices: 24.6 us -> 5.14 us
  local copies, waits for them, and re-layouts: 23.9 us -> 4.47 us
  between operations: 14.1 us -> 0.15 us
  matrix products: 8.86 us -> 0 us
  Pallas kernels: 0 us -> 6.58 us
    another operation x3 -> x0, other arithmetic: 52.9 us -> none
    all_to_all x0 -> x1, blocking collectives: none -> 32.8 us  [body(): lax.all_to_all(rows, ('gx', 'gy'), split_axis=0, concat_axis=0, tiled=True)]
    reduce_scatter x1 -> x0, waiting for transfers between devices: 24.5 us -> none  [body(): lax.psum_scatter(weighted, 'band', scatter_dimension=1, tiled=True)]
    all_to_all x1 -> x0, starting transfers between devices: 12.2 us -> none  [body(): lax.all_to_all(spectra[:, None], ('gx', 'gy'), split_axis=4, concat_axis=...]
    ppermute x0 -> x4, starting transfers between devices: none -> 11.3 us  [the longest x3 5.91 us: body(): lax.ppermute(pieces[step], 'band', [(i, (i + step) % BANDS) for i in rang...]
    dot_general x2 -> x0, matrix products: 8.86 us -> none  [the longest x1 7.91 us: body(): lax.dot_general(transposed.reshape(2 * KX, M * local_rows), table_along_x...]
    another operation x5 -> x1, local copies, waits for them, and re-layouts: 8.97 us -> 1.01 us  [body(): own = spectral[0].reshape(2, WAVES * MEMBERS, KY)]
    reshape x2 -> x0, local copies, waits for them, and re-layouts: 7.22 us -> none  [the longest x1 3.7 us: body(): alpha_field.reshape(M, local_rows, NX) * ensemble[0].astype(jnp.float32)]
  transfers between devices with their start and end apart: 2 -> 4, of which waited for: 1 -> 3; matrix products, arithmetic and copies ran while one was open for 32% -> 0% of each run, Pallas kernels for 0% -> 2%
where the time goes in v1:
time: 61.3 us; the launch traced here: 61.1 us
  blocking collectives  32.8 us (54%)
  starting transfers between devices  11.3 us (18%)
  Pallas kernels  6.58 us (11%)
  waiting for transfers between devices  5.14 us (8%)
  local copies, waits for them, and re-layouts  4.47 us (7%)
  other arithmetic  0.64 us (1%)
    all_to_all x1, blocking collectives, body(): lax.all_to_all(rows, ('gx', 'gy'), split_axis=0, concat_axis=0, tiled=True)  32.8 us
    ppermute x3, starting transfers between devices, body(): lax.ppermute(pieces[step], 'band', [(i, (i + step) % BANDS) for i in rang...  5.91 us
    ppermute x1, starting transfers between devices, body(): lax.ppermute(own[:, HALF * MEMBERS:], 'gx', [(i, GX - 1 - i) for i in ran...  5.38 us
    pallas_call x1, Pallas kernels, body(): pl.pallas_call(field_kernel, out_shape=[jax.ShapeDtypeStruct((ROWS, CHUNK...  4.05 us
    unnamed x28, local copies, waits for them, and re-layouts  3.45 us
    ppermute x3, waiting for transfers between devices, body(): lax.ppermute(pieces[step], 'band', [(i, (i + step) % BANDS) for i in rang...  2.87 us
    ppermute x1, waiting for transfers between devices, body(): lax.ppermute(own[:, HALF * MEMBERS:], 'gx', [(i, GX - 1 - i) for i in ran...  2.27 us
    pallas_call x1, Pallas kernels, body(): pl.pallas_call(rows_kernel, out_shape=jax.ShapeDtypeStruct((DESTS * PAD,...  1.5 us
  transfers between devices with their start and end apart: 4, of which 3 were waited for; matrix products, arithmetic and copies ran while one was open for 0% of the time, Pallas kernels for 2%

profile of v1, /device:TPU:2, one launch (start us, length us, event | category | flops | bytes accessed | tf_op | source)
XLA Modules:
  0.0 61.1 jit_solution(15211303309403009181)
XLA Ops:
  0.0 1.0 %reshape_squeeze.3.own_ref = bf16[2,256,256]{2,1,0:T(8,128)(2,1)S(1)} reshape(bf16[1,2,64,4,256]{4,3,2,1,0:T(4,128)(2,1)} %param.15) | data formatting | bytes 524288 | tf_op jit(solution)/shard_map/reshape;squeeze | solution.py:226
  1.0 5.4 %collective-permute-start = (bf16[2,128,256]{2,1,0:T(8,128)(2,1)S(1)}, bf16[2,128,256]{2,1,0:T(8,128)(2,1)S(1)}, u32[]{:S(2)}, u32[]{:S(2)}) collective-permute-start(bf16[2,128,256]{2,1,0:T(8,128)(2,1)S(1)} %slice.4), channel_id=1, source_target_pairs={{0,60},{4,56},{8,52},{12,48},{16,44},{20,40},{24,36},{28,32},{32,2... | collective-permute-start | bytes 393224 | tf_op jit(solution)/shard_map/ppermute | solution.py:227
  6.4 0.7 %copy-done.1 = s32[4]{0:T(128)S(1)} copy-done((s32[4]{0:T(128)S(1)}, s32[4]{0:T(128)}, u32[]{:S(2)}) %copy-start.1) | copy-done | bytes 40
  7.1 1.0 %copy-done.4 = bf16[2,256,384]{2,1,0:T(8,128)(2,1)S(1)} copy-done((bf16[2,256,384]{2,1,0:T(8,128)(2,1)S(1)}, bf16[2,256,384]{2,1,0:T(8,128)(2,1)}, u32[]{:S(2)}) %copy-start.4) | copy-done | bytes 393240
  8.1 0.9 %copy-done.10 = bf16[128,512]{1,0:T(8,128)(2,1)S(1)} copy-done((bf16[128,512]{1,0:T(8,128)(2,1)S(1)}, bf16[128,512]{1,0:T(8,128)(2,1)}, u32[]{:S(2)}) %copy-start.10) | copy-done | bytes 131096
  9.0 0.8 %copy-done.11 = f32[2,32,256]{2,1,0:T(8,128)S(1)} copy-done((f32[2,32,256]{2,1,0:T(8,128)S(1)}, f32[2,32,256]{2,1,0:T(8,128)}, u32[]{:S(2)}) %copy-start.11) | copy-done | bytes 65560
  9.8 1.0 %own_kernel.1 = (f32[2,256,256]{2,1,0:T(8,128)S(1)}, bf16[256,128]{1,0:T(8,128)(2,1)S(1)}, f32[8,128]{1,0:T(8,128)S(1)}) custom-call(s32[4]{0:T(128)S(1)} %copy-done.1, bf16[2,256,256]{2,1,0:T(8,128)(2,1)S(1)} %reshape_squeeze.3.own_ref, bf16[2,256,384]{2,1,0:T(8,128)(2,1)S(1)} %copy-done.4, bf16[128,512]{1,0:T(8,128)(2,1)S(1)} %copy-done.10, ...), custom_call_target="tpu_custom_call" | custom-call | flops 10000000000 | bytes 1048576 | tf_op jit(solution)/shard_map/own_kernel/pallas_call | solution.py:230
  10.8 2.3 %collective-permute-done.mirror_ref = bf16[2,128,256]{2,1,0:T(8,128)(2,1)S(1)} collective-permute-done((bf16[2,128,256]{2,1,0:T(8,128)(2,1)S(1)}, bf16[2,128,256]{2,1,0:T(8,128)(2,1)S(1)}, u32[]{:S(2)}, u32[]{:S(2)}) %collective-permute-start) | collective-permute-done | bytes 131104 | tf_op jit(solution)/shard_map/ppermute | solution.py:227
  13.1 0.0 copy-done.2
  13.1 0.0 copy-start.5
  13.1 0.0 copy-start.6
  13.2 0.0 copy-start.7
  13.2 0.0 copy-start.8
  13.2 0.0 copy-start.9
  13.2 1.5 %rows_kernel.1 = bf16[1536,256]{1,0:T(8,128)(2,1)S(1)} custom-call(s32[4]{0:T(128)S(1)} %copy-done.1, f32[2,256,256]{2,1,0:T(8,128)S(1)} %get-tuple-element.13.folded_ref, bf16[256,128]{1,0:T(8,128)(2,1)S(1)} %get-tuple-element.14.extra_ref, bf16[2,128,256]{2,1,0:T(8,128)(2,1)S(1)} %collective-permute-done.mirror_ref, bf16[2,256,384]{2,1,0:T(8,128)(2,1)S(1)} %copy-done.4, ...), custom_call_target="tpu_custom_call" | custom-call | flops 20000000000 | bytes 4194304 | tf_op jit(solution)/shard_map/rows_kernel/pallas_call | solution.py:243
  14.7 32.8 %all_to_all.11 = bf16[64,24,256]{2,1,0:T(8,128)(2,1)S(1)} all-to-all(bf16[64,24,256]{2,1,0:T(8,128)(2,1)S(1)} %bitcast.6), channel_id=1, replica_groups=mesh['band'=4,'gx'=16,'gy'=4] {'gx','gy'}, dimensions={0} | all-to-all | bytes 1572864 | tf_op jit(solution)/shard_map/all_to_all | solution.py:252
  47.5 0.0 slice-done
  47.5 0.0 copy-done
  47.5 0.0 copy-done.3
  47.5 0.0 copy-done.5
  47.5 0.0 copy-done.6
  47.5 0.0 copy-done.7
  47.5 0.0 copy-done.8
  47.6 0.0 copy-done.9
  47.6 4.1 %field_kernel.1 = (f32[22,640]{1,0:T(8,128)S(1)}, f32[22,640]{1,0:T(8,128)S(1)}, f32[22,640]{1,0:T(8,128)S(1)}, f32[22,640]{1,0:T(8,128)S(1)}) custom-call(f32[8,128]{1,0:T(8,128)S(1)} %get-tuple-element.12.scale_ref, bf16[1536,256]{1,0:T(8,128)(2,1)S(1)} %bitcast.5, bf16[22,16,2560]{2,1,0:T(8,128)(2,1)S(1)} %bitcast.7, bf16[1152,2560]{1,0:T(8,128)(2,1)S(1)} %bitcast.9, ...), custom_call_target="tpu_custom_call" | custom-call | flops 3221225472 | bytes 16777216 | tf_op jit(solution)/shard_map/field_kernel/pallas_call | solution.py:253
  51.6 1.7 %collective-permute-start.1 = (f32[22,640]{1,0:T(8,128)S(1)}, f32[22,640]{1,0:T(8,128)S(1)}, u32[]{:S(2)}, u32[]{:S(2)}) collective-permute-start(f32[22,640]{1,0:T(8,128)S(1)} %get-tuple-element.16), channel_id=1, source_target_pairs={{0,64},{64,128},{128,192},{192,0},{1,65},{65,129},{129,193},{193,1... | collective-permute-start | bytes 168968 | tf_op jit(solution)/shard_map/ppermute | solution.py:265
  53.3 2.9 %collective-permute-start.2 = (f32[22,640]{1,0:T(8,128)S(1)}, f32[22,640]{1,0:T(8,128)S(1)}, u32[]{:S(2)}, u32[]{:S(2)}) collective-permute-start(f32[22,640]{1,0:T(8,128)S(1)} %get-tuple-element.17), channel_id=1, source_target_pairs={{0,128},{64,192},{128,0},{192,64},{1,129},{65,193},{129,1},{193,65... | collective-permute-start | bytes 168968 | tf_op jit(solution)/shard_map/ppermute | solution.py:265
  56.2 1.3 %collective-permute-start.3 = (f32[22,640]{1,0:T(8,128)S(1)}, f32[22,640]{1,0:T(8,128)S(1)}, u32[]{:S(2)}, u32[]{:S(2)}) collective-permute-start(f32[22,640]{1,0:T(8,128)S(1)} %get-tuple-element.18), channel_id=1, source_target_pairs={{0,192},{64,0},{128,64},{192,128},{1,193},{65,1},{129,65},{193,129... | collective-permute-start | bytes 168968 | tf_op jit(solution)/shard_map/ppermute | solution.py:265
  57.6 0.0 collective-permute-done.1
  57.6 1.5 %collective-permute-done.2 = f32[22,640]{1,0:T(8,128)S(1)} collective-permute-done((f32[22,640]{1,0:T(8,128)S(1)}, f32[22,640]{1,0:T(8,128)S(1)}, u32[]{:S(2)}, u32[]{:S(2)}) %collective-permute-start.2) | collective-permute-done | bytes 56352 | tf_op jit(solution)/shard_map/ppermute | solution.py:265
  59.1 1.4 %collective-permute-done.3 = f32[22,640]{1,0:T(8,128)S(1)} collective-permute-done((f32[22,640]{1,0:T(8,128)S(1)}, f32[22,640]{1,0:T(8,128)S(1)}, u32[]{:S(2)}, u32[]{:S(2)}) %collective-permute-start.3) | collective-permute-done | bytes 56352 | tf_op jit(solution)/shard_map/ppermute | solution.py:265
  60.4 0.6 %add_add_fusion = f32[22,640]{1,0:T(8,128)} fusion(f32[22,640]{1,0:T(8,128)S(1)} %collective-permute-done.3, f32[22,640]{1,0:T(8,128)S(1)} %collective-permute-done.2, f32[22,640]{1,0:T(8,128)S(1)} %get-tuple-element.15, f32[22,640]{1,0:T(8,128)S(1)} %collective-permute-done.1), kind=kLoop, calls=%fused_computation | loop fusion | flops 42240 | bytes 281600 | tf_op jit(solution)/shard_map/add | solution.py:265
  (12 shorter events, 0.0 us)
Async XLA Ops:
  1.0 12.1 %collective-permute-start = (bf16[2,128,256]{2,1,0:T(8,128)(2,1)S(1)}, bf16[2,128,256]{2,1,0:T(8,128)(2,1)S(1)}, u32[]{:S(2)}, u32[]{:S(2)}) collective-permute-start(bf16[2,128,256]{2,1,0:T(8,128)(2,1)S(1)} %slice.4), channel_id=1, source_target_pairs={{0,60},{4,56},{8,52},{12,48},{16,44},{20,40},{24,36},{28,32},{32,2... | collective-permute-start | bytes 393224 | tf_op jit(solution)/shard_map/ppermute | solution.py:227
  6.4 0.7 %copy-start.1 = (s32[4]{0:T(128)S(1)}, s32[4]{0:T(128)}, u32[]{:S(2)}) copy-start(s32[4]{0:T(128)} %cut_ref.3) | copy-start | bytes 52
  7.1 1.0 %copy-start.4 = (bf16[2,256,384]{2,1,0:T(8,128)(2,1)S(1)}, bf16[2,256,384]{2,1,0:T(8,128)(2,1)}, u32[]{:S(2)}) copy-start(bf16[2,256,384]{2,1,0:T(8,128)(2,1)} %constant.22.clone.fold_ref) | copy-start | bytes 1179652
  8.1 0.9 %copy-start.10 = (bf16[128,512]{1,0:T(8,128)(2,1)S(1)}, bf16[128,512]{1,0:T(8,128)(2,1)}, u32[]{:S(2)}) copy-start(bf16[128,512]{1,0:T(8,128)(2,1)} %constant.23.clone.coarse_ref) | copy-start | bytes 393220
  9.0 0.8 %copy-start.11 = (f32[2,32,256]{2,1,0:T(8,128)S(1)}, f32[2,32,256]{2,1,0:T(8,128)}, u32[]{:S(2)}) copy-start(f32[2,32,256]{2,1,0:T(8,128)} %constant.24.clone.fine_ref) | copy-start | bytes 196612
  9.8 3.3 %copy-start.2 = (bf16[1536,640]{1,0:T(8,128)(2,1)S(1)}, bf16[1536,640]{1,0:T(8,128)(2,1)}, u32[]{:S(2)}) copy-start(bf16[1536,640]{1,0:T(8,128)(2,1)} %constant.25.clone.table_ref) | copy-start | bytes 5898244
  9.8 37.7 %slice-start = ((s8[5898240]{0:T(1024)(128)(4,1)}), s8[4194304]{0:T(1024)(128)(4,1)S(1)}, s32[]{:S(2)}) async-start(s8[5898240]{0:T(1024)(128)(4,1)} %bitcast.8), calls=%async_computation.1 | async-start | bytes 8388608
  13.1 34.4 %copy-start = (bf16[1,16,22,2560]{3,1,2,0:T(8,128)(2,1)S(1)}, bf16[1,16,22,2560]{3,1,2,0:T(8,128)(2,1)}, u32[]{:S(2)}) copy-start(bf16[1,16,22,2560]{3,1,2,0:T(8,128)(2,1)} %param.14) | copy-start | bytes 5406724
  13.1 34.4 %slice-start.1 = ((s8[5898240]{0:T(1024)(128)(4,1)}), s8[1703936]{0:T(1024)(128)(4,1)S(1)}, s32[]{:S(2)}) async-start(s8[5898240]{0:T(1024)(128)(4,1)} %bitcast.8), calls=%async_computation.2 | async-start | bytes 3407872
  13.1 34.4 %copy-start.3 = (bf16[512,512]{1,0:T(8,128)(2,1)S(1)}, bf16[512,512]{1,0:T(8,128)(2,1)}, u32[]{:S(2)}) copy-start(bf16[512,512]{1,0:T(8,128)(2,1)} %constant.27.clone.lane_ref) | copy-start | bytes 1572868
  13.1 34.4 %copy-start.5 = (bf16[352,384]{1,0:T(8,128)(2,1)S(1)}, bf16[352,384]{1,0:T(8,128)(2,1)}, u32[]{:S(2)}) copy-start(bf16[352,384]{1,0:T(8,128)(2,1)} %constant.28.clone.row_ref) | copy-start | bytes 811012
  13.1 34.4 %copy-start.6 = (bf16[128,768]{1,0:T(8,128)(2,1)S(1)}, bf16[128,768]{1,0:T(8,128)(2,1)}, u32[]{:S(2)}) copy-start(bf16[128,768]{1,0:T(8,128)(2,1)} %constant.31.clone.gather_ref) | copy-start | bytes 589828
  13.2 34.4 %copy-start.7 = (f32[352,128]{1,0:T(8,128)S(1)}, f32[352,128]{1,0:T(8,128)}, u32[]{:S(2)}) copy-start(f32[352,128]{1,0:T(8,128)} %constant.30.clone.same_ref) | copy-start | bytes 540676
  13.2 34.4 %copy-start.8 = (bf16[352,256]{1,0:T(8,128)(2,1)S(1)}, bf16[352,256]{1,0:T(8,128)(2,1)}, u32[]{:S(2)}) copy-start(bf16[352,256]{1,0:T(8,128)(2,1)} %constant.29.clone.pick_ref) | copy-start | bytes 540676
  13.2 34.4 %copy-start.9 = (f32[128,256]{1,0:T(8,128)S(1)}, f32[128,256]{1,0:T(8,128)}, u32[]{:S(2)}) copy-start(f32[128,256]{1,0:T(8,128)} %constant.32.clone.part_ref) | copy-start | bytes 393220
  51.6 5.9 %collective-permute-start.1 = (f32[22,640]{1,0:T(8,128)S(1)}, f32[22,640]{1,0:T(8,128)S(1)}, u32[]{:S(2)}, u32[]{:S(2)}) collective-permute-start(f32[22,640]{1,0:T(8,128)S(1)} %get-tuple-element.16), channel_id=1, source_target_pairs={{0,64},{64,128},{128,192},{192,0},{1,65},{65,129},{129,193},{193,1... | collective-permute-start | bytes 168968 | tf_op jit(solution)/shard_map/ppermute | solution.py:265
  53.3 5.8 %collective-permute-start.2 = (f32[22,640]{1,0:T(8,128)S(1)}, f32[22,640]{1,0:T(8,128)S(1)}, u32[]{:S(2)}, u32[]{:S(2)}) collective-permute-start(f32[22,640]{1,0:T(8,128)S(1)} %get-tuple-element.17), channel_id=1, source_target_pairs={{0,128},{64,192},{128,0},{192,64},{1,129},{65,193},{129,1},{193,65... | collective-permute-start | bytes 168968 | tf_op jit(solution)/shard_map/ppermute | solution.py:265
  56.2 4.2 %collective-permute-start.3 = (f32[22,640]{1,0:T(8,128)S(1)}, f32[22,640]{1,0:T(8,128)S(1)}, u32[]{:S(2)}, u32[]{:S(2)}) collective-permute-start(f32[22,640]{1,0:T(8,128)S(1)} %get-tuple-element.18), channel_id=1, source_target_pairs={{0,192},{64,0},{128,64},{192,128},{1,193},{65,1},{129,65},{193,129... | collective-permute-start | bytes 168968 | tf_op jit(solution)/shard_map/ppermute | solution.py:265

commit v2 on v1

--- a/solution.py
+++ b/solution.py
@@ -27,6 +27,7 @@
 CHUNK = NX // BANDS
 SCRATCH = 16 * 1024 * 1024
 OWN_FLOPS = 10 ** 10
+NEAR_FLOPS = 10 ** 10
 ROWS_FLOPS = 2 * 10 ** 10
 
 
@@ -61,23 +62,23 @@
 @functools.lru_cache(None)
 def row_tables():
     cosine, sine = trig(np.arange(NY), np.arange(KY), NY)
-    table = np.zeros((DESTS, PAD, 2 * KY + 128))
-    table[:, :ROWS, :KY] = cosine.reshape(DESTS, ROWS, KY)
-    table[:, :ROWS, KY : 2 * KY] = sine.reshape(DESTS, ROWS, KY)
-    table[np.arange(DESTS), ROWS, 2 * KY + np.arange(DESTS)] = 1.0
-    coarse = np.zeros((128, 2 * KY))
-    coarse[:DESTS] = np.concatenate(trig(np.arange(DESTS) * ROWS, np.arange(KY), NY), axis=1)
+    table = np.zeros((GX, GY, PAD, 2 * KY))
+    table[:, :, :ROWS] = np.concatenate([cosine, sine], axis=1).reshape(GX, GY, ROWS, 2 * KY)
+    firsts = np.arange(DESTS).reshape(GX, GY).T.reshape(-1) * ROWS
+    coarse = np.concatenate(trig(firsts, np.arange(KY), NY), axis=1)
     fine = np.stack(trig(np.arange(32), np.arange(KY), NY)).astype(np.float32)
-    return low(table.reshape(DESTS * PAD, -1)), low(coarse), fine
+    return low(table.transpose(1, 0, 2, 3).reshape(DESTS * PAD, 2 * KY)), low(coarse), fine
 
 
 @functools.lru_cache(None)
 def column_tables():
-    waves = np.concatenate([first_wave(block) + np.arange(HALF) for block in range(GX)])
-    cosine, sine = trig(waves, np.arange(NX), NX)
-    extra = np.repeat(KX // 2 - WAVES * np.arange(GX // 2), GY)
-    extra_cosine, extra_sine = trig(extra, np.arange(NX), NX)
-    return low(np.concatenate([cosine, -sine, extra_cosine, extra_sine, np.zeros((64, NX))]))
+    blocks = np.arange(GX).reshape(4, 4).T.reshape(-1)
+    waves = np.concatenate([first_wave(block) + np.arange(HALF) for block in blocks])
+    columns = np.arange(NX + 2 * CHUNK)
+    cosine, sine = trig(waves, columns, NX)
+    last = np.zeros((8, columns.size))
+    last[0], last[1] = trig(np.array([KX // 2]), columns, NX)
+    return low(np.concatenate([cosine, -sine])), low(last).astype(np.float32)
 
 
 @functools.lru_cache(None)
@@ -95,11 +96,19 @@
                 row_order[row, column, member, member, column, row] = 1.0
                 pick[row, column, member, :, member, row] = 1.0
                 same[row, column, member, column:64:GY] = 1.0
-    gather = np.zeros((128, DESTS // 2, PAD))
+    gather = np.zeros((128, GY, GX // 2, PAD))
     lane_part = np.zeros((128, 256))
+    join = np.zeros((128, KX))
+    spread = np.zeros((128, 256))
     for slot in range(64):
-        gather[slot, slot % 32, ROWS] = 1.0
-        lane_part[slot, slot // 32 * 128 : slot // 32 * 128 + 128] = 1.0
+        part, block, column = slot // 32, slot % 32 // GY, slot % GY
+        gather[slot, column, block, ROWS] = 1.0
+        lane_part[slot, part * 128 : part * 128 + 128] = 1.0
+        if block == 0:
+            spread[slot, part * 128 : part * 128 + 128] = 1.0
+        else:
+            other = GX - block
+            join[slot, part * 512 + other % 4 * 128 + other // 4 * 32] = 1.0 - 2.0 * part
     return (
         low(lane_order),
         low(row_order.reshape(ROWS * M, MEMBERS * GY * PAD)),
@@ -107,6 +116,8 @@
         same.reshape(ROWS * M, 128).astype(np.float32),
         low(gather.reshape(128, DESTS // 2 * PAD)),
         lane_part.astype(np.float32),
+        low(join),
+        low(spread),
     )
 
 
@@ -154,7 +165,7 @@
     turned = jnp.concatenate(
         [jnp.concatenate([even, -odd], axis=1), jnp.concatenate([odd, even], axis=1)], axis=0
     ).astype(jnp.bfloat16)
-    extra_ref[...] = nt(turned, coarse_ref[...]).astype(jnp.bfloat16)
+    extra_ref[...] = nt(coarse_ref[...], turned)
 
     shape = (KX, KY)
     wave_x = lax.broadcasted_iota(jnp.int32, shape, 0) - KX // 2
@@ -175,47 +186,92 @@
     with_cosine = jnp.concatenate([real[:half], imag[half:]], axis=0)
     with_sine = jnp.concatenate([-imag[:half], real[half:]], axis=0)
     weights = jnp.concatenate([with_cosine, with_sine], axis=1).astype(jnp.bfloat16)
-    weights = jnp.concatenate([weights, extra_ref[...]], axis=1)
+    dests = DESTS // 4
+    row = lax.broadcasted_iota(jnp.int32, (dests, PAD, 256), 1)
     for part in range(4):
-        rows = pl.ds(part * 384, 384)
-        out_ref[rows, :] = nt(table_ref[rows, :], weights).astype(jnp.bfloat16)
-
-
-def field_kernel(
-    scale_ref, got_ref, ensemble_ref, table_ref, lane_ref, row_ref, pick_ref, same_ref, gather_ref, part_ref, *rest
+        rows = pl.ds(part * dests * PAD, dests * PAD)
+        block = nt(table_ref[rows, :], weights).reshape(dests, PAD, 256)
+        extra = extra_ref[part * dests : (part + 1) * dests, :].reshape(dests, 1, 256)
+        out_ref[rows, :] = jnp.where(row == ROWS, extra, block).reshape(dests * PAD, 256).astype(jnp.bfloat16)
+
+
+def weigh(alpha, edge, last_ref, start, ensemble_ref, chunk, scale_ref):
+    columns = pl.ds(pl.multiple_of(start, CHUNK), CHUNK)
+    repeat = CHUNK // 128
+    cosine, sine = last_ref[:1, columns], last_ref[1:2, columns]
+    alpha = alpha + jnp.concatenate([edge[:, :128]] * repeat, axis=1) * cosine
+    alpha = alpha + jnp.concatenate([edge[:, 128:]] * repeat, axis=1) * sine
+    fields = ensemble_ref[:, :, pl.ds(pl.multiple_of(chunk * CHUNK, CHUNK), CHUNK)].astype(jnp.float32)
+    return jnp.sum(alpha.reshape(ROWS, M, CHUNK) * fields, axis=1) * scale_ref[:1, :1]
+
+
+def far_kernel(
+    scale_ref,
+    got_ref,
+    ensemble_ref,
+    table_ref,
+    lane_ref,
+    row_ref,
+    pick_ref,
+    same_ref,
+    gather_ref,
+    part_ref,
+    join_ref,
+    spread_ref,
+    last_ref,
+    joined_ref,
+    edge_ref,
+    *far_refs,
 ):
-    outs, joined = rest[:BANDS], rest[BANDS]
-    span = GY * PAD
-    groups = []
-    for part in range(2):
-        for high in range(4):
-            groups.append(
-                jnp.concatenate(
-                    [
-                        got_ref[(4 * high + least) * span : (4 * high + least + 1) * span, part * 128 : part * 128 + 128]
-                        for least in range(4)
-                    ],
-                    axis=1,
+    span = 4 * PAD
+    groups = [
+        jnp.concatenate(
+            [
+                got_ref[(4 * column + least) * span : (4 * column + least + 1) * span, part * 128 : part * 128 + 128]
+                for least in range(4)
+            ],
+            axis=1,
+        )
+        for part in range(2)
+        for column in range(GY)
+    ]
+    ordered = nn(jnp.concatenate(groups, axis=0), lane_ref[...])
+    members = []
+    for m in range(MEMBERS):
+        blocks = []
+        for part in range(2):
+            for high in range(4):
+                starts = [((part * GY + column) * 4 + high) * PAD for column in range(GY)]
+                blocks.append(
+                    jnp.concatenate([ordered[at : at + PAD, m * 128 : m * 128 + 128] for at in starts], axis=0)
                 )
-            )
-    ordered = nn(jnp.concatenate(groups, axis=0), lane_ref[...]).astype(jnp.bfloat16)
-    members = [
-        jnp.concatenate(
-            [ordered[group * span : (group + 1) * span, m * 128 : m * 128 + 128] for group in range(8)], axis=1
-        )
-        for m in range(MEMBERS)
-    ]
-    joined[:, : 2 * KX // 2] = nn(row_ref[...], jnp.concatenate(members, axis=0)).astype(jnp.bfloat16)
-    edge = nn(gather_ref[...], got_ref[: DESTS // 2 * PAD, :]) * part_ref[...]
-    joined[:, KX:] = (nt(pick_ref[...], edge.astype(jnp.bfloat16)) * same_ref[...]).astype(jnp.bfloat16)
-    scale = scale_ref[:1, :1]
+        members.append(jnp.concatenate(blocks, axis=1).astype(jnp.bfloat16))
+    sources = GX // 2 * PAD
+    edge = nn(
+        gather_ref[...],
+        jnp.concatenate([got_ref[2 * q * sources : (2 * q + 1) * sources, :] for q in range(GY)], axis=0),
+    )
+    edge = (nt(pick_ref[...], (edge * part_ref[...]).astype(jnp.bfloat16)) * same_ref[...]).astype(jnp.bfloat16)
+    joined = nn(
+        jnp.concatenate([row_ref[...], edge], axis=1), jnp.concatenate(members + [join_ref[...]], axis=0)
+    ).astype(jnp.bfloat16)
+    joined_ref[...] = joined
+    edge = nn(edge, spread_ref[...])
+    edge_ref[...] = edge
     band = lax.axis_index("band")
-    for step in range(BANDS):
-        start = pl.multiple_of(lax.rem(band + step, BANDS) * CHUNK, CHUNK)
-        columns = pl.ds(start, CHUNK)
-        alpha = nn(joined[...], table_ref[:, columns]).reshape(ROWS, M, CHUNK)
-        weighted = alpha * ensemble_ref[:, :, columns].astype(jnp.float32)
-        outs[step][...] = jnp.sum(weighted, axis=1) * scale
+    first = lax.rem(band + 1, BANDS) * CHUNK
+    alpha = nn(joined, table_ref[:, pl.ds(pl.multiple_of(first, CHUNK), 3 * CHUNK)])
+    for step, far_ref in enumerate(far_refs):
+        part = alpha[:, step * CHUNK : (step + 1) * CHUNK]
+        chunk = lax.rem(band + 1 + step, BANDS)
+        far_ref[...] = weigh(part, edge, last_ref, first + step * CHUNK, ensemble_ref, chunk, scale_ref)
+
+
+def near_kernel(scale_ref, joined_ref, edge_ref, ensemble_ref, table_ref, last_ref, own_ref):
+    band = lax.axis_index("band")
+    start = pl.multiple_of(band * CHUNK, CHUNK)
+    alpha = nn(joined_ref[...], table_ref[:, pl.ds(start, CHUNK)])
+    own_ref[...] = weigh(alpha, edge_ref[...], last_ref, start, ensemble_ref, band, scale_ref)
 
 
 def whole(count):
@@ -231,7 +287,7 @@
         own_kernel,
         out_shape=[
             jax.ShapeDtypeStruct((2, 256, KY), jnp.float32),
-            jax.ShapeDtypeStruct((256, 128), jnp.bfloat16),
+            jax.ShapeDtypeStruct((DESTS, 256), jnp.float32),
             jax.ShapeDtypeStruct((8, 128), jnp.float32),
         ],
         in_specs=[smem] + whole(4),
@@ -249,21 +305,39 @@
         cost_estimate=pl.CostEstimate(flops=ROWS_FLOPS, bytes_accessed=4 << 20, transcendentals=0),
         name="rows_kernel",
     )(band_cut, folded, extra, mirror, fold_tables(), table_y)
-    got = lax.all_to_all(rows, ("gx", "gy"), split_axis=0, concat_axis=0, tiled=True)
-    pieces = pl.pallas_call(
-        field_kernel,
-        out_shape=[jax.ShapeDtypeStruct((ROWS, CHUNK), jnp.float32)] * BANDS,
-        in_specs=whole(10),
-        out_specs=whole(BANDS),
-        scratch_shapes=[pltpu.VMEM((ROWS * M, KX + 128), jnp.bfloat16)],
+    got = lax.all_to_all(rows, ("gy", "gx"), split_axis=0, concat_axis=0, tiled=True)
+    fields, (table_x, last) = ensemble[0].transpose(1, 0, 2), column_tables()
+    piece = jax.ShapeDtypeStruct((ROWS, CHUNK), jnp.float32)
+    joined, edge, *far = pl.pallas_call(
+        far_kernel,
+        out_shape=[
+            jax.ShapeDtypeStruct((ROWS * M, KX), jnp.bfloat16),
+            jax.ShapeDtypeStruct((ROWS * M, 256), jnp.float32),
+        ]
+        + [piece] * (BANDS - 1),
+        in_specs=whole(13),
+        out_specs=whole(1 + BANDS),
         compiler_params=pltpu.CompilerParams(vmem_limit_bytes=SCRATCH),
-        cost_estimate=pl.CostEstimate(flops=3 << 30, bytes_accessed=16 << 20, transcendentals=0),
-        name="field_kernel",
-    )(scale, got, ensemble[0].transpose(1, 0, 2), column_tables(), *order_tables())
-    total = pieces[0]
-    for step in range(1, BANDS):
-        total = total + lax.ppermute(pieces[step], "band", [(i, (i + step) % BANDS) for i in range(BANDS)])
+        cost_estimate=pl.CostEstimate(flops=3 << 30, bytes_accessed=8 << 20, transcendentals=0),
+        name="far_kernel",
+    )(scale, got, fields, table_x, *order_tables(), last)
+    moved = [ahead(part, step + 1) for step, part in enumerate(far)]
+    total = pl.pallas_call(
+        near_kernel,
+        out_shape=piece,
+        in_specs=whole(6),
+        out_specs=pl.BlockSpec(memory_space=pltpu.VMEM),
+        compiler_params=pltpu.CompilerParams(vmem_limit_bytes=SCRATCH),
+        cost_estimate=pl.CostEstimate(flops=NEAR_FLOPS, bytes_accessed=4 << 20, transcendentals=0),
+        name="near_kernel",
+    )(scale, joined, edge, fields, table_x, last)
+    for part in moved:
+        total = total + part
     return total
+
+
+def ahead(piece, step):
+    return lax.ppermute(piece, "band", [(i, (i + step) % BANDS) for i in range(BANDS)])
 
 
 def solution(mesh):

time: 61.3 us -> 60 us (0.979)
  blocking collectives: 32.8 us -> 31.6 us
    all_to_all x1, blocking collectives: 32.8 us -> 31.6 us  [body(): lax.all_to_all(rows, ('gy', 'gx'), split_axis=0, concat_axis=0, tiled=True)]
    ppermute x3, waiting for transfers between devices: 2.87 us -> 2.23 us  [ahead(): lax.ppermute(piece, 'band', [(i, (i + step) % BANDS) for i in range(BANDS)])]
    unnamed x28 -> x34, local copies, waits for them, and re-layouts: 3.45 us -> 3.4 us
    pallas_call x1 -> x2, Pallas kernels: 4.05 us -> 4.06 us  [the longest x1 3.23 us: body(): pl.pallas_call(far_kernel, out_shape=[jax.ShapeDtypeStruct((ROWS * M, KX)...]
  transfers between devices with their start and end apart: 4 -> 4, of which waited for: 3 -> 3; matrix products, arithmetic and copies ran while one was open for 0% -> 0% of each run, Pallas kernels for 2% -> 3%
where the time goes in v2:
time: 60 us; the launch traced here: 59.2 us
  blocking collectives  31.6 us (53%)
  starting transfers between devices  11.4 us (19%)
  Pallas kernels  6.38 us (11%)
  waiting for transfers between devices  4.56 us (8%)
  local copies, waits for them, and re-layouts  4.43 us (7%)
  other arithmetic  0.64 us (1%)
    all_to_all x1, blocking collectives, body(): lax.all_to_all(rows, ('gy', 'gx'), split_axis=0, concat_axis=0, tiled=True)  31.6 us
    ppermute x3, starting transfers between devices, ahead(): lax.ppermute(piece, 'band', [(i, (i + step) % BANDS) for i in range(BANDS)])  5.98 us
    ppermute x1, starting transfers between devices, body(): lax.ppermute(own[:, HALF * MEMBERS:], 'gx', [(i, GX - 1 - i) for i in ran...  5.38 us
    unnamed x34, local copies, waits for them, and re-layouts  3.4 us
    pallas_call x1, Pallas kernels, body(): pl.pallas_call(far_kernel, out_shape=[jax.ShapeDtypeStruct((ROWS * M, KX)...  3.23 us
    ppermute x1, waiting for transfers between devices, body(): lax.ppermute(own[:, HALF * MEMBERS:], 'gx', [(i, GX - 1 - i) for i in ran...  2.33 us
    ppermute x3, waiting for transfers between devices, ahead(): lax.ppermute(piece, 'band', [(i, (i + step) % BANDS) for i in range(BANDS)])  2.23 us
    pallas_call x1, Pallas kernels, body(): pl.pallas_call(rows_kernel, out_shape=jax.ShapeDtypeStruct((DESTS * PAD,...  1.29 us
  transfers between devices with their start and end apart: 4, of which 3 were waited for; matrix products, arithmetic and copies ran while one was open for 0% of the time, Pallas kernels for 3%

profile of v2, /device:TPU:2, one launch (start us, length us, event | category | flops | bytes accessed | tf_op | source)
XLA Modules:
  0.0 59.2 jit_solution(4094238156259411490)
XLA Ops:
  0.0 1.0 %reshape_squeeze.3.own_ref = bf16[2,256,256]{2,1,0:T(8,128)(2,1)S(1)} reshape(bf16[1,2,64,4,256]{4,3,2,1,0:T(4,128)(2,1)} %param.18) | data formatting | bytes 524288 | tf_op jit(solution)/shard_map/reshape;squeeze | solution.py:282
  1.0 5.4 %collective-permute-start = (bf16[2,128,256]{2,1,0:T(8,128)(2,1)S(1)}, bf16[2,128,256]{2,1,0:T(8,128)(2,1)S(1)}, u32[]{:S(2)}, u32[]{:S(2)}) collective-permute-start(bf16[2,128,256]{2,1,0:T(8,128)(2,1)S(1)} %slice.4), channel_id=1, source_target_pairs={{0,60},{4,56},{8,52},{12,48},{16,44},{20,40},{24,36},{28,32},{32,2... | collective-permute-start | bytes 393224 | tf_op jit(solution)/shard_map/ppermute | solution.py:283
  6.4 0.7 %copy-done.10 = s32[4]{0:T(128)S(1)} copy-done((s32[4]{0:T(128)S(1)}, s32[4]{0:T(128)}, u32[]{:S(2)}) %copy-start.10) | copy-done | bytes 40
  7.1 1.0 %copy-done.12 = bf16[2,256,384]{2,1,0:T(8,128)(2,1)S(1)} copy-done((bf16[2,256,384]{2,1,0:T(8,128)(2,1)S(1)}, bf16[2,256,384]{2,1,0:T(8,128)(2,1)}, u32[]{:S(2)}) %copy-start.12) | copy-done | bytes 393240
  8.1 0.8 %copy-done.13 = f32[2,32,256]{2,1,0:T(8,128)S(1)} copy-done((f32[2,32,256]{2,1,0:T(8,128)S(1)}, f32[2,32,256]{2,1,0:T(8,128)}, u32[]{:S(2)}) %copy-start.13) | copy-done | bytes 65560
  8.9 0.8 %copy-done.14 = bf16[64,512]{1,0:T(8,128)(2,1)S(1)} copy-done((bf16[64,512]{1,0:T(8,128)(2,1)S(1)}, bf16[64,512]{1,0:T(8,128)(2,1)}, u32[]{:S(2)}) %copy-start.14) | copy-done | bytes 65560
  9.8 1.0 %own_kernel.1 = (f32[2,256,256]{2,1,0:T(8,128)S(1)}, f32[64,256]{1,0:T(8,128)S(1)}, f32[8,128]{1,0:T(8,128)S(1)}) custom-call(s32[4]{0:T(128)S(1)} %copy-done.10, bf16[2,256,256]{2,1,0:T(8,128)(2,1)S(1)} %reshape_squeeze.3.own_ref, bf16[2,256,384]{2,1,0:T(8,128)(2,1)S(1)} %copy-done.12, bf16[64,512]{1,0:T(8,128)(2,1)S(1)} %copy-done.14, ...), custom_call_target="tpu_custom_call" | custom-call | flops 10000000000 | bytes 1048576 | tf_op jit(solution)/shard_map/own_kernel/pallas_call | solution.py:286
  10.8 2.3 %collective-permute-done.mirror_ref = bf16[2,128,256]{2,1,0:T(8,128)(2,1)S(1)} collective-permute-done((bf16[2,128,256]{2,1,0:T(8,128)(2,1)S(1)}, bf16[2,128,256]{2,1,0:T(8,128)(2,1)S(1)}, u32[]{:S(2)}, u32[]{:S(2)}) %collective-permute-start) | collective-permute-done | bytes 131104 | tf_op jit(solution)/shard_map/ppermute | solution.py:283
  13.1 0.0 copy-done.11
  13.1 0.0 copy-start.3
  13.1 0.0 copy-start.4
  13.2 0.0 copy-start.5
  13.2 0.0 copy-start.6
  13.2 0.0 copy-start.7
  13.2 0.0 copy-start.8
  13.2 0.0 copy-start.9
  13.2 1.3 %rows_kernel.1 = bf16[1536,256]{1,0:T(8,128)(2,1)S(1)} custom-call(s32[4]{0:T(128)S(1)} %copy-done.10, f32[2,256,256]{2,1,0:T(8,128)S(1)} %get-tuple-element.14.folded_ref, f32[64,256]{1,0:T(8,128)S(1)} %get-tuple-element.15.extra_ref, bf16[2,128,256]{2,1,0:T(8,128)(2,1)S(1)} %collective-permute-done.mirror_ref, bf16[2,256,384]{2,1,0:T(8,128)(2,1)S(1)} %copy-done.12, ...), custom_call_target="tpu_custom_call" | custom-call | flops 20000000000 | bytes 4194304 | tf_op jit(solution)/shard_map/rows_kernel/pallas_call | solution.py:299
  14.5 0.0 copy-start.1
  14.5 31.6 %all_to_all.11 = bf16[64,24,256]{2,1,0:T(8,128)(2,1)S(1)} all-to-all(bf16[64,24,256]{2,1,0:T(8,128)(2,1)S(1)} %bitcast.10), channel_id=1, replica_groups=mesh['band'=4,'gx'=16,'gy'=4] {'gy','gx'}, dimensions={0} | all-to-all | bytes 1572864 | tf_op jit(solution)/shard_map/all_to_all | solution.py:308
  46.2 0.0 slice-done
  46.2 0.0 slice-done.1
  46.2 0.0 copy-done
  46.2 0.0 copy-done.2
  46.3 3.2 %far_kernel.1 = (bf16[352,1024]{1,0:T(8,128)(2,1)S(1)}, f32[352,256]{1,0:T(8,128)S(1)}, f32[22,640]{1,0:T(8,128)S(1)}, f32[22,640]{1,0:T(8,128)S(1)}, f32[22,640]{1,0:T(8,128)S(1)}) custom-call(f32[8,128]{1,0:T(8,128)S(1)} %get-tuple-element.13.scale_ref, bf16[1536,256]{1,0:T(8,128)(2,1)S(1)} %bitcast.7, bf16[22,16,2560]{2,1,0:T(8,128)(2,1)S(1)} %bitcast.8, ...), custom_call_target="tpu_custom_call" | custom-call | flops 3221225472 | bytes 8388608 | tf_op jit(solution)/shard_map/far_kernel/pallas_call | solution.py:311
  49.5 1.7 %collective-permute-start.1 = (f32[22,640]{1,0:T(8,128)S(1)}, f32[22,640]{1,0:T(8,128)S(1)}, u32[]{:S(2)}, u32[]{:S(2)}) collective-permute-start(f32[22,640]{1,0:T(8,128)S(1)} %get-tuple-element.18), channel_id=1, source_target_pairs={{0,64},{64,128},{128,192},{192,0},{1,65},{65,129},{129,193},{193,1... | collective-permute-start | bytes 168968 | tf_op jit(solution)/shard_map/ppermute | solution.py:340
  51.2 3.0 %collective-permute-start.2 = (f32[22,640]{1,0:T(8,128)S(1)}, f32[22,640]{1,0:T(8,128)S(1)}, u32[]{:S(2)}, u32[]{:S(2)}) collective-permute-start(f32[22,640]{1,0:T(8,128)S(1)} %get-tuple-element.19), channel_id=1, source_target_pairs={{0,128},{64,192},{128,0},{192,64},{1,129},{65,193},{129,1},{193,65... | collective-permute-start | bytes 168968 | tf_op jit(solution)/shard_map/ppermute | solution.py:340
  54.2 1.3 %collective-permute-start.3 = (f32[22,640]{1,0:T(8,128)S(1)}, f32[22,640]{1,0:T(8,128)S(1)}, u32[]{:S(2)}, u32[]{:S(2)}) collective-permute-start(f32[22,640]{1,0:T(8,128)S(1)} %get-tuple-element.20), channel_id=1, source_target_pairs={{0,192},{64,0},{128,64},{192,128},{1,193},{65,1},{129,65},{193,129... | collective-permute-start | bytes 168968 | tf_op jit(solution)/shard_map/ppermute | solution.py:340
  55.5 0.8 %near_kernel.1 = f32[22,640]{1,0:T(8,128)S(1)} custom-call(f32[8,128]{1,0:T(8,128)S(1)} %get-tuple-element.13.scale_ref, bf16[352,1024]{1,0:T(8,128)(2,1)S(1)} %get-tuple-element.16.joined_ref, f32[352,256]{1,0:T(8,128)S(1)} %get-tuple-element.17.edge_ref, bf16[22,16,2560]{2,1,0:T(8,128)(2,1)S(1)} %bitcast.9, bf16[1024,3840]{1,0:T(8,128)(2,1)S(1)} %bitcast.6, ...), custom_call_target="tpu_custom_call" | custom-call | flops 10000000000 | bytes 4194304 | tf_op jit(solution)/shard_map/near_kernel/pallas_call | solution.py:325
  56.3 0.0 collective-permute-done.1
  56.3 1.9 %collective-permute-done.2 = f32[22,640]{1,0:T(8,128)S(1)} collective-permute-done((f32[22,640]{1,0:T(8,128)S(1)}, f32[22,640]{1,0:T(8,128)S(1)}, u32[]{:S(2)}, u32[]{:S(2)}) %collective-permute-start.2) | collective-permute-done | bytes 56352 | tf_op jit(solution)/shard_map/ppermute | solution.py:340
  58.3 0.3 collective-permute-done.3
  58.6 0.6 %add_add_fusion = f32[22,640]{1,0:T(8,128)} fusion(f32[22,640]{1,0:T(8,128)S(1)} %collective-permute-done.3, f32[22,640]{1,0:T(8,128)S(1)} %collective-permute-done.2, f32[22,640]{1,0:T(8,128)S(1)} %near_kernel.1, f32[22,640]{1,0:T(8,128)S(1)} %collective-permute-done.1), kind=kLoop, calls=%fused_computation | loop fusion | flops 42240 | bytes 281600 | tf_op jit(solution)/shard_map/add | solution.py:335
  (19 shorter events, 0.0 us)
Async XLA Ops:
  1.0 12.1 %collective-permute-start = (bf16[2,128,256]{2,1,0:T(8,128)(2,1)S(1)}, bf16[2,128,256]{2,1,0:T(8,128)(2,1)S(1)}, u32[]{:S(2)}, u32[]{:S(2)}) collective-permute-start(bf16[2,128,256]{2,1,0:T(8,128)(2,1)S(1)} %slice.4), channel_id=1, source_target_pairs={{0,60},{4,56},{8,52},{12,48},{16,44},{20,40},{24,36},{28,32},{32,2... | collective-permute-start | bytes 393224 | tf_op jit(solution)/shard_map/ppermute | solution.py:283
  6.4 0.7 %copy-start.10 = (s32[4]{0:T(128)S(1)}, s32[4]{0:T(128)}, u32[]{:S(2)}) copy-start(s32[4]{0:T(128)} %cut_ref.3) | copy-start | bytes 52
  7.1 1.0 %copy-start.12 = (bf16[2,256,384]{2,1,0:T(8,128)(2,1)S(1)}, bf16[2,256,384]{2,1,0:T(8,128)(2,1)}, u32[]{:S(2)}) copy-start(bf16[2,256,384]{2,1,0:T(8,128)(2,1)} %constant.28.clone.fold_ref) | copy-start | bytes 1179652
  8.1 0.8 %copy-start.13 = (f32[2,32,256]{2,1,0:T(8,128)S(1)}, f32[2,32,256]{2,1,0:T(8,128)}, u32[]{:S(2)}) copy-start(f32[2,32,256]{2,1,0:T(8,128)} %constant.30.clone.fine_ref) | copy-start | bytes 196612
  8.9 0.8 %copy-start.14 = (bf16[64,512]{1,0:T(8,128)(2,1)S(1)}, bf16[64,512]{1,0:T(8,128)(2,1)}, u32[]{:S(2)}) copy-start(bf16[64,512]{1,0:T(8,128)(2,1)} %constant.29.clone.coarse_ref) | copy-start | bytes 196612
  9.8 3.4 %copy-start.11 = (bf16[1536,512]{1,0:T(8,128)(2,1)S(1)}, bf16[1536,512]{1,0:T(8,128)(2,1)}, u32[]{:S(2)}) copy-start(bf16[1536,512]{1,0:T(8,128)(2,1)} %constant.31.clone.table_ref) | copy-start | bytes 4718596
  9.8 36.4 %slice-start = ((s8[7864320]{0:T(1024)(128)(4,1)}), s8[4194304]{0:T(1024)(128)(4,1)S(1)}, s32[]{:S(2)}) async-start(s8[7864320]{0:T(1024)(128)(4,1)} %bitcast.5), calls=%async_computation.1 | async-start | bytes 8388608
  13.1 33.0 %slice-start.1 = ((s8[7864320]{0:T(1024)(128)(4,1)}), s8[3670016]{0:T(1024)(128)(4,1)S(1)}, s32[]{:S(2)}) async-start(s8[7864320]{0:T(1024)(128)(4,1)} %bitcast.5), calls=%async_computation.2 | async-start | bytes 7340032
  13.1 33.0 %copy-start = (bf16[1,16,22,2560]{3,1,2,0:T(8,128)(2,1)S(1)}, bf16[1,16,22,2560]{3,1,2,0:T(8,128)(2,1)}, u32[]{:S(2)}) copy-start(bf16[1,16,22,2560]{3,1,2,0:T(8,128)(2,1)} %param.17) | copy-start | bytes 5406724
  13.1 33.1 %copy-start.2 = (bf16[352,384]{1,0:T(8,128)(2,1)S(1)}, bf16[352,384]{1,0:T(8,128)(2,1)}, u32[]{:S(2)}) copy-start(bf16[352,384]{1,0:T(8,128)(2,1)} %constant.34.clone.row_ref) | copy-start | bytes 811012
  13.1 33.1 %copy-start.3 = (bf16[128,1024]{1,0:T(8,128)(2,1)S(1)}, bf16[128,1024]{1,0:T(8,128)(2,1)}, u32[]{:S(2)}) copy-start(bf16[128,1024]{1,0:T(8,128)(2,1)} %constant.39.clone.join_ref) | copy-start | bytes 786436
  13.1 33.1 %copy-start.4 = (bf16[128,768]{1,0:T(8,128)(2,1)S(1)}, bf16[128,768]{1,0:T(8,128)(2,1)}, u32[]{:S(2)}) copy-start(bf16[128,768]{1,0:T(8,128)(2,1)} %constant.37.clone.gather_ref) | copy-start | bytes 589828
  13.2 33.1 %copy-start.5 = (f32[352,128]{1,0:T(8,128)S(1)}, f32[352,128]{1,0:T(8,128)}, u32[]{:S(2)}) copy-start(f32[352,128]{1,0:T(8,128)} %constant.36.clone.same_ref) | copy-start | bytes 540676
  13.2 33.1 %copy-start.6 = (bf16[352,256]{1,0:T(8,128)(2,1)S(1)}, bf16[352,256]{1,0:T(8,128)(2,1)}, u32[]{:S(2)}) copy-start(bf16[352,256]{1,0:T(8,128)(2,1)} %constant.35.clone.pick_ref) | copy-start | bytes 540676
  13.2 33.0 %copy-start.7 = (f32[128,256]{1,0:T(8,128)S(1)}, f32[128,256]{1,0:T(8,128)}, u32[]{:S(2)}) copy-start(f32[128,256]{1,0:T(8,128)} %constant.38.clone.part_ref) | copy-start | bytes 393220
  13.2 33.0 %copy-start.8 = (f32[8,3840]{1,0:T(8,128)S(1)}, f32[8,3840]{1,0:T(8,128)}, u32[]{:S(2)}) copy-start(f32[8,3840]{1,0:T(8,128)} %constant.41.clone.last_ref) | copy-start | bytes 368644
  13.2 33.0 %copy-start.9 = (bf16[128,256]{1,0:T(8,128)(2,1)S(1)}, bf16[128,256]{1,0:T(8,128)(2,1)}, u32[]{:S(2)}) copy-start(bf16[128,256]{1,0:T(8,128)(2,1)} %constant.40.clone.spread_ref) | copy-start | bytes 196612
  14.5 31.7 %copy-start.1 = (bf16[512,512]{1,0:T(8,128)(2,1)S(1)}, bf16[512,512]{1,0:T(8,128)(2,1)}, u32[]{:S(2)}) copy-start(bf16[512,512]{1,0:T(8,128)(2,1)} %constant.33.clone.lane_ref) | copy-start | bytes 1572868
  49.5 6.8 %collective-permute-start.1 = (f32[22,640]{1,0:T(8,128)S(1)}, f32[22,640]{1,0:T(8,128)S(1)}, u32[]{:S(2)}, u32[]{:S(2)}) collective-permute-start(f32[22,640]{1,0:T(8,128)S(1)} %get-tuple-element.18), channel_id=1, source_target_pairs={{0,64},{64,128},{128,192},{192,0},{1,65},{65,129},{129,193},{193,1... | collective-permute-start | bytes 168968 | tf_op jit(solution)/shard_map/ppermute | solution.py:340
  51.2 7.1 %collective-permute-start.2 = (f32[22,640]{1,0:T(8,128)S(1)}, f32[22,640]{1,0:T(8,128)S(1)}, u32[]{:S(2)}, u32[]{:S(2)}) collective-permute-start(f32[22,640]{1,0:T(8,128)S(1)} %get-tuple-element.19), channel_id=1, source_target_pairs={{0,128},{64,192},{128,0},{192,64},{1,129},{65,193},{129,1},{193,65... | collective-permute-start | bytes 168968 | tf_op jit(solution)/shard_map/ppermute | solution.py:340
  54.2 4.4 %collective-permute-start.3 = (f32[22,640]{1,0:T(8,128)S(1)}, f32[22,640]{1,0:T(8,128)S(1)}, u32[]{:S(2)}, u32[]{:S(2)}) collective-permute-start(f32[22,640]{1,0:T(8,128)S(1)} %get-tuple-element.20), channel_id=1, source_target_pairs={{0,192},{64,0},{128,64},{192,128},{1,193},{65,1},{129,65},{193,129... | collective-permute-start | bytes 168968 | tf_op jit(solution)/shard_map/ppermute | solution.py:340

commit v3 on v2

--- a/solution.py
+++ b/solution.py
@@ -62,18 +62,16 @@
 @functools.lru_cache(None)
 def row_tables():
     cosine, sine = trig(np.arange(NY), np.arange(KY), NY)
-    table = np.zeros((GX, GY, PAD, 2 * KY))
-    table[:, :, :ROWS] = np.concatenate([cosine, sine], axis=1).reshape(GX, GY, ROWS, 2 * KY)
-    firsts = np.arange(DESTS).reshape(GX, GY).T.reshape(-1) * ROWS
-    coarse = np.concatenate(trig(firsts, np.arange(KY), NY), axis=1)
+    table = np.zeros((DESTS, PAD, 2 * KY))
+    table[:, :ROWS] = np.concatenate([cosine, sine], axis=1).reshape(DESTS, ROWS, 2 * KY)
+    coarse = np.concatenate(trig(np.arange(DESTS) * ROWS, np.arange(KY), NY), axis=1)
     fine = np.stack(trig(np.arange(32), np.arange(KY), NY)).astype(np.float32)
-    return low(table.transpose(1, 0, 2, 3).reshape(DESTS * PAD, 2 * KY)), low(coarse), fine
+    return low(table.reshape(DESTS * PAD, 2 * KY)), low(coarse), fine
 
 
 @functools.lru_cache(None)
 def column_tables():
-    blocks = np.arange(GX).reshape(4, 4).T.reshape(-1)
-    waves = np.concatenate([first_wave(block) + np.arange(HALF) for block in blocks])
+    waves = np.concatenate([first_wave(block) + np.arange(HALF) for block in range(GX)])
     columns = np.arange(NX + 2 * CHUNK)
     cosine, sine = trig(waves, columns, NX)
     last = np.zeros((8, columns.size))
@@ -83,10 +81,6 @@
 
 @functools.lru_cache(None)
 def order_tables():
-    lanes = np.arange(512)
-    lane_order = np.zeros((512, 512))
-    block, member, pair = lanes // 128, lanes // 32 % 4, lanes % 32
-    lane_order[lanes, member * 128 + block * 32 + pair] = 1.0
     row_order = np.zeros((ROWS, GY, MEMBERS, MEMBERS, GY, PAD))
     pick = np.zeros((ROWS, GY, MEMBERS, 2, MEMBERS, 32))
     same = np.zeros((ROWS, GY, MEMBERS, 128))
@@ -96,21 +90,20 @@
                 row_order[row, column, member, member, column, row] = 1.0
                 pick[row, column, member, :, member, row] = 1.0
                 same[row, column, member, column:64:GY] = 1.0
-    gather = np.zeros((128, GY, GX // 2, PAD))
+    gather = np.zeros((128, GX // 2, GY, PAD))
     lane_part = np.zeros((128, 256))
     join = np.zeros((128, KX))
     spread = np.zeros((128, 256))
     for slot in range(64):
         part, block, column = slot // 32, slot % 32 // GY, slot % GY
-        gather[slot, column, block, ROWS] = 1.0
+        gather[slot, block, column, ROWS] = 1.0
         lane_part[slot, part * 128 : part * 128 + 128] = 1.0
         if block == 0:
             spread[slot, part * 128 : part * 128 + 128] = 1.0
         else:
             other = GX - block
-            join[slot, part * 512 + other % 4 * 128 + other // 4 * 32] = 1.0 - 2.0 * part
+            join[slot, part * 512 + other * 32] = 1.0 - 2.0 * part
     return (
-        low(lane_order),
         low(row_order.reshape(ROWS * M, MEMBERS * GY * PAD)),
         low(pick.reshape(ROWS * M, 256)),
         same.reshape(ROWS * M, 128).astype(np.float32),
@@ -210,7 +203,6 @@
     got_ref,
     ensemble_ref,
     table_ref,
-    lane_ref,
     row_ref,
     pick_ref,
     same_ref,
@@ -223,33 +215,17 @@
     edge_ref,
     *far_refs,
 ):
-    span = 4 * PAD
-    groups = [
-        jnp.concatenate(
-            [
-                got_ref[(4 * column + least) * span : (4 * column + least + 1) * span, part * 128 : part * 128 + 128]
-                for least in range(4)
-            ],
-            axis=1,
-        )
-        for part in range(2)
-        for column in range(GY)
-    ]
-    ordered = nn(jnp.concatenate(groups, axis=0), lane_ref[...])
+    span = GY * PAD
     members = []
     for m in range(MEMBERS):
-        blocks = []
+        pieces = []
         for part in range(2):
-            for high in range(4):
-                starts = [((part * GY + column) * 4 + high) * PAD for column in range(GY)]
-                blocks.append(
-                    jnp.concatenate([ordered[at : at + PAD, m * 128 : m * 128 + 128] for at in starts], axis=0)
-                )
-        members.append(jnp.concatenate(blocks, axis=1).astype(jnp.bfloat16))
-    sources = GX // 2 * PAD
+            lane = part * 128 + m * HALF
+            pieces += [got_ref[block * span : (block + 1) * span, lane : lane + HALF] for block in range(GX)]
+        members.append(jnp.concatenate(pieces, axis=1))
     edge = nn(
         gather_ref[...],
-        jnp.concatenate([got_ref[2 * q * sources : (2 * q + 1) * sources, :] for q in range(GY)], axis=0),
+        got_ref[: GX // 2 * GY * PAD, :],
     )
     edge = (nt(pick_ref[...], (edge * part_ref[...]).astype(jnp.bfloat16)) * same_ref[...]).astype(jnp.bfloat16)
     joined = nn(
@@ -261,10 +237,15 @@
     band = lax.axis_index("band")
     first = lax.rem(band + 1, BANDS) * CHUNK
     alpha = nn(joined, table_ref[:, pl.ds(pl.multiple_of(first, CHUNK), 3 * CHUNK)])
-    for step, far_ref in enumerate(far_refs):
+    pieces = []
+    for step in range(BANDS - 1):
         part = alpha[:, step * CHUNK : (step + 1) * CHUNK]
         chunk = lax.rem(band + 1 + step, BANDS)
-        far_ref[...] = weigh(part, edge, last_ref, first + step * CHUNK, ensemble_ref, chunk, scale_ref)
+        pieces.append(weigh(part, edge, last_ref, first + step * CHUNK, ensemble_ref, chunk, scale_ref))
+    odd = (band & 1) == 1
+    far_refs[0][...] = jnp.where(odd, pieces[2], pieces[0])
+    far_refs[1][...] = jnp.where(odd, pieces[0], pieces[2])
+    far_refs[2][...] = pieces[1]
 
 
 def near_kernel(scale_ref, joined_ref, edge_ref, ensemble_ref, table_ref, last_ref, own_ref):
@@ -305,7 +286,7 @@
         cost_estimate=pl.CostEstimate(flops=ROWS_FLOPS, bytes_accessed=4 << 20, transcendentals=0),
         name="rows_kernel",
     )(band_cut, folded, extra, mirror, fold_tables(), table_y)
-    got = lax.all_to_all(rows, ("gy", "gx"), split_axis=0, concat_axis=0, tiled=True)
+    got = lax.all_to_all(rows, ("gx", "gy"), split_axis=0, concat_axis=0, tiled=True)
     fields, (table_x, last) = ensemble[0].transpose(1, 0, 2), column_tables()
     piece = jax.ShapeDtypeStruct((ROWS, CHUNK), jnp.float32)
     joined, edge, *far = pl.pallas_call(
@@ -315,13 +296,13 @@
             jax.ShapeDtypeStruct((ROWS * M, 256), jnp.float32),
         ]
         + [piece] * (BANDS - 1),
-        in_specs=whole(13),
+        in_specs=whole(12),
         out_specs=whole(1 + BANDS),
         compiler_params=pltpu.CompilerParams(vmem_limit_bytes=SCRATCH),
         cost_estimate=pl.CostEstimate(flops=3 << 30, bytes_accessed=8 << 20, transcendentals=0),
         name="far_kernel",
     )(scale, got, fields, table_x, *order_tables(), last)
-    moved = [ahead(part, step + 1) for step, part in enumerate(far)]
+    moved = [ahead(part, flip) for flip, part in zip((2, 3, 1), (far[2], far[1], far[0]))]
     total = pl.pallas_call(
         near_kernel,
         out_shape=piece,
@@ -337,7 +318,7 @@
 
 
 def ahead(piece, step):
-    return lax.ppermute(piece, "band", [(i, (i + step) % BANDS) for i in range(BANDS)])
+    return lax.ppermute(piece, "band", [(i, i ^ step) for i in range(BANDS)])
 
 
 def solution(mesh):

time: 60 us -> 60.1 us (level)
  starting transfers between devices: 11.4 us -> 9.8 us
  blocking collectives: 31.6 us -> 32.9 us
  waiting for transfers between devices: 4.56 us -> 5.83 us
    ppermute x3, starting transfers between devices: 5.98 us -> 4.42 us  [ahead(): return lax.ppermute(piece, 'band', [(i, i ^ step) for i in range(BANDS)])]
    all_to_all x1, blocking collectives: 31.6 us -> 32.9 us  [body(): lax.all_to_all(rows, ('gx', 'gy'), split_axis=0, concat_axis=0, tiled=True)]
    ppermute x3, waiting for transfers between devices: 2.23 us -> 3.5 us  [ahead(): return lax.ppermute(piece, 'band', [(i, i ^ step) for i in range(BANDS)])]
    unnamed x34 -> x32, local copies, waits for them, and re-layouts: 3.4 us -> 3.39 us
where the time goes in v3:
time: 60.1 us; the launch traced here: 59.8 us
  blocking collectives  32.9 us (55%)
  starting transfers between devices  9.8 us (16%)
  Pallas kernels  6.05 us (10%)
  waiting for transfers between devices  5.83 us (10%)
  local copies, waits for them, and re-layouts  4.42 us (7%)
  other arithmetic  0.64 us (1%)
    all_to_all x1, blocking collectives, body(): lax.all_to_all(rows, ('gx', 'gy'), split_axis=0, concat_axis=0, tiled=True)  32.9 us
    ppermute x1, starting transfers between devices, body(): lax.ppermute(own[:, HALF * MEMBERS:], 'gx', [(i, GX - 1 - i) for i in ran...  5.38 us
    ppermute x3, starting transfers between devices, ahead(): return lax.ppermute(piece, 'band', [(i, i ^ step) for i in range(BANDS)])  4.42 us
    ppermute x3, waiting for transfers between devices, ahead(): return lax.ppermute(piece, 'band', [(i, i ^ step) for i in range(BANDS)])  3.5 us
    unnamed x32, local copies, waits for them, and re-layouts  3.39 us
    pallas_call x1, Pallas kernels, body(): pl.pallas_call(far_kernel, out_shape=[jax.ShapeDtypeStruct((ROWS * M, KX)...  2.88 us
    ppermute x1, waiting for transfers between devices, body(): lax.ppermute(own[:, HALF * MEMBERS:], 'gx', [(i, GX - 1 - i) for i in ran...  2.33 us
    pallas_call x1, Pallas kernels, body(): pl.pallas_call(rows_kernel, out_shape=jax.ShapeDtypeStruct((DESTS * PAD,...  1.31 us
  transfers between devices with their start and end apart: 4, of which 3 were waited for; matrix products, arithmetic and copies ran while one was open for 0% of the time, Pallas kernels for 3%

profile of v3, /device:TPU:2, one launch (start us, length us, event | category | flops | bytes accessed | tf_op | source)
XLA Modules:
  0.0 59.8 jit_solution(18395012430639807247)
XLA Ops:
  0.0 1.0 %reshape_squeeze.3.own_ref = bf16[2,256,256]{2,1,0:T(8,128)(2,1)S(1)} reshape(bf16[1,2,64,4,256]{4,3,2,1,0:T(4,128)(2,1)} %param.17) | data formatting | bytes 524288 | tf_op jit(solution)/shard_map/reshape;squeeze | solution.py:263
  1.0 5.4 %collective-permute-start = (bf16[2,128,256]{2,1,0:T(8,128)(2,1)S(1)}, bf16[2,128,256]{2,1,0:T(8,128)(2,1)S(1)}, u32[]{:S(2)}, u32[]{:S(2)}) collective-permute-start(bf16[2,128,256]{2,1,0:T(8,128)(2,1)S(1)} %slice.4), channel_id=1, source_target_pairs={{0,60},{4,56},{8,52},{12,48},{16,44},{20,40},{24,36},{28,32},{32,2... | collective-permute-start | bytes 393224 | tf_op jit(solution)/shard_map/ppermute | solution.py:264
  6.4 0.7 %copy-done.1 = s32[4]{0:T(128)S(1)} copy-done((s32[4]{0:T(128)S(1)}, s32[4]{0:T(128)}, u32[]{:S(2)}) %copy-start.1) | copy-done | bytes 40
  7.1 1.0 %copy-done.3 = bf16[2,256,384]{2,1,0:T(8,128)(2,1)S(1)} copy-done((bf16[2,256,384]{2,1,0:T(8,128)(2,1)S(1)}, bf16[2,256,384]{2,1,0:T(8,128)(2,1)}, u32[]{:S(2)}) %copy-start.3) | copy-done | bytes 393240
  8.1 0.8 %copy-done.12 = f32[2,32,256]{2,1,0:T(8,128)S(1)} copy-done((f32[2,32,256]{2,1,0:T(8,128)S(1)}, f32[2,32,256]{2,1,0:T(8,128)}, u32[]{:S(2)}) %copy-start.12) | copy-done | bytes 65560
  8.9 0.8 %copy-done.13 = bf16[64,512]{1,0:T(8,128)(2,1)S(1)} copy-done((bf16[64,512]{1,0:T(8,128)(2,1)S(1)}, bf16[64,512]{1,0:T(8,128)(2,1)}, u32[]{:S(2)}) %copy-start.13) | copy-done | bytes 65560
  9.8 1.0 %own_kernel.1 = (f32[2,256,256]{2,1,0:T(8,128)S(1)}, f32[64,256]{1,0:T(8,128)S(1)}, f32[8,128]{1,0:T(8,128)S(1)}) custom-call(s32[4]{0:T(128)S(1)} %copy-done.1, bf16[2,256,256]{2,1,0:T(8,128)(2,1)S(1)} %reshape_squeeze.3.own_ref, bf16[2,256,384]{2,1,0:T(8,128)(2,1)S(1)} %copy-done.3, bf16[64,512]{1,0:T(8,128)(2,1)S(1)} %copy-done.13, ...), custom_call_target="tpu_custom_call" | custom-call | flops 10000000000 | bytes 1048576 | tf_op jit(solution)/shard_map/own_kernel/pallas_call | solution.py:267
  10.8 2.3 %collective-permute-done.mirror_ref = bf16[2,128,256]{2,1,0:T(8,128)(2,1)S(1)} collective-permute-done((bf16[2,128,256]{2,1,0:T(8,128)(2,1)S(1)}, bf16[2,128,256]{2,1,0:T(8,128)(2,1)S(1)}, u32[]{:S(2)}, u32[]{:S(2)}) %collective-permute-start) | collective-permute-done | bytes 131104 | tf_op jit(solution)/shard_map/ppermute | solution.py:264
  13.1 0.0 copy-done.2
  13.1 0.0 copy-start.5
  13.1 0.0 copy-start.6
  13.2 0.0 copy-start.7
  13.2 0.0 copy-start.8
  13.2 0.0 copy-start.9
  13.2 0.0 copy-start.10
  13.2 0.0 copy-start.11
  13.2 1.3 %rows_kernel.1 = bf16[1536,256]{1,0:T(8,128)(2,1)S(1)} custom-call(s32[4]{0:T(128)S(1)} %copy-done.1, f32[2,256,256]{2,1,0:T(8,128)S(1)} %get-tuple-element.14.folded_ref, f32[64,256]{1,0:T(8,128)S(1)} %get-tuple-element.15.extra_ref, bf16[2,128,256]{2,1,0:T(8,128)(2,1)S(1)} %collective-permute-done.mirror_ref, bf16[2,256,384]{2,1,0:T(8,128)(2,1)S(1)} %copy-done.3, ...), custom_call_target="tpu_custom_call" | custom-call | flops 20000000000 | bytes 4194304 | tf_op jit(solution)/shard_map/rows_kernel/pallas_call | solution.py:280
  14.5 32.9 %all_to_all.11 = bf16[64,24,256]{2,1,0:T(8,128)(2,1)S(1)} all-to-all(bf16[64,24,256]{2,1,0:T(8,128)(2,1)S(1)} %bitcast.6), channel_id=1, replica_groups=mesh['band'=4,'gx'=16,'gy'=4] {'gx','gy'}, dimensions={0} | all-to-all | bytes 1572864 | tf_op jit(solution)/shard_map/all_to_all | solution.py:289
  47.5 0.0 slice-done
  47.5 0.0 copy-done
  47.5 0.0 slice-done.1
  47.5 0.0 copy-done.4
  47.5 0.0 copy-done.5
  47.6 2.9 %far_kernel.1 = (bf16[352,1024]{1,0:T(8,128)(2,1)S(1)}, f32[352,256]{1,0:T(8,128)S(1)}, f32[22,640]{1,0:T(8,128)S(1)}, f32[22,640]{1,0:T(8,128)S(1)}, f32[22,640]{1,0:T(8,128)S(1)}) custom-call(f32[8,128]{1,0:T(8,128)S(1)} %get-tuple-element.13.scale_ref, bf16[1536,256]{1,0:T(8,128)(2,1)S(1)} %bitcast.5, bf16[22,16,2560]{2,1,0:T(8,128)(2,1)S(1)} %bitcast.7, ...), custom_call_target="tpu_custom_call" | custom-call | flops 3221225472 | bytes 8388608 | tf_op jit(solution)/shard_map/far_kernel/pallas_call | solution.py:292
  50.4 3.3 %collective-permute-start.1 = (f32[22,640]{1,0:T(8,128)S(1)}, f32[22,640]{1,0:T(8,128)S(1)}, u32[]{:S(2)}, u32[]{:S(2)}) collective-permute-start(f32[22,640]{1,0:T(8,128)S(1)} %get-tuple-element.18), channel_id=1, source_target_pairs={{0,128},{64,192},{128,0},{192,64},{1,129},{65,193},{129,1},{193,65... | collective-permute-start | bytes 168968 | tf_op jit(solution)/shard_map/ppermute | solution.py:321
  53.8 1.1 %collective-permute-start.2 = (f32[22,640]{1,0:T(8,128)S(1)}, f32[22,640]{1,0:T(8,128)S(1)}, u32[]{:S(2)}, u32[]{:S(2)}) collective-permute-start(f32[22,640]{1,0:T(8,128)S(1)} %get-tuple-element.19), channel_id=1, source_target_pairs={{0,192},{64,128},{128,64},{192,0},{1,193},{65,129},{129,65},{193,1... | collective-permute-start | bytes 168968 | tf_op jit(solution)/shard_map/ppermute | solution.py:321
  54.9 0.0 collective-permute-start.3
  54.9 0.8 %near_kernel.1 = f32[22,640]{1,0:T(8,128)S(1)} custom-call(f32[8,128]{1,0:T(8,128)S(1)} %get-tuple-element.13.scale_ref, bf16[352,1024]{1,0:T(8,128)(2,1)S(1)} %get-tuple-element.16.joined_ref, f32[352,256]{1,0:T(8,128)S(1)} %get-tuple-element.17.edge_ref, bf16[22,16,2560]{2,1,0:T(8,128)(2,1)S(1)} %bitcast.8, bf16[1024,3840]{1,0:T(8,128)(2,1)S(1)} %bitcast.10, ...), custom_call_target="tpu_custom_call" | custom-call | flops 10000000000 | bytes 4194304 | tf_op jit(solution)/shard_map/near_kernel/pallas_call | solution.py:306
  55.7 0.6 collective-permute-done.1
  56.3 2.9 %collective-permute-done.2 = f32[22,640]{1,0:T(8,128)S(1)} collective-permute-done((f32[22,640]{1,0:T(8,128)S(1)}, f32[22,640]{1,0:T(8,128)S(1)}, u32[]{:S(2)}, u32[]{:S(2)}) %collective-permute-start.2) | collective-permute-done | bytes 56352 | tf_op jit(solution)/shard_map/ppermute | solution.py:321
  59.2 0.0 collective-permute-done.3
  59.2 0.6 %add_add_fusion = f32[22,640]{1,0:T(8,128)} fusion(f32[22,640]{1,0:T(8,128)S(1)} %collective-permute-done.3, f32[22,640]{1,0:T(8,128)S(1)} %collective-permute-done.2, f32[22,640]{1,0:T(8,128)S(1)} %near_kernel.1, f32[22,640]{1,0:T(8,128)S(1)} %collective-permute-done.1), kind=kLoop, calls=%fused_computation | loop fusion | flops 42240 | bytes 281600 | tf_op jit(solution)/shard_map/add | solution.py:316
  (17 shorter events, 0.0 us)
Async XLA Ops:
  1.0 12.1 %collective-permute-start = (bf16[2,128,256]{2,1,0:T(8,128)(2,1)S(1)}, bf16[2,128,256]{2,1,0:T(8,128)(2,1)S(1)}, u32[]{:S(2)}, u32[]{:S(2)}) collective-permute-start(bf16[2,128,256]{2,1,0:T(8,128)(2,1)S(1)} %slice.4), channel_id=1, source_target_pairs={{0,60},{4,56},{8,52},{12,48},{16,44},{20,40},{24,36},{28,32},{32,2... | collective-permute-start | bytes 393224 | tf_op jit(solution)/shard_map/ppermute | solution.py:264
  6.4 0.7 %copy-start.1 = (s32[4]{0:T(128)S(1)}, s32[4]{0:T(128)}, u32[]{:S(2)}) copy-start(s32[4]{0:T(128)} %cut_ref.3) | copy-start | bytes 52
  7.1 1.0 %copy-start.3 = (bf16[2,256,384]{2,1,0:T(8,128)(2,1)S(1)}, bf16[2,256,384]{2,1,0:T(8,128)(2,1)}, u32[]{:S(2)}) copy-start(bf16[2,256,384]{2,1,0:T(8,128)(2,1)} %constant.26.clone.fold_ref) | copy-start | bytes 1179652
  8.1 0.8 %copy-start.12 = (f32[2,32,256]{2,1,0:T(8,128)S(1)}, f32[2,32,256]{2,1,0:T(8,128)}, u32[]{:S(2)}) copy-start(f32[2,32,256]{2,1,0:T(8,128)} %constant.28.clone.fine_ref) | copy-start | bytes 196612
  8.9 0.8 %copy-start.13 = (bf16[64,512]{1,0:T(8,128)(2,1)S(1)}, bf16[64,512]{1,0:T(8,128)(2,1)}, u32[]{:S(2)}) copy-start(bf16[64,512]{1,0:T(8,128)(2,1)} %constant.27.clone.coarse_ref) | copy-start | bytes 196612
  9.8 3.4 %copy-start.2 = (bf16[1536,512]{1,0:T(8,128)(2,1)S(1)}, bf16[1536,512]{1,0:T(8,128)(2,1)}, u32[]{:S(2)}) copy-start(bf16[1536,512]{1,0:T(8,128)(2,1)} %constant.29.clone.table_ref) | copy-start | bytes 4718596
  9.8 37.7 %slice-start = ((s8[7864320]{0:T(1024)(128)(4,1)}), s8[4194304]{0:T(1024)(128)(4,1)S(1)}, s32[]{:S(2)}) async-start(s8[7864320]{0:T(1024)(128)(4,1)} %bitcast.9), calls=%async_computation.1 | async-start | bytes 8388608
  13.1 34.3 %copy-start = (bf16[1,16,22,2560]{3,1,2,0:T(8,128)(2,1)S(1)}, bf16[1,16,22,2560]{3,1,2,0:T(8,128)(2,1)}, u32[]{:S(2)}) copy-start(bf16[1,16,22,2560]{3,1,2,0:T(8,128)(2,1)} %param.16) | copy-start | bytes 5406724
  13.1 34.3 %slice-start.1 = ((s8[7864320]{0:T(1024)(128)(4,1)}), s8[3670016]{0:T(1024)(128)(4,1)S(1)}, s32[]{:S(2)}) async-start(s8[7864320]{0:T(1024)(128)(4,1)} %bitcast.9), calls=%async_computation.2 | async-start | bytes 7340032
  13.1 34.3 %copy-start.4 = (bf16[352,384]{1,0:T(8,128)(2,1)S(1)}, bf16[352,384]{1,0:T(8,128)(2,1)}, u32[]{:S(2)}) copy-start(bf16[352,384]{1,0:T(8,128)(2,1)} %constant.31.clone.row_ref) | copy-start | bytes 811012
  13.1 34.3 %copy-start.5 = (bf16[128,1024]{1,0:T(8,128)(2,1)S(1)}, bf16[128,1024]{1,0:T(8,128)(2,1)}, u32[]{:S(2)}) copy-start(bf16[128,1024]{1,0:T(8,128)(2,1)} %constant.36.clone.join_ref) | copy-start | bytes 786436
  13.1 34.3 %copy-start.6 = (bf16[128,768]{1,0:T(8,128)(2,1)S(1)}, bf16[128,768]{1,0:T(8,128)(2,1)}, u32[]{:S(2)}) copy-start(bf16[128,768]{1,0:T(8,128)(2,1)} %constant.34.clone.gather_ref) | copy-start | bytes 589828
  13.2 34.3 %copy-start.7 = (f32[352,128]{1,0:T(8,128)S(1)}, f32[352,128]{1,0:T(8,128)}, u32[]{:S(2)}) copy-start(f32[352,128]{1,0:T(8,128)} %constant.33.clone.same_ref) | copy-start | bytes 540676
  13.2 34.3 %copy-start.8 = (bf16[352,256]{1,0:T(8,128)(2,1)S(1)}, bf16[352,256]{1,0:T(8,128)(2,1)}, u32[]{:S(2)}) copy-start(bf16[352,256]{1,0:T(8,128)(2,1)} %constant.32.clone.pick_ref) | copy-start | bytes 540676
  13.2 34.3 %copy-start.9 = (f32[128,256]{1,0:T(8,128)S(1)}, f32[128,256]{1,0:T(8,128)}, u32[]{:S(2)}) copy-start(f32[128,256]{1,0:T(8,128)} %constant.35.clone.part_ref) | copy-start | bytes 393220
  13.2 34.3 %copy-start.10 = (f32[8,3840]{1,0:T(8,128)S(1)}, f32[8,3840]{1,0:T(8,128)}, u32[]{:S(2)}) copy-start(f32[8,3840]{1,0:T(8,128)} %constant.38.clone.last_ref) | copy-start | bytes 368644
  13.2 34.3 %copy-start.11 = (bf16[128,256]{1,0:T(8,128)(2,1)S(1)}, bf16[128,256]{1,0:T(8,128)(2,1)}, u32[]{:S(2)}) copy-start(bf16[128,256]{1,0:T(8,128)(2,1)} %constant.37.clone.spread_ref) | copy-start | bytes 196612
  50.4 5.8 %collective-permute-start.1 = (f32[22,640]{1,0:T(8,128)S(1)}, f32[22,640]{1,0:T(8,128)S(1)}, u32[]{:S(2)}, u32[]{:S(2)}) collective-permute-start(f32[22,640]{1,0:T(8,128)S(1)} %get-tuple-element.18), channel_id=1, source_target_pairs={{0,128},{64,192},{128,0},{192,64},{1,129},{65,193},{129,1},{193,65... | collective-permute-start | bytes 168968 | tf_op jit(solution)/shard_map/ppermute | solution.py:321
  53.8 5.4 %collective-permute-start.2 = (f32[22,640]{1,0:T(8,128)S(1)}, f32[22,640]{1,0:T(8,128)S(1)}, u32[]{:S(2)}, u32[]{:S(2)}) collective-permute-start(f32[22,640]{1,0:T(8,128)S(1)} %get-tuple-element.19), channel_id=1, source_target_pairs={{0,192},{64,128},{128,64},{192,0},{1,193},{65,129},{129,65},{193,1... | collective-permute-start | bytes 168968 | tf_op jit(solution)/shard_map/ppermute | solution.py:321
  54.9 4.3 %collective-permute-start.3 = (f32[22,640]{1,0:T(8,128)S(1)}, f32[22,640]{1,0:T(8,128)S(1)}, u32[]{:S(2)}, u32[]{:S(2)}) collective-permute-start(f32[22,640]{1,0:T(8,128)S(1)} %get-tuple-element.20), channel_id=1, source_target_pairs={{0,64},{64,0},{128,192},{192,128},{1,65},{65,1},{129,193},{193,129... | collective-permute-start | bytes 168968 | tf_op jit(solution)/shard_map/ppermute | solution.py:321

commit v4 on v3

--- a/solution.py
+++ b/solution.py
@@ -25,6 +25,7 @@
 HALF = WAVES // 2
 MEMBERS = M // GY
 CHUNK = NX // BANDS
+SENT = jnp.bfloat16
 SCRATCH = 16 * 1024 * 1024
 OWN_FLOPS = 10 ** 10
 NEAR_FLOPS = 10 ** 10
@@ -213,7 +214,7 @@
     last_ref,
     joined_ref,
     edge_ref,
-    *far_refs,
+    relay_ref,
 ):
     span = GY * PAD
     members = []
@@ -234,25 +235,28 @@
     joined_ref[...] = joined
     edge = nn(edge, spread_ref[...])
     edge_ref[...] = edge
+    chunk = BANDS - 1 - (lax.axis_index("band") ^ 1)
+    start = pl.multiple_of(chunk * CHUNK, CHUNK)
+    alpha = nn(joined, table_ref[:, pl.ds(start, CHUNK)])
+    relay_ref[...] = weigh(alpha, edge, last_ref, start, ensemble_ref, chunk, scale_ref).astype(relay_ref.dtype)
+
+
+def near_kernel(
+    scale_ref, joined_ref, edge_ref, ensemble_ref, table_ref, last_ref, direct_ref, mirrored_ref, own_ref
+):
     band = lax.axis_index("band")
-    first = lax.rem(band + 1, BANDS) * CHUNK
-    alpha = nn(joined, table_ref[:, pl.ds(pl.multiple_of(first, CHUNK), 3 * CHUNK)])
+    after = BANDS - (band ^ 1)
+    first = lax.rem(after, BANDS) * CHUNK
+    alpha = nn(joined_ref[...], table_ref[:, pl.ds(pl.multiple_of(first, CHUNK), 3 * CHUNK)])
     pieces = []
     for step in range(BANDS - 1):
         part = alpha[:, step * CHUNK : (step + 1) * CHUNK]
-        chunk = lax.rem(band + 1 + step, BANDS)
-        pieces.append(weigh(part, edge, last_ref, first + step * CHUNK, ensemble_ref, chunk, scale_ref))
+        chunk = lax.rem(after + step, BANDS)
+        pieces.append(weigh(part, edge_ref[...], last_ref, first + step * CHUNK, ensemble_ref, chunk, scale_ref))
     odd = (band & 1) == 1
-    far_refs[0][...] = jnp.where(odd, pieces[2], pieces[0])
-    far_refs[1][...] = jnp.where(odd, pieces[0], pieces[2])
-    far_refs[2][...] = pieces[1]
-
-
-def near_kernel(scale_ref, joined_ref, edge_ref, ensemble_ref, table_ref, last_ref, own_ref):
-    band = lax.axis_index("band")
-    start = pl.multiple_of(band * CHUNK, CHUNK)
-    alpha = nn(joined_ref[...], table_ref[:, pl.ds(start, CHUNK)])
-    own_ref[...] = weigh(alpha, edge_ref[...], last_ref, start, ensemble_ref, band, scale_ref)
+    direct_ref[...] = jnp.where(odd, pieces[0], pieces[2]).astype(direct_ref.dtype)
+    mirrored_ref[...] = jnp.where(odd, pieces[2], pieces[0])
+    own_ref[...] = pieces[1]
 
 
 def whole(count):
@@ -289,32 +293,33 @@
     got = lax.all_to_all(rows, ("gx", "gy"), split_axis=0, concat_axis=0, tiled=True)
     fields, (table_x, last) = ensemble[0].transpose(1, 0, 2), column_tables()
     piece = jax.ShapeDtypeStruct((ROWS, CHUNK), jnp.float32)
-    joined, edge, *far = pl.pallas_call(
+    sent = jax.ShapeDtypeStruct((ROWS, CHUNK), SENT)
+    joined, edge, relay = pl.pallas_call(
         far_kernel,
         out_shape=[
             jax.ShapeDtypeStruct((ROWS * M, KX), jnp.bfloat16),
             jax.ShapeDtypeStruct((ROWS * M, 256), jnp.float32),
-        ]
-        + [piece] * (BANDS - 1),
+            sent,
+        ],
         in_specs=whole(12),
-        out_specs=whole(1 + BANDS),
+        out_specs=whole(3),
         compiler_params=pltpu.CompilerParams(vmem_limit_bytes=SCRATCH),
         cost_estimate=pl.CostEstimate(flops=3 << 30, bytes_accessed=8 << 20, transcendentals=0),
         name="far_kernel",
     )(scale, got, fields, table_x, *order_tables(), last)
-    moved = [ahead(part, flip) for flip, part in zip((2, 3, 1), (far[2], far[1], far[0]))]
-    total = pl.pallas_call(
+    relay = ahead(relay, 1)
+    direct, mirrored, own = pl.pallas_call(
         near_kernel,
-        out_shape=piece,
+        out_shape=[sent, piece, piece],
         in_specs=whole(6),
-        out_specs=pl.BlockSpec(memory_space=pltpu.VMEM),
+        out_specs=whole(3),
         compiler_params=pltpu.CompilerParams(vmem_limit_bytes=SCRATCH),
         cost_estimate=pl.CostEstimate(flops=NEAR_FLOPS, bytes_accessed=4 << 20, transcendentals=0),
         name="near_kernel",
     )(scale, joined, edge, fields, table_x, last)
-    for part in moved:
-        total = total + part
-    return total
+    direct = ahead(direct, 1)
+    across = ahead((mirrored + relay.astype(jnp.float32)).astype(SENT), 3)
+    return (own + direct.astype(jnp.float32)) + across.astype(jnp.float32)
 
 
 def ahead(piece, step):

time: 60.1 us -> 59.8 us (level)
  waiting for transfers between devices: 5.83 us -> 4.41 us
  starting transfers between devices: 9.8 us -> 10.7 us
    ppermute x3, waiting for transfers between devices: 3.5 us -> 2.08 us  [ahead(): return lax.ppermute(piece, 'band', [(i, i ^ step) for i in range(BANDS)])]
    pallas_call x1, Pallas kernels: 0.84 us -> 2.04 us  [body(): pl.pallas_call(near_kernel, out_shape=[sent, piece, piece], in_specs=whol...]
    pallas_call x1, Pallas kernels: 2.88 us -> 1.7 us  [body(): pl.pallas_call(far_kernel, out_shape=[jax.ShapeDtypeStruct((ROWS * M, KX)...]
    ppermute x3, starting transfers between devices: 4.42 us -> 5.34 us  [ahead(): return lax.ppermute(piece, 'band', [(i, i ^ step) for i in range(BANDS)])]
  transfers between devices with their start and end apart: 4 -> 4, of which waited for: 3 -> 3; matrix products, arithmetic and copies ran while one was open for 0% -> 0% of each run, Pallas kernels for 3% -> 5%
where the time goes in v4:
time: 59.8 us; the launch traced here: 59.4 us
  blocking collectives  32.9 us (55%)
  starting transfers between devices  10.7 us (18%)
  Pallas kernels  6.06 us (10%)
  local copies, waits for them, and re-layouts  4.42 us (7%)
  waiting for transfers between devices  4.41 us (7%)
  other arithmetic  0.65 us (1%)
    all_to_all x1, blocking collectives, body(): lax.all_to_all(rows, ('gx', 'gy'), split_axis=0, concat_axis=0, tiled=True)  32.9 us
    ppermute x1, starting transfers between devices, body(): lax.ppermute(own[:, HALF * MEMBERS:], 'gx', [(i, GX - 1 - i) for i in ran...  5.38 us
    ppermute x3, starting transfers between devices, ahead(): return lax.ppermute(piece, 'band', [(i, i ^ step) for i in range(BANDS)])  5.34 us
    unnamed x32, local copies, waits for them, and re-layouts  3.39 us
    ppermute x1, waiting for transfers between devices, body(): lax.ppermute(own[:, HALF * MEMBERS:], 'gx', [(i, GX - 1 - i) for i in ran...  2.33 us
    ppermute x3, waiting for transfers between devices, ahead(): return lax.ppermute(piece, 'band', [(i, i ^ step) for i in range(BANDS)])  2.08 us
    pallas_call x1, Pallas kernels, body(): pl.pallas_call(near_kernel, out_shape=[sent, piece, piece], in_specs=whol...  2.04 us
    pallas_call x1, Pallas kernels, body(): pl.pallas_call(far_kernel, out_shape=[jax.ShapeDtypeStruct((ROWS * M, KX)...  1.7 us
  transfers between devices with their start and end apart: 4, of which 3 were waited for; matrix products, arithmetic and copies ran while one was open for 0% of the time, Pallas kernels for 5%

profile of v4, /device:TPU:2, one launch (start us, length us, event | category | flops | bytes accessed | tf_op | source)
XLA Modules:
  0.0 59.4 jit_solution(10048466148193033293)
XLA Ops:
  0.0 1.0 %reshape_squeeze.3.own_ref = bf16[2,256,256]{2,1,0:T(8,128)(2,1)S(1)} reshape(bf16[1,2,64,4,256]{4,3,2,1,0:T(4,128)(2,1)} %param.17) | data formatting | bytes 524288 | tf_op jit(solution)/shard_map/reshape;squeeze | solution.py:267
  1.0 5.4 %collective-permute-start = (bf16[2,128,256]{2,1,0:T(8,128)(2,1)S(1)}, bf16[2,128,256]{2,1,0:T(8,128)(2,1)S(1)}, u32[]{:S(2)}, u32[]{:S(2)}) collective-permute-start(bf16[2,128,256]{2,1,0:T(8,128)(2,1)S(1)} %slice.4), channel_id=1, source_target_pairs={{0,60},{4,56},{8,52},{12,48},{16,44},{20,40},{24,36},{28,32},{32,2... | collective-permute-start | bytes 393224 | tf_op jit(solution)/shard_map/ppermute | solution.py:268
  6.4 0.7 %copy-done.1 = s32[4]{0:T(128)S(1)} copy-done((s32[4]{0:T(128)S(1)}, s32[4]{0:T(128)}, u32[]{:S(2)}) %copy-start.1) | copy-done | bytes 40
  7.1 1.0 %copy-done.3 = bf16[2,256,384]{2,1,0:T(8,128)(2,1)S(1)} copy-done((bf16[2,256,384]{2,1,0:T(8,128)(2,1)S(1)}, bf16[2,256,384]{2,1,0:T(8,128)(2,1)}, u32[]{:S(2)}) %copy-start.3) | copy-done | bytes 393240
  8.1 0.8 %copy-done.12 = f32[2,32,256]{2,1,0:T(8,128)S(1)} copy-done((f32[2,32,256]{2,1,0:T(8,128)S(1)}, f32[2,32,256]{2,1,0:T(8,128)}, u32[]{:S(2)}) %copy-start.12) | copy-done | bytes 65560
  8.9 0.8 %copy-done.13 = bf16[64,512]{1,0:T(8,128)(2,1)S(1)} copy-done((bf16[64,512]{1,0:T(8,128)(2,1)S(1)}, bf16[64,512]{1,0:T(8,128)(2,1)}, u32[]{:S(2)}) %copy-start.13) | copy-done | bytes 65560
  9.8 1.0 %own_kernel.1 = (f32[2,256,256]{2,1,0:T(8,128)S(1)}, f32[64,256]{1,0:T(8,128)S(1)}, f32[8,128]{1,0:T(8,128)S(1)}) custom-call(s32[4]{0:T(128)S(1)} %copy-done.1, bf16[2,256,256]{2,1,0:T(8,128)(2,1)S(1)} %reshape_squeeze.3.own_ref, bf16[2,256,384]{2,1,0:T(8,128)(2,1)S(1)} %copy-done.3, bf16[64,512]{1,0:T(8,128)(2,1)S(1)} %copy-done.13, ...), custom_call_target="tpu_custom_call" | custom-call | flops 10000000000 | bytes 1048576 | tf_op jit(solution)/shard_map/own_kernel/pallas_call | solution.py:271
  10.8 2.3 %collective-permute-done.mirror_ref = bf16[2,128,256]{2,1,0:T(8,128)(2,1)S(1)} collective-permute-done((bf16[2,128,256]{2,1,0:T(8,128)(2,1)S(1)}, bf16[2,128,256]{2,1,0:T(8,128)(2,1)S(1)}, u32[]{:S(2)}, u32[]{:S(2)}) %collective-permute-start) | collective-permute-done | bytes 131104 | tf_op jit(solution)/shard_map/ppermute | solution.py:268
  13.1 0.0 copy-start.5
  13.1 0.0 copy-start.6
  13.2 0.0 copy-start.7
  13.2 0.0 copy-start.8
  13.2 0.0 copy-start.9
  13.2 0.0 copy-start.10
  13.2 0.0 copy-start.11
  13.2 1.3 %rows_kernel.1 = bf16[1536,256]{1,0:T(8,128)(2,1)S(1)} custom-call(s32[4]{0:T(128)S(1)} %copy-done.1, f32[2,256,256]{2,1,0:T(8,128)S(1)} %get-tuple-element.15.folded_ref, f32[64,256]{1,0:T(8,128)S(1)} %get-tuple-element.16.extra_ref, bf16[2,128,256]{2,1,0:T(8,128)(2,1)S(1)} %collective-permute-done.mirror_ref, bf16[2,256,384]{2,1,0:T(8,128)(2,1)S(1)} %copy-done.3, ...), custom_call_target="tpu_custom_call" | custom-call | flops 20000000000 | bytes 4194304 | tf_op jit(solution)/shard_map/rows_kernel/pallas_call | solution.py:284
  14.5 32.9 %all_to_all.11 = bf16[64,24,256]{2,1,0:T(8,128)(2,1)S(1)} all-to-all(bf16[64,24,256]{2,1,0:T(8,128)(2,1)S(1)} %bitcast.6), channel_id=1, replica_groups=mesh['band'=4,'gx'=16,'gy'=4] {'gx','gy'}, dimensions={0} | all-to-all | bytes 1572864 | tf_op jit(solution)/shard_map/all_to_all | solution.py:293
  47.5 0.0 copy-done.4
  47.5 0.0 copy-done.5
  47.5 0.0 copy-done.6
  47.5 0.0 copy-done.7
  47.5 0.0 copy-done.8
  47.5 0.0 copy-done.9
  47.5 1.7 %far_kernel.1 = (bf16[352,1024]{1,0:T(8,128)(2,1)S(1)}, f32[352,256]{1,0:T(8,128)S(1)}, bf16[22,640]{1,0:T(8,128)(2,1)S(1)}) custom-call(f32[8,128]{1,0:T(8,128)S(1)} %get-tuple-element.14.scale_ref, bf16[1536,256]{1,0:T(8,128)(2,1)S(1)} %bitcast.5, bf16[22,16,2560]{2,1,0:T(8,128)(2,1)S(1)} %bitcast.7, bf16[1024,3840]{1,0:T(8,128)(2,1)S(1)} %bitcast.10, ...), custom_call_target="tpu_custom_call" | custom-call | flops 3221225472 | bytes 8388608 | tf_op jit(solution)/shard_map/far_kernel/pallas_call | solution.py:297
  49.3 1.7 %collective-permute-start.2 = (bf16[22,640]{1,0:T(8,128)(2,1)S(1)}, bf16[22,640]{1,0:T(8,128)(2,1)S(1)}, u32[]{:S(2)}, u32[]{:S(2)}) collective-permute-start(bf16[22,640]{1,0:T(8,128)(2,1)S(1)} %get-tuple-element.22), channel_id=1, source_target_pairs={{0,64},{64,0},{128,192},{192,128},{1,65},{65,1},{129,193},{193,129... | collective-permute-start | bytes 84488 | tf_op jit(solution)/shard_map/ppermute | solution.py:326
  50.9 2.0 %near_kernel.1 = (bf16[22,640]{1,0:T(8,128)(2,1)S(1)}, f32[22,640]{1,0:T(8,128)S(1)}, f32[22,640]{1,0:T(8,128)S(1)}) custom-call(f32[8,128]{1,0:T(8,128)S(1)} %get-tuple-element.14.scale_ref, bf16[352,1024]{1,0:T(8,128)(2,1)S(1)} %get-tuple-element.17.joined_ref, f32[352,256]{1,0:T(8,128)S(1)} %get-tuple-element.18.edge_ref, ...), custom_call_target="tpu_custom_call" | custom-call | flops 10000000000 | bytes 4194304 | tf_op jit(solution)/shard_map/near_kernel/pallas_call | solution.py:311
  53.0 0.6 collective-permute-start.1
  53.5 0.0 collective-permute-done.2
  53.5 3.1 %collective-permute-start.3 = (bf16[22,640]{1,0:T(8,128)(2,1)S(1)}, bf16[22,640]{1,0:T(8,128)(2,1)S(1)}, u32[]{:S(2)}, u32[]{:S(2)}) collective-permute-start(bf16[22,640]{1,0:T(8,128)(2,1)S(1)} %add_convert_fusion), channel_id=1, source_target_pairs={{0,192},{64,128},{128,64},{192,0},{1,193},{65,129},{129,65},{193,1... | collective-permute-start | bytes 84488 | tf_op jit(solution)/shard_map/ppermute | solution.py:326
  56.7 0.3 collective-permute-done.1
  56.9 1.8 %collective-permute-done.3 = bf16[22,640]{1,0:T(8,128)(2,1)S(1)} collective-permute-done((bf16[22,640]{1,0:T(8,128)(2,1)S(1)}, bf16[22,640]{1,0:T(8,128)(2,1)S(1)}, u32[]{:S(2)}, u32[]{:S(2)}) %collective-permute-start.3) | collective-permute-done | bytes 28192 | tf_op jit(solution)/shard_map/ppermute | solution.py:326
  58.7 0.6 %convert_add_fusion = f32[22,640]{1,0:T(8,128)} fusion(bf16[22,640]{1,0:T(8,128)(2,1)S(1)} %collective-permute-done.3, f32[22,640]{1,0:T(8,128)S(1)} %get-tuple-element.19, bf16[22,640]{1,0:T(8,128)(2,1)S(1)} %collective-permute-done.1), kind=kLoop, calls=%fused_computation | loop fusion | flops 56320 | bytes 168960 | tf_op jit(solution)/shard_map/add | solution.py:322
  (18 shorter events, 0.0 us)
Async XLA Ops:
  1.0 12.1 %collective-permute-start = (bf16[2,128,256]{2,1,0:T(8,128)(2,1)S(1)}, bf16[2,128,256]{2,1,0:T(8,128)(2,1)S(1)}, u32[]{:S(2)}, u32[]{:S(2)}) collective-permute-start(bf16[2,128,256]{2,1,0:T(8,128)(2,1)S(1)} %slice.4), channel_id=1, source_target_pairs={{0,60},{4,56},{8,52},{12,48},{16,44},{20,40},{24,36},{28,32},{32,2... | collective-permute-start | bytes 393224 | tf_op jit(solution)/shard_map/ppermute | solution.py:268
  6.4 0.7 %copy-start.1 = (s32[4]{0:T(128)S(1)}, s32[4]{0:T(128)}, u32[]{:S(2)}) copy-start(s32[4]{0:T(128)} %cut_ref.3) | copy-start | bytes 52
  7.1 1.0 %copy-start.3 = (bf16[2,256,384]{2,1,0:T(8,128)(2,1)S(1)}, bf16[2,256,384]{2,1,0:T(8,128)(2,1)}, u32[]{:S(2)}) copy-start(bf16[2,256,384]{2,1,0:T(8,128)(2,1)} %constant.26.clone.fold_ref) | copy-start | bytes 1179652
  8.1 0.8 %copy-start.12 = (f32[2,32,256]{2,1,0:T(8,128)S(1)}, f32[2,32,256]{2,1,0:T(8,128)}, u32[]{:S(2)}) copy-start(f32[2,32,256]{2,1,0:T(8,128)} %constant.28.clone.fine_ref) | copy-start | bytes 196612
  8.9 0.8 %copy-start.13 = (bf16[64,512]{1,0:T(8,128)(2,1)S(1)}, bf16[64,512]{1,0:T(8,128)(2,1)}, u32[]{:S(2)}) copy-start(bf16[64,512]{1,0:T(8,128)(2,1)} %constant.27.clone.coarse_ref) | copy-start | bytes 196612
  9.8 3.4 %copy-start.2 = (bf16[1536,512]{1,0:T(8,128)(2,1)S(1)}, bf16[1536,512]{1,0:T(8,128)(2,1)}, u32[]{:S(2)}) copy-start(bf16[1536,512]{1,0:T(8,128)(2,1)} %constant.29.clone.table_ref) | copy-start | bytes 4718596
  9.8 37.7 %slice-start = ((s8[7864320]{0:T(1024)(128)(4,1)}), s8[4194304]{0:T(1024)(128)(4,1)S(1)}, s32[]{:S(2)}) async-start(s8[7864320]{0:T(1024)(128)(4,1)} %bitcast.9), calls=%async_computation.1 | async-start | bytes 8388608
  13.1 34.3 %copy-start = (bf16[1,16,22,2560]{3,1,2,0:T(8,128)(2,1)S(1)}, bf16[1,16,22,2560]{3,1,2,0:T(8,128)(2,1)}, u32[]{:S(2)}) copy-start(bf16[1,16,22,2560]{3,1,2,0:T(8,128)(2,1)} %param.16) | copy-start | bytes 5406724
  13.1 34.3 %slice-start.1 = ((s8[7864320]{0:T(1024)(128)(4,1)}), s8[3670016]{0:T(1024)(128)(4,1)S(1)}, s32[]{:S(2)}) async-start(s8[7864320]{0:T(1024)(128)(4,1)} %bitcast.9), calls=%async_computation.2 | async-start | bytes 7340032
  13.1 34.3 %copy-start.4 = (bf16[352,384]{1,0:T(8,128)(2,1)S(1)}, bf16[352,384]{1,0:T(8,128)(2,1)}, u32[]{:S(2)}) copy-start(bf16[352,384]{1,0:T(8,128)(2,1)} %constant.31.clone.row_ref) | copy-start | bytes 811012
  13.1 34.3 %copy-start.5 = (bf16[128,1024]{1,0:T(8,128)(2,1)S(1)}, bf16[128,1024]{1,0:T(8,128)(2,1)}, u32[]{:S(2)}) copy-start(bf16[128,1024]{1,0:T(8,128)(2,1)} %constant.36.clone.join_ref) | copy-start | bytes 786436
  13.1 34.3 %copy-start.6 = (bf16[128,768]{1,0:T(8,128)(2,1)S(1)}, bf16[128,768]{1,0:T(8,128)(2,1)}, u32[]{:S(2)}) copy-start(bf16[128,768]{1,0:T(8,128)(2,1)} %constant.34.clone.gather_ref) | copy-start | bytes 589828
  13.2 34.3 %copy-start.7 = (f32[352,128]{1,0:T(8,128)S(1)}, f32[352,128]{1,0:T(8,128)}, u32[]{:S(2)}) copy-start(f32[352,128]{1,0:T(8,128)} %constant.33.clone.same_ref) | copy-start | bytes 540676
  13.2 34.3 %copy-start.8 = (bf16[352,256]{1,0:T(8,128)(2,1)S(1)}, bf16[352,256]{1,0:T(8,128)(2,1)}, u32[]{:S(2)}) copy-start(bf16[352,256]{1,0:T(8,128)(2,1)} %constant.32.clone.pick_ref) | copy-start | bytes 540676
  13.2 34.3 %copy-start.9 = (f32[128,256]{1,0:T(8,128)S(1)}, f32[128,256]{1,0:T(8,128)}, u32[]{:S(2)}) copy-start(f32[128,256]{1,0:T(8,128)} %constant.35.clone.part_ref) | copy-start | bytes 393220
  13.2 34.3 %copy-start.10 = (f32[8,3840]{1,0:T(8,128)S(1)}, f32[8,3840]{1,0:T(8,128)}, u32[]{:S(2)}) copy-start(f32[8,3840]{1,0:T(8,128)} %constant.38.clone.last_ref) | copy-start | bytes 368644
  13.2 34.3 %copy-start.11 = (bf16[128,256]{1,0:T(8,128)(2,1)S(1)}, bf16[128,256]{1,0:T(8,128)(2,1)}, u32[]{:S(2)}) copy-start(bf16[128,256]{1,0:T(8,128)(2,1)} %constant.37.clone.spread_ref) | copy-start | bytes 196612
  49.3 4.3 %collective-permute-start.2 = (bf16[22,640]{1,0:T(8,128)(2,1)S(1)}, bf16[22,640]{1,0:T(8,128)(2,1)S(1)}, u32[]{:S(2)}, u32[]{:S(2)}) collective-permute-start(bf16[22,640]{1,0:T(8,128)(2,1)S(1)} %get-tuple-element.22), channel_id=1, source_target_pairs={{0,64},{64,0},{128,192},{192,128},{1,65},{65,1},{129,193},{193,129... | collective-permute-start | bytes 84488 | tf_op jit(solution)/shard_map/ppermute | solution.py:326
  53.0 4.0 %collective-permute-start.1 = (bf16[22,640]{1,0:T(8,128)(2,1)S(1)}, bf16[22,640]{1,0:T(8,128)(2,1)S(1)}, u32[]{:S(2)}, u32[]{:S(2)}) collective-permute-start(bf16[22,640]{1,0:T(8,128)(2,1)S(1)} %get-tuple-element.20), channel_id=1, source_target_pairs={{0,64},{64,0},{128,192},{192,128},{1,65},{65,1},{129,193},{193,129... | collective-permute-start | bytes 84488 | tf_op jit(solution)/shard_map/ppermute | solution.py:326
  53.5 5.2 %collective-permute-start.3 = (bf16[22,640]{1,0:T(8,128)(2,1)S(1)}, bf16[22,640]{1,0:T(8,128)(2,1)S(1)}, u32[]{:S(2)}, u32[]{:S(2)}) collective-permute-start(bf16[22,640]{1,0:T(8,128)(2,1)S(1)} %add_convert_fusion), channel_id=1, source_target_pairs={{0,192},{64,128},{128,64},{192,0},{1,193},{65,129},{129,65},{193,1... | collective-permute-start | bytes 84488 | tf_op jit(solution)/shard_map/ppermute | solution.py:326

commit v5 on v4

--- a/solution.py
+++ b/solution.py
@@ -241,22 +241,25 @@
     relay_ref[...] = weigh(alpha, edge, last_ref, start, ensemble_ref, chunk, scale_ref).astype(relay_ref.dtype)
 
 
-def near_kernel(
-    scale_ref, joined_ref, edge_ref, ensemble_ref, table_ref, last_ref, direct_ref, mirrored_ref, own_ref
-):
+def chunk_field(chunk, joined, edge, last_ref, ensemble_ref, table_ref, scale_ref):
+    start = pl.multiple_of(chunk * CHUNK, CHUNK)
+    alpha = nn(joined, table_ref[:, pl.ds(start, CHUNK)])
+    return weigh(alpha, edge, last_ref, start, ensemble_ref, chunk, scale_ref)
+
+
+def near_kernel(scale_ref, joined_ref, edge_ref, ensemble_ref, table_ref, last_ref, direct_ref, mirrored_ref):
     band = lax.axis_index("band")
-    after = BANDS - (band ^ 1)
-    first = lax.rem(after, BANDS) * CHUNK
-    alpha = nn(joined_ref[...], table_ref[:, pl.ds(pl.multiple_of(first, CHUNK), 3 * CHUNK)])
-    pieces = []
-    for step in range(BANDS - 1):
-        part = alpha[:, step * CHUNK : (step + 1) * CHUNK]
-        chunk = lax.rem(after + step, BANDS)
-        pieces.append(weigh(part, edge_ref[...], last_ref, first + step * CHUNK, ensemble_ref, chunk, scale_ref))
-    odd = (band & 1) == 1
-    direct_ref[...] = jnp.where(odd, pieces[0], pieces[2]).astype(direct_ref.dtype)
-    mirrored_ref[...] = jnp.where(odd, pieces[2], pieces[0])
-    own_ref[...] = pieces[1]
+    refs = (last_ref, ensemble_ref, table_ref, scale_ref)
+    joined, edge = joined_ref[...], edge_ref[...]
+    mirrored_ref[...] = chunk_field(BANDS - 1 - band, joined, edge, *refs)
+    direct_ref[...] = chunk_field(band ^ 1, joined, edge, *refs).astype(direct_ref.dtype)
+
+
+def own_field_kernel(scale_ref, joined_ref, edge_ref, ensemble_ref, table_ref, last_ref, own_ref):
+    band = lax.axis_index("band")
+    own_ref[...] = chunk_field(
+        band, joined_ref[...], edge_ref[...], last_ref, ensemble_ref, table_ref, scale_ref
+    )
 
 
 def whole(count):
@@ -308,17 +311,28 @@
         name="far_kernel",
     )(scale, got, fields, table_x, *order_tables(), last)
     relay = ahead(relay, 1)
-    direct, mirrored, own = pl.pallas_call(
+    direct, mirrored = pl.pallas_call(
         near_kernel,
-        out_shape=[sent, piece, piece],
+        out_shape=[sent, piece],
         in_specs=whole(6),
-        out_specs=whole(3),
+        out_specs=whole(2),
         compiler_params=pltpu.CompilerParams(vmem_limit_bytes=SCRATCH),
         cost_estimate=pl.CostEstimate(flops=NEAR_FLOPS, bytes_accessed=4 << 20, transcendentals=0),
         name="near_kernel",
     )(scale, joined, edge, fields, table_x, last)
     direct = ahead(direct, 1)
-    across = ahead((mirrored + relay.astype(jnp.float32)).astype(SENT), 3)
+    passed = (mirrored + relay.astype(jnp.float32)).astype(SENT)
+    passed, joined = lax.optimization_barrier((passed, joined))
+    across = ahead(passed, 3)
+    own = pl.pallas_call(
+        own_field_kernel,
+        out_shape=piece,
+        in_specs=whole(6),
+        out_specs=pl.BlockSpec(memory_space=pltpu.VMEM),
+        compiler_params=pltpu.CompilerParams(vmem_limit_bytes=SCRATCH),
+        cost_estimate=pl.CostEstimate(flops=NEAR_FLOPS, bytes_accessed=4 << 20, transcendentals=0),
+        name="own_field_kernel",
+    )(scale, joined, edge, fields, table_x, last)
     return (own + direct.astype(jnp.float32)) + across.astype(jnp.float32)
 
 

time: 59.8 us -> 59.6 us (level)
  waiting for transfers between devices: 4.41 us -> 3.59 us
    ppermute x3, waiting for transfers between devices: 2.08 us -> 1.26 us  [ahead(): return lax.ppermute(piece, 'band', [(i, i ^ step) for i in range(BANDS)])]
    pallas_call x1 -> x2, Pallas kernels: 2.04 us -> 2.37 us  [the longest x1 1.56 us: body(): pl.pallas_call(near_kernel, out_shape=[sent, piece], in_specs=whole(6), o...]
  transfers between devices with their start and end apart: 4 -> 4, of which waited for: 3 -> 3; matrix products, arithmetic and copies ran while one was open for 0% -> 0% of each run, Pallas kernels for 5% -> 6%
where the time goes in v5:
time: 59.6 us; the launch traced here: 59.1 us
  blocking collectives  32.9 us (55%)
  starting transfers between devices  10.9 us (18%)
  Pallas kernels  6.39 us (11%)
  local copies, waits for them, and re-layouts  4.42 us (7%)
  waiting for transfers between devices  3.59 us (6%)
  other arithmetic  0.65 us (1%)
    all_to_all x1, blocking collectives, body(): lax.all_to_all(rows, ('gx', 'gy'), split_axis=0, concat_axis=0, tiled=True)  32.9 us
    ppermute x3, starting transfers between devices, ahead(): return lax.ppermute(piece, 'band', [(i, i ^ step) for i in range(BANDS)])  5.53 us
    ppermute x1, starting transfers between devices, body(): lax.ppermute(own[:, HALF * MEMBERS:], 'gx', [(i, GX - 1 - i) for i in ran...  5.38 us
    unnamed x32, local copies, waits for them, and re-layouts  3.39 us
    ppermute x1, waiting for transfers between devices, body(): lax.ppermute(own[:, HALF * MEMBERS:], 'gx', [(i, GX - 1 - i) for i in ran...  2.33 us
    pallas_call x1, Pallas kernels, body(): pl.pallas_call(far_kernel, out_shape=[jax.ShapeDtypeStruct((ROWS * M, KX)...  1.7 us
    pallas_call x1, Pallas kernels, body(): pl.pallas_call(near_kernel, out_shape=[sent, piece], in_specs=whole(6), o...  1.56 us
    pallas_call x1, Pallas kernels, body(): pl.pallas_call(rows_kernel, out_shape=jax.ShapeDtypeStruct((DESTS * PAD,...  1.29 us
  transfers between devices with their start and end apart: 4, of which 3 were waited for; matrix products, arithmetic and copies ran while one was open for 0% of the time, Pallas kernels for 6%

profile of v5, /device:TPU:2, one launch (start us, length us, event | category | flops | bytes accessed | tf_op | source)
XLA Modules:
  0.0 59.1 jit_solution(14249001185113009686)
XLA Ops:
  0.0 1.0 %reshape_squeeze.3.own_ref = bf16[2,256,256]{2,1,0:T(8,128)(2,1)S(1)} reshape(bf16[1,2,64,4,256]{4,3,2,1,0:T(4,128)(2,1)} %param.17) | data formatting | bytes 524288 | tf_op jit(solution)/shard_map/reshape;squeeze | solution.py:270
  1.0 5.4 %collective-permute-start = (bf16[2,128,256]{2,1,0:T(8,128)(2,1)S(1)}, bf16[2,128,256]{2,1,0:T(8,128)(2,1)S(1)}, u32[]{:S(2)}, u32[]{:S(2)}) collective-permute-start(bf16[2,128,256]{2,1,0:T(8,128)(2,1)S(1)} %slice.4), channel_id=1, source_target_pairs={{0,60},{4,56},{8,52},{12,48},{16,44},{20,40},{24,36},{28,32},{32,2... | collective-permute-start | bytes 393224 | tf_op jit(solution)/shard_map/ppermute | solution.py:271
  6.4 0.7 %copy-done.1 = s32[4]{0:T(128)S(1)} copy-done((s32[4]{0:T(128)S(1)}, s32[4]{0:T(128)}, u32[]{:S(2)}) %copy-start.1) | copy-done | bytes 40
  7.1 1.0 %copy-done.3 = bf16[2,256,384]{2,1,0:T(8,128)(2,1)S(1)} copy-done((bf16[2,256,384]{2,1,0:T(8,128)(2,1)S(1)}, bf16[2,256,384]{2,1,0:T(8,128)(2,1)}, u32[]{:S(2)}) %copy-start.3) | copy-done | bytes 393240
  8.1 0.8 %copy-done.12 = f32[2,32,256]{2,1,0:T(8,128)S(1)} copy-done((f32[2,32,256]{2,1,0:T(8,128)S(1)}, f32[2,32,256]{2,1,0:T(8,128)}, u32[]{:S(2)}) %copy-start.12) | copy-done | bytes 65560
  8.9 0.8 %copy-done.13 = bf16[64,512]{1,0:T(8,128)(2,1)S(1)} copy-done((bf16[64,512]{1,0:T(8,128)(2,1)S(1)}, bf16[64,512]{1,0:T(8,128)(2,1)}, u32[]{:S(2)}) %copy-start.13) | copy-done | bytes 65560
  9.8 1.0 %own_kernel.1 = (f32[2,256,256]{2,1,0:T(8,128)S(1)}, f32[64,256]{1,0:T(8,128)S(1)}, f32[8,128]{1,0:T(8,128)S(1)}) custom-call(s32[4]{0:T(128)S(1)} %copy-done.1, bf16[2,256,256]{2,1,0:T(8,128)(2,1)S(1)} %reshape_squeeze.3.own_ref, bf16[2,256,384]{2,1,0:T(8,128)(2,1)S(1)} %copy-done.3, bf16[64,512]{1,0:T(8,128)(2,1)S(1)} %copy-done.13, ...), custom_call_target="tpu_custom_call" | custom-call | flops 10000000000 | bytes 1048576 | tf_op jit(solution)/shard_map/own_kernel/pallas_call | solution.py:274
  10.8 2.3 %collective-permute-done.mirror_ref = bf16[2,128,256]{2,1,0:T(8,128)(2,1)S(1)} collective-permute-done((bf16[2,128,256]{2,1,0:T(8,128)(2,1)S(1)}, bf16[2,128,256]{2,1,0:T(8,128)(2,1)S(1)}, u32[]{:S(2)}, u32[]{:S(2)}) %collective-permute-start) | collective-permute-done | bytes 131104 | tf_op jit(solution)/shard_map/ppermute | solution.py:271
  13.1 0.0 copy-done.2
  13.1 0.0 copy-start.5
  13.1 0.0 copy-start.6
  13.2 0.0 copy-start.7
  13.2 0.0 copy-start.8
  13.2 0.0 copy-start.9
  13.2 0.0 copy-start.10
  13.2 0.0 copy-start.11
  13.2 1.3 %rows_kernel.1 = bf16[1536,256]{1,0:T(8,128)(2,1)S(1)} custom-call(s32[4]{0:T(128)S(1)} %copy-done.1, f32[2,256,256]{2,1,0:T(8,128)S(1)} %get-tuple-element.16.folded_ref, f32[64,256]{1,0:T(8,128)S(1)} %get-tuple-element.17.extra_ref, bf16[2,128,256]{2,1,0:T(8,128)(2,1)S(1)} %collective-permute-done.mirror_ref, bf16[2,256,384]{2,1,0:T(8,128)(2,1)S(1)} %copy-done.3, ...), custom_call_target="tpu_custom_call" | custom-call | flops 20000000000 | bytes 4194304 | tf_op jit(solution)/shard_map/rows_kernel/pallas_call | solution.py:287
  14.5 32.9 %all_to_all.11 = bf16[64,24,256]{2,1,0:T(8,128)(2,1)S(1)} all-to-all(bf16[64,24,256]{2,1,0:T(8,128)(2,1)S(1)} %bitcast.6), channel_id=1, replica_groups=mesh['band'=4,'gx'=16,'gy'=4] {'gx','gy'}, dimensions={0} | all-to-all | bytes 1572864 | tf_op jit(solution)/shard_map/all_to_all | solution.py:296
  47.4 0.0 slice-done
  47.5 0.0 copy-done
  47.5 0.0 slice-done.1
  47.5 0.0 copy-done.4
  47.5 1.7 %far_kernel.1 = (bf16[352,1024]{1,0:T(8,128)(2,1)S(1)}, f32[352,256]{1,0:T(8,128)S(1)}, bf16[22,640]{1,0:T(8,128)(2,1)S(1)}) custom-call(f32[8,128]{1,0:T(8,128)S(1)} %get-tuple-element.15.scale_ref, bf16[1536,256]{1,0:T(8,128)(2,1)S(1)} %bitcast.5, bf16[22,16,2560]{2,1,0:T(8,128)(2,1)S(1)} %bitcast.7, bf16[1024,3840]{1,0:T(8,128)(2,1)S(1)} %bitcast.11, ...), custom_call_target="tpu_custom_call" | custom-call | flops 3221225472 | bytes 8388608 | tf_op jit(solution)/shard_map/far_kernel/pallas_call | solution.py:300
  49.3 1.7 %collective-permute-start.1 = (bf16[22,640]{1,0:T(8,128)(2,1)S(1)}, bf16[22,640]{1,0:T(8,128)(2,1)S(1)}, u32[]{:S(2)}, u32[]{:S(2)}) collective-permute-start(bf16[22,640]{1,0:T(8,128)(2,1)S(1)} %get-tuple-element.21), channel_id=1, source_target_pairs={{0,64},{64,0},{128,192},{192,128},{1,65},{65,1},{129,193},{193,129... | collective-permute-start | bytes 84488 | tf_op jit(solution)/shard_map/ppermute | solution.py:340
  50.9 1.6 %near_kernel.1 = (bf16[22,640]{1,0:T(8,128)(2,1)S(1)}, f32[22,640]{1,0:T(8,128)S(1)}) custom-call(f32[8,128]{1,0:T(8,128)S(1)} %get-tuple-element.15.scale_ref, bf16[352,1024]{1,0:T(8,128)(2,1)S(1)} %get-tuple-element.22.joined_ref, f32[352,256]{1,0:T(8,128)S(1)} %get-tuple-element.19.edge_ref, bf16[22,16,2560]{2,1,0:T(8,128)(2,1)S(1)} %bitcast.8, ...), custom_call_target="tpu_custom_call" | custom-call | flops 10000000000 | bytes 4194304 | tf_op jit(solution)/shard_map/near_kernel/pallas_call | solution.py:314
  52.5 0.5 collective-permute-start.2
  53.0 0.2 collective-permute-done.1
  53.2 3.3 %collective-permute-start.3 = (bf16[22,640]{1,0:T(8,128)(2,1)S(1)}, bf16[22,640]{1,0:T(8,128)(2,1)S(1)}, u32[]{:S(2)}, u32[]{:S(2)}) collective-permute-start(bf16[22,640]{1,0:T(8,128)(2,1)S(1)} %add_convert_fusion), channel_id=1, source_target_pairs={{0,192},{64,128},{128,64},{192,0},{1,193},{65,129},{129,65},{193,1... | collective-permute-start | bytes 84488 | tf_op jit(solution)/shard_map/ppermute | solution.py:340
  56.6 0.8 %own_field_kernel.1 = f32[22,640]{1,0:T(8,128)S(1)} custom-call(f32[8,128]{1,0:T(8,128)S(1)} %get-tuple-element.15.scale_ref, bf16[352,1024]{1,0:T(8,128)(2,1)S(1)} %get-tuple-element.22.joined_ref, f32[352,256]{1,0:T(8,128)S(1)} %get-tuple-element.19.edge_ref, bf16[22,16,2560]{2,1,0:T(8,128)(2,1)S(1)} %bitcast.9, bf16[1024,3840]{1,0:T(8,128)(2,1)S(1)} %bitcast.11, ...), custom_call_target="tpu_custom_call" | custom-call | flops 10000000000 | bytes 4194304 | tf_op jit(solution)/shard_map/own_field_kernel/pallas_call | solution.py:327
  57.4 0.0 collective-permute-done.2
  57.4 1.0 %collective-permute-done.3 = bf16[22,640]{1,0:T(8,128)(2,1)S(1)} collective-permute-done((bf16[22,640]{1,0:T(8,128)(2,1)S(1)}, bf16[22,640]{1,0:T(8,128)(2,1)S(1)}, u32[]{:S(2)}, u32[]{:S(2)}) %collective-permute-start.3) | collective-permute-done | bytes 28192 | tf_op jit(solution)/shard_map/ppermute | solution.py:340
  58.5 0.6 %convert_add_fusion = f32[22,640]{1,0:T(8,128)} fusion(bf16[22,640]{1,0:T(8,128)(2,1)S(1)} %collective-permute-done.3, f32[22,640]{1,0:T(8,128)S(1)} %own_field_kernel.1, bf16[22,640]{1,0:T(8,128)(2,1)S(1)} %collective-permute-done.2), kind=kLoop, calls=%fused_computation | loop fusion | flops 56320 | bytes 168960 | tf_op jit(solution)/shard_map/add | solution.py:336
  (19 shorter events, 0.1 us)
Async XLA Ops:
  1.0 12.1 %collective-permute-start = (bf16[2,128,256]{2,1,0:T(8,128)(2,1)S(1)}, bf16[2,128,256]{2,1,0:T(8,128)(2,1)S(1)}, u32[]{:S(2)}, u32[]{:S(2)}) collective-permute-start(bf16[2,128,256]{2,1,0:T(8,128)(2,1)S(1)} %slice.4), channel_id=1, source_target_pairs={{0,60},{4,56},{8,52},{12,48},{16,44},{20,40},{24,36},{28,32},{32,2... | collective-permute-start | bytes 393224 | tf_op jit(solution)/shard_map/ppermute | solution.py:271
  6.4 0.7 %copy-start.1 = (s32[4]{0:T(128)S(1)}, s32[4]{0:T(128)}, u32[]{:S(2)}) copy-start(s32[4]{0:T(128)} %cut_ref.3) | copy-start | bytes 52
  7.1 1.0 %copy-start.3 = (bf16[2,256,384]{2,1,0:T(8,128)(2,1)S(1)}, bf16[2,256,384]{2,1,0:T(8,128)(2,1)}, u32[]{:S(2)}) copy-start(bf16[2,256,384]{2,1,0:T(8,128)(2,1)} %constant.26.clone.fold_ref) | copy-start | bytes 1179652
  8.1 0.8 %copy-start.12 = (f32[2,32,256]{2,1,0:T(8,128)S(1)}, f32[2,32,256]{2,1,0:T(8,128)}, u32[]{:S(2)}) copy-start(f32[2,32,256]{2,1,0:T(8,128)} %constant.28.clone.fine_ref) | copy-start | bytes 196612
  8.9 0.8 %copy-start.13 = (bf16[64,512]{1,0:T(8,128)(2,1)S(1)}, bf16[64,512]{1,0:T(8,128)(2,1)}, u32[]{:S(2)}) copy-start(bf16[64,512]{1,0:T(8,128)(2,1)} %constant.27.clone.coarse_ref) | copy-start | bytes 196612
  9.8 3.4 %copy-start.2 = (bf16[1536,512]{1,0:T(8,128)(2,1)S(1)}, bf16[1536,512]{1,0:T(8,128)(2,1)}, u32[]{:S(2)}) copy-start(bf16[1536,512]{1,0:T(8,128)(2,1)} %constant.29.clone.table_ref) | copy-start | bytes 4718596
  9.8 37.7 %slice-start = ((s8[7864320]{0:T(1024)(128)(4,1)}), s8[4194304]{0:T(1024)(128)(4,1)S(1)}, s32[]{:S(2)}) async-start(s8[7864320]{0:T(1024)(128)(4,1)} %bitcast.10), calls=%async_computation.1 | async-start | bytes 8388608
  13.1 34.3 %copy-start = (bf16[1,16,22,2560]{3,1,2,0:T(8,128)(2,1)S(1)}, bf16[1,16,22,2560]{3,1,2,0:T(8,128)(2,1)}, u32[]{:S(2)}) copy-start(bf16[1,16,22,2560]{3,1,2,0:T(8,128)(2,1)} %param.16) | copy-start | bytes 5406724
  13.1 34.3 %slice-start.1 = ((s8[7864320]{0:T(1024)(128)(4,1)}), s8[3670016]{0:T(1024)(128)(4,1)S(1)}, s32[]{:S(2)}) async-start(s8[7864320]{0:T(1024)(128)(4,1)} %bitcast.10), calls=%async_computation.2 | async-start | bytes 7340032
  13.1 34.3 %copy-start.4 = (bf16[352,384]{1,0:T(8,128)(2,1)S(1)}, bf16[352,384]{1,0:T(8,128)(2,1)}, u32[]{:S(2)}) copy-start(bf16[352,384]{1,0:T(8,128)(2,1)} %constant.31.clone.row_ref) | copy-start | bytes 811012
  13.1 34.3 %copy-start.5 = (bf16[128,1024]{1,0:T(8,128)(2,1)S(1)}, bf16[128,1024]{1,0:T(8,128)(2,1)}, u32[]{:S(2)}) copy-start(bf16[128,1024]{1,0:T(8,128)(2,1)} %constant.36.clone.join_ref) | copy-start | bytes 786436
  13.1 34.3 %copy-start.6 = (bf16[128,768]{1,0:T(8,128)(2,1)S(1)}, bf16[128,768]{1,0:T(8,128)(2,1)}, u32[]{:S(2)}) copy-start(bf16[128,768]{1,0:T(8,128)(2,1)} %constant.34.clone.gather_ref) | copy-start | bytes 589828
  13.2 34.3 %copy-start.7 = (f32[352,128]{1,0:T(8,128)S(1)}, f32[352,128]{1,0:T(8,128)}, u32[]{:S(2)}) copy-start(f32[352,128]{1,0:T(8,128)} %constant.33.clone.same_ref) | copy-start | bytes 540676
  13.2 34.3 %copy-start.8 = (bf16[352,256]{1,0:T(8,128)(2,1)S(1)}, bf16[352,256]{1,0:T(8,128)(2,1)}, u32[]{:S(2)}) copy-start(bf16[352,256]{1,0:T(8,128)(2,1)} %constant.32.clone.pick_ref) | copy-start | bytes 540676
  13.2 34.3 %copy-start.9 = (f32[128,256]{1,0:T(8,128)S(1)}, f32[128,256]{1,0:T(8,128)}, u32[]{:S(2)}) copy-start(f32[128,256]{1,0:T(8,128)} %constant.35.clone.part_ref) | copy-start | bytes 393220
  13.2 34.3 %copy-start.10 = (f32[8,3840]{1,0:T(8,128)S(1)}, f32[8,3840]{1,0:T(8,128)}, u32[]{:S(2)}) copy-start(f32[8,3840]{1,0:T(8,128)} %constant.38.clone.last_ref) | copy-start | bytes 368644
  13.2 34.3 %copy-start.11 = (bf16[128,256]{1,0:T(8,128)(2,1)S(1)}, bf16[128,256]{1,0:T(8,128)(2,1)}, u32[]{:S(2)}) copy-start(bf16[128,256]{1,0:T(8,128)(2,1)} %constant.37.clone.spread_ref) | copy-start | bytes 196612
  49.3 4.0 %collective-permute-start.1 = (bf16[22,640]{1,0:T(8,128)(2,1)S(1)}, bf16[22,640]{1,0:T(8,128)(2,1)S(1)}, u32[]{:S(2)}, u32[]{:S(2)}) collective-permute-start(bf16[22,640]{1,0:T(8,128)(2,1)S(1)} %get-tuple-element.21), channel_id=1, source_target_pairs={{0,64},{64,0},{128,192},{192,128},{1,65},{65,1},{129,193},{193,129... | collective-permute-start | bytes 84488 | tf_op jit(solution)/shard_map/ppermute | solution.py:340
  52.5 4.9 %collective-permute-start.2 = (bf16[22,640]{1,0:T(8,128)(2,1)S(1)}, bf16[22,640]{1,0:T(8,128)(2,1)S(1)}, u32[]{:S(2)}, u32[]{:S(2)}) collective-permute-start(bf16[22,640]{1,0:T(8,128)(2,1)S(1)} %get-tuple-element.23), channel_id=1, source_target_pairs={{0,64},{64,0},{128,192},{192,128},{1,65},{65,1},{129,193},{193,129... | collective-permute-start | bytes 84488 | tf_op jit(solution)/shard_map/ppermute | solution.py:340
  53.2 5.2 %collective-permute-start.3 = (bf16[22,640]{1,0:T(8,128)(2,1)S(1)}, bf16[22,640]{1,0:T(8,128)(2,1)S(1)}, u32[]{:S(2)}, u32[]{:S(2)}) collective-permute-start(bf16[22,640]{1,0:T(8,128)(2,1)S(1)} %add_convert_fusion), channel_id=1, source_target_pairs={{0,192},{64,128},{128,64},{192,0},{1,193},{65,129},{129,65},{193,1... | collective-permute-start | bytes 84488 | tf_op jit(solution)/shard_map/ppermute | solution.py:340

commit v6 on v5

--- a/solution.py
+++ b/solution.py
@@ -73,7 +73,7 @@
 @functools.lru_cache(None)
 def column_tables():
     waves = np.concatenate([first_wave(block) + np.arange(HALF) for block in range(GX)])
-    columns = np.arange(NX + 2 * CHUNK)
+    columns = np.arange(NX)
     cosine, sine = trig(waves, columns, NX)
     last = np.zeros((8, columns.size))
     last[0], last[1] = trig(np.array([KX // 2]), columns, NX)

time: 59.6 us -> 59.5 us (level)
  no operation moved by 1% of the time
where the time goes in v6:
time: 59.5 us; the launch traced here: 59 us
  blocking collectives  32.8 us (55%)
  starting transfers between devices  10.9 us (18%)
  Pallas kernels  6.4 us (11%)
  local copies, waits for them, and re-layouts  4.42 us (7%)
  waiting for transfers between devices  3.58 us (6%)
  other arithmetic  0.65 us (1%)
    all_to_all x1, blocking collectives, body(): lax.all_to_all(rows, ('gx', 'gy'), split_axis=0, concat_axis=0, tiled=True)  32.8 us
    ppermute x3, starting transfers between devices, ahead(): return lax.ppermute(piece, 'band', [(i, i ^ step) for i in range(BANDS)])  5.54 us
    ppermute x1, starting transfers between devices, body(): lax.ppermute(own[:, HALF * MEMBERS:], 'gx', [(i, GX - 1 - i) for i in ran...  5.38 us
    unnamed x32, local copies, waits for them, and re-layouts  3.39 us
    ppermute x1, waiting for transfers between devices, body(): lax.ppermute(own[:, HALF * MEMBERS:], 'gx', [(i, GX - 1 - i) for i in ran...  2.33 us
    pallas_call x1, Pallas kernels, body(): pl.pallas_call(far_kernel, out_shape=[jax.ShapeDtypeStruct((ROWS * M, KX)...  1.68 us
    pallas_call x1, Pallas kernels, body(): pl.pallas_call(near_kernel, out_shape=[sent, piece], in_specs=whole(6), o...  1.57 us
    pallas_call x1, Pallas kernels, body(): pl.pallas_call(rows_kernel, out_shape=jax.ShapeDtypeStruct((DESTS * PAD,...  1.31 us
  transfers between devices with their start and end apart: 4, of which 3 were waited for; matrix products, arithmetic and copies ran while one was open for 0% of the time, Pallas kernels for 6%

profile of v6, /device:TPU:2, one launch (start us, length us, event | category | flops | bytes accessed | tf_op | source)
XLA Modules:
  0.0 59.0 jit_solution(14796362429330192265)
XLA Ops:
  0.0 1.0 %reshape_squeeze.3.own_ref = bf16[2,256,256]{2,1,0:T(8,128)(2,1)S(1)} reshape(bf16[1,2,64,4,256]{4,3,2,1,0:T(4,128)(2,1)} %param.17) | data formatting | bytes 524288 | tf_op jit(solution)/shard_map/reshape;squeeze | solution.py:270
  1.0 5.4 %collective-permute-start = (bf16[2,128,256]{2,1,0:T(8,128)(2,1)S(1)}, bf16[2,128,256]{2,1,0:T(8,128)(2,1)S(1)}, u32[]{:S(2)}, u32[]{:S(2)}) collective-permute-start(bf16[2,128,256]{2,1,0:T(8,128)(2,1)S(1)} %slice.4), channel_id=1, source_target_pairs={{0,60},{4,56},{8,52},{12,48},{16,44},{20,40},{24,36},{28,32},{32,2... | collective-permute-start | bytes 393224 | tf_op jit(solution)/shard_map/ppermute | solution.py:271
  6.4 0.7 %copy-done.1 = s32[4]{0:T(128)S(1)} copy-done((s32[4]{0:T(128)S(1)}, s32[4]{0:T(128)}, u32[]{:S(2)}) %copy-start.1) | copy-done | bytes 40
  7.1 1.0 %copy-done.3 = bf16[2,256,384]{2,1,0:T(8,128)(2,1)S(1)} copy-done((bf16[2,256,384]{2,1,0:T(8,128)(2,1)S(1)}, bf16[2,256,384]{2,1,0:T(8,128)(2,1)}, u32[]{:S(2)}) %copy-start.3) | copy-done | bytes 393240
  8.1 0.8 %copy-done.12 = f32[2,32,256]{2,1,0:T(8,128)S(1)} copy-done((f32[2,32,256]{2,1,0:T(8,128)S(1)}, f32[2,32,256]{2,1,0:T(8,128)}, u32[]{:S(2)}) %copy-start.12) | copy-done | bytes 65560
  8.9 0.8 %copy-done.13 = bf16[64,512]{1,0:T(8,128)(2,1)S(1)} copy-done((bf16[64,512]{1,0:T(8,128)(2,1)S(1)}, bf16[64,512]{1,0:T(8,128)(2,1)}, u32[]{:S(2)}) %copy-start.13) | copy-done | bytes 65560
  9.8 1.0 %own_kernel.1 = (f32[2,256,256]{2,1,0:T(8,128)S(1)}, f32[64,256]{1,0:T(8,128)S(1)}, f32[8,128]{1,0:T(8,128)S(1)}) custom-call(s32[4]{0:T(128)S(1)} %copy-done.1, bf16[2,256,256]{2,1,0:T(8,128)(2,1)S(1)} %reshape_squeeze.3.own_ref, bf16[2,256,384]{2,1,0:T(8,128)(2,1)S(1)} %copy-done.3, bf16[64,512]{1,0:T(8,128)(2,1)S(1)} %copy-done.13, ...), custom_call_target="tpu_custom_call" | custom-call | flops 10000000000 | bytes 1048576 | tf_op jit(solution)/shard_map/own_kernel/pallas_call | solution.py:274
  10.8 2.3 %collective-permute-done.mirror_ref = bf16[2,128,256]{2,1,0:T(8,128)(2,1)S(1)} collective-permute-done((bf16[2,128,256]{2,1,0:T(8,128)(2,1)S(1)}, bf16[2,128,256]{2,1,0:T(8,128)(2,1)S(1)}, u32[]{:S(2)}, u32[]{:S(2)}) %collective-permute-start) | collective-permute-done | bytes 131104 | tf_op jit(solution)/shard_map/ppermute | solution.py:271
  13.1 0.0 copy-done.2
  13.1 0.0 copy-start.5
  13.1 0.0 copy-start.6
  13.2 0.0 copy-start.7
  13.2 0.0 copy-start.8
  13.2 0.0 copy-start.9
  13.2 0.0 copy-start.10
  13.2 0.0 copy-start.11
  13.2 1.3 %rows_kernel.1 = bf16[1536,256]{1,0:T(8,128)(2,1)S(1)} custom-call(s32[4]{0:T(128)S(1)} %copy-done.1, f32[2,256,256]{2,1,0:T(8,128)S(1)} %get-tuple-element.16.folded_ref, f32[64,256]{1,0:T(8,128)S(1)} %get-tuple-element.17.extra_ref, bf16[2,128,256]{2,1,0:T(8,128)(2,1)S(1)} %collective-permute-done.mirror_ref, bf16[2,256,384]{2,1,0:T(8,128)(2,1)S(1)} %copy-done.3, ...), custom_call_target="tpu_custom_call" | custom-call | flops 20000000000 | bytes 4194304 | tf_op jit(solution)/shard_map/rows_kernel/pallas_call | solution.py:287
  14.5 32.8 %all_to_all.11 = bf16[64,24,256]{2,1,0:T(8,128)(2,1)S(1)} all-to-all(bf16[64,24,256]{2,1,0:T(8,128)(2,1)S(1)} %bitcast.6), channel_id=1, replica_groups=mesh['band'=4,'gx'=16,'gy'=4] {'gx','gy'}, dimensions={0} | all-to-all | bytes 1572864 | tf_op jit(solution)/shard_map/all_to_all | solution.py:296
  47.3 0.0 slice-done
  47.3 0.0 copy-done
  47.3 0.0 slice-done.1
  47.3 0.0 copy-done.4
  47.4 1.7 %far_kernel.1 = (bf16[352,1024]{1,0:T(8,128)(2,1)S(1)}, f32[352,256]{1,0:T(8,128)S(1)}, bf16[22,640]{1,0:T(8,128)(2,1)S(1)}) custom-call(f32[8,128]{1,0:T(8,128)S(1)} %get-tuple-element.15.scale_ref, bf16[1536,256]{1,0:T(8,128)(2,1)S(1)} %bitcast.5, bf16[22,16,2560]{2,1,0:T(8,128)(2,1)S(1)} %bitcast.7, bf16[1024,2560]{1,0:T(8,128)(2,1)S(1)} %bitcast.11, ...), custom_call_target="tpu_custom_call" | custom-call | flops 3221225472 | bytes 8388608 | tf_op jit(solution)/shard_map/far_kernel/pallas_call | solution.py:300
  49.1 1.7 %collective-permute-start.1 = (bf16[22,640]{1,0:T(8,128)(2,1)S(1)}, bf16[22,640]{1,0:T(8,128)(2,1)S(1)}, u32[]{:S(2)}, u32[]{:S(2)}) collective-permute-start(bf16[22,640]{1,0:T(8,128)(2,1)S(1)} %get-tuple-element.21), channel_id=1, source_target_pairs={{0,64},{64,0},{128,192},{192,128},{1,65},{65,1},{129,193},{193,129... | collective-permute-start | bytes 84488 | tf_op jit(solution)/shard_map/ppermute | solution.py:340
  50.8 1.6 %near_kernel.1 = (bf16[22,640]{1,0:T(8,128)(2,1)S(1)}, f32[22,640]{1,0:T(8,128)S(1)}) custom-call(f32[8,128]{1,0:T(8,128)S(1)} %get-tuple-element.15.scale_ref, bf16[352,1024]{1,0:T(8,128)(2,1)S(1)} %get-tuple-element.22.joined_ref, f32[352,256]{1,0:T(8,128)S(1)} %get-tuple-element.19.edge_ref, bf16[22,16,2560]{2,1,0:T(8,128)(2,1)S(1)} %bitcast.8, ...), custom_call_target="tpu_custom_call" | custom-call | flops 10000000000 | bytes 4194304 | tf_op jit(solution)/shard_map/near_kernel/pallas_call | solution.py:314
  52.4 0.5 collective-permute-start.2
  52.9 0.2 collective-permute-done.1
  53.1 3.3 %collective-permute-start.3 = (bf16[22,640]{1,0:T(8,128)(2,1)S(1)}, bf16[22,640]{1,0:T(8,128)(2,1)S(1)}, u32[]{:S(2)}, u32[]{:S(2)}) collective-permute-start(bf16[22,640]{1,0:T(8,128)(2,1)S(1)} %add_convert_fusion), channel_id=1, source_target_pairs={{0,192},{64,128},{128,64},{192,0},{1,193},{65,129},{129,65},{193,1... | collective-permute-start | bytes 84488 | tf_op jit(solution)/shard_map/ppermute | solution.py:340
  56.4 0.8 %own_field_kernel.1 = f32[22,640]{1,0:T(8,128)S(1)} custom-call(f32[8,128]{1,0:T(8,128)S(1)} %get-tuple-element.15.scale_ref, bf16[352,1024]{1,0:T(8,128)(2,1)S(1)} %get-tuple-element.22.joined_ref, f32[352,256]{1,0:T(8,128)S(1)} %get-tuple-element.19.edge_ref, bf16[22,16,2560]{2,1,0:T(8,128)(2,1)S(1)} %bitcast.9, bf16[1024,2560]{1,0:T(8,128)(2,1)S(1)} %bitcast.11, ...), custom_call_target="tpu_custom_call" | custom-call | flops 10000000000 | bytes 4194304 | tf_op jit(solution)/shard_map/own_field_kernel/pallas_call | solution.py:327
  57.3 0.0 collective-permute-done.2
  57.3 1.0 %collective-permute-done.3 = bf16[22,640]{1,0:T(8,128)(2,1)S(1)} collective-permute-done((bf16[22,640]{1,0:T(8,128)(2,1)S(1)}, bf16[22,640]{1,0:T(8,128)(2,1)S(1)}, u32[]{:S(2)}, u32[]{:S(2)}) %collective-permute-start.3) | collective-permute-done | bytes 28192 | tf_op jit(solution)/shard_map/ppermute | solution.py:340
  58.3 0.6 %convert_add_fusion = f32[22,640]{1,0:T(8,128)} fusion(bf16[22,640]{1,0:T(8,128)(2,1)S(1)} %collective-permute-done.3, f32[22,640]{1,0:T(8,128)S(1)} %own_field_kernel.1, bf16[22,640]{1,0:T(8,128)(2,1)S(1)} %collective-permute-done.2), kind=kLoop, calls=%fused_computation | loop fusion | flops 56320 | bytes 168960 | tf_op jit(solution)/shard_map/add | solution.py:336
  (19 shorter events, 0.1 us)
Async XLA Ops:
  1.0 12.1 %collective-permute-start = (bf16[2,128,256]{2,1,0:T(8,128)(2,1)S(1)}, bf16[2,128,256]{2,1,0:T(8,128)(2,1)S(1)}, u32[]{:S(2)}, u32[]{:S(2)}) collective-permute-start(bf16[2,128,256]{2,1,0:T(8,128)(2,1)S(1)} %slice.4), channel_id=1, source_target_pairs={{0,60},{4,56},{8,52},{12,48},{16,44},{20,40},{24,36},{28,32},{32,2... | collective-permute-start | bytes 393224 | tf_op jit(solution)/shard_map/ppermute | solution.py:271
  6.4 0.7 %copy-start.1 = (s32[4]{0:T(128)S(1)}, s32[4]{0:T(128)}, u32[]{:S(2)}) copy-start(s32[4]{0:T(128)} %cut_ref.3) | copy-start | bytes 52
  7.1 1.0 %copy-start.3 = (bf16[2,256,384]{2,1,0:T(8,128)(2,1)S(1)}, bf16[2,256,384]{2,1,0:T(8,128)(2,1)}, u32[]{:S(2)}) copy-start(bf16[2,256,384]{2,1,0:T(8,128)(2,1)} %constant.26.clone.fold_ref) | copy-start | bytes 1179652
  8.1 0.8 %copy-start.12 = (f32[2,32,256]{2,1,0:T(8,128)S(1)}, f32[2,32,256]{2,1,0:T(8,128)}, u32[]{:S(2)}) copy-start(f32[2,32,256]{2,1,0:T(8,128)} %constant.28.clone.fine_ref) | copy-start | bytes 196612
  8.9 0.8 %copy-start.13 = (bf16[64,512]{1,0:T(8,128)(2,1)S(1)}, bf16[64,512]{1,0:T(8,128)(2,1)}, u32[]{:S(2)}) copy-start(bf16[64,512]{1,0:T(8,128)(2,1)} %constant.27.clone.coarse_ref) | copy-start | bytes 196612
  9.8 3.4 %copy-start.2 = (bf16[1536,512]{1,0:T(8,128)(2,1)S(1)}, bf16[1536,512]{1,0:T(8,128)(2,1)}, u32[]{:S(2)}) copy-start(bf16[1536,512]{1,0:T(8,128)(2,1)} %constant.29.clone.table_ref) | copy-start | bytes 4718596
  9.8 37.6 %slice-start = ((s8[5242880]{0:T(1024)(128)(4,1)}), s8[4194304]{0:T(1024)(128)(4,1)S(1)}, s32[]{:S(2)}) async-start(s8[5242880]{0:T(1024)(128)(4,1)} %bitcast.10), calls=%async_computation.1 | async-start | bytes 8388608
  13.1 34.2 %copy-start = (bf16[1,16,22,2560]{3,1,2,0:T(8,128)(2,1)S(1)}, bf16[1,16,22,2560]{3,1,2,0:T(8,128)(2,1)}, u32[]{:S(2)}) copy-start(bf16[1,16,22,2560]{3,1,2,0:T(8,128)(2,1)} %param.16) | copy-start | bytes 5406724
  13.1 34.2 %slice-start.1 = ((s8[5242880]{0:T(1024)(128)(4,1)}), s8[1048576]{0:T(1024)(128)(4,1)S(1)}, s32[]{:S(2)}) async-start(s8[5242880]{0:T(1024)(128)(4,1)} %bitcast.10), calls=%async_computation.2 | async-start | bytes 2097152
  13.1 34.2 %copy-start.4 = (bf16[352,384]{1,0:T(8,128)(2,1)S(1)}, bf16[352,384]{1,0:T(8,128)(2,1)}, u32[]{:S(2)}) copy-start(bf16[352,384]{1,0:T(8,128)(2,1)} %constant.31.clone.row_ref) | copy-start | bytes 811012
  13.1 34.2 %copy-start.5 = (bf16[128,1024]{1,0:T(8,128)(2,1)S(1)}, bf16[128,1024]{1,0:T(8,128)(2,1)}, u32[]{:S(2)}) copy-start(bf16[128,1024]{1,0:T(8,128)(2,1)} %constant.36.clone.join_ref) | copy-start | bytes 786436
  13.1 34.2 %copy-start.6 = (bf16[128,768]{1,0:T(8,128)(2,1)S(1)}, bf16[128,768]{1,0:T(8,128)(2,1)}, u32[]{:S(2)}) copy-start(bf16[128,768]{1,0:T(8,128)(2,1)} %constant.34.clone.gather_ref) | copy-start | bytes 589828
  13.2 34.2 %copy-start.7 = (f32[352,128]{1,0:T(8,128)S(1)}, f32[352,128]{1,0:T(8,128)}, u32[]{:S(2)}) copy-start(f32[352,128]{1,0:T(8,128)} %constant.33.clone.same_ref) | copy-start | bytes 540676
  13.2 34.2 %copy-start.8 = (bf16[352,256]{1,0:T(8,128)(2,1)S(1)}, bf16[352,256]{1,0:T(8,128)(2,1)}, u32[]{:S(2)}) copy-start(bf16[352,256]{1,0:T(8,128)(2,1)} %constant.32.clone.pick_ref) | copy-start | bytes 540676
  13.2 34.2 %copy-start.9 = (f32[128,256]{1,0:T(8,128)S(1)}, f32[128,256]{1,0:T(8,128)}, u32[]{:S(2)}) copy-start(f32[128,256]{1,0:T(8,128)} %constant.35.clone.part_ref) | copy-start | bytes 393220
  13.2 34.2 %copy-start.10 = (f32[8,2560]{1,0:T(8,128)S(1)}, f32[8,2560]{1,0:T(8,128)}, u32[]{:S(2)}) copy-start(f32[8,2560]{1,0:T(8,128)} %constant.38.clone.last_ref) | copy-start | bytes 245764
  13.2 34.2 %copy-start.11 = (bf16[128,256]{1,0:T(8,128)(2,1)S(1)}, bf16[128,256]{1,0:T(8,128)(2,1)}, u32[]{:S(2)}) copy-start(bf16[128,256]{1,0:T(8,128)(2,1)} %constant.37.clone.spread_ref) | copy-start | bytes 196612
  49.1 4.0 %collective-permute-start.1 = (bf16[22,640]{1,0:T(8,128)(2,1)S(1)}, bf16[22,640]{1,0:T(8,128)(2,1)S(1)}, u32[]{:S(2)}, u32[]{:S(2)}) collective-permute-start(bf16[22,640]{1,0:T(8,128)(2,1)S(1)} %get-tuple-element.21), channel_id=1, source_target_pairs={{0,64},{64,0},{128,192},{192,128},{1,65},{65,1},{129,193},{193,129... | collective-permute-start | bytes 84488 | tf_op jit(solution)/shard_map/ppermute | solution.py:340
  52.4 4.9 %collective-permute-start.2 = (bf16[22,640]{1,0:T(8,128)(2,1)S(1)}, bf16[22,640]{1,0:T(8,128)(2,1)S(1)}, u32[]{:S(2)}, u32[]{:S(2)}) collective-permute-start(bf16[22,640]{1,0:T(8,128)(2,1)S(1)} %get-tuple-element.23), channel_id=1, source_target_pairs={{0,64},{64,0},{128,192},{192,128},{1,65},{65,1},{129,193},{193,129... | collective-permute-start | bytes 84488 | tf_op jit(solution)/shard_map/ppermute | solution.py:340
  53.1 5.2 %collective-permute-start.3 = (bf16[22,640]{1,0:T(8,128)(2,1)S(1)}, bf16[22,640]{1,0:T(8,128)(2,1)S(1)}, u32[]{:S(2)}, u32[]{:S(2)}) collective-permute-start(bf16[22,640]{1,0:T(8,128)(2,1)S(1)} %add_convert_fusion), channel_id=1, source_target_pairs={{0,192},{64,128},{128,64},{192,0},{1,193},{65,129},{129,65},{193,1... | collective-permute-start | bytes 84488 | tf_op jit(solution)/shard_map/ppermute | solution.py:340

commit v7 on v6

--- a/solution.py
+++ b/solution.py
@@ -180,9 +180,9 @@
     with_cosine = jnp.concatenate([real[:half], imag[half:]], axis=0)
     with_sine = jnp.concatenate([-imag[:half], real[half:]], axis=0)
     weights = jnp.concatenate([with_cosine, with_sine], axis=1).astype(jnp.bfloat16)
-    dests = DESTS // 4
+    dests = DESTS // 2
     row = lax.broadcasted_iota(jnp.int32, (dests, PAD, 256), 1)
-    for part in range(4):
+    for part in range(2):
         rows = pl.ds(part * dests * PAD, dests * PAD)
         block = nt(table_ref[rows, :], weights).reshape(dests, PAD, 256)
         extra = extra_ref[part * dests : (part + 1) * dests, :].reshape(dests, 1, 256)
@@ -234,7 +234,7 @@
     ).astype(jnp.bfloat16)
     joined_ref[...] = joined
     edge = nn(edge, spread_ref[...])
-    edge_ref[...] = edge
+    edge_ref[...] = edge.astype(jnp.bfloat16)
     chunk = BANDS - 1 - (lax.axis_index("band") ^ 1)
     start = pl.multiple_of(chunk * CHUNK, CHUNK)
     alpha = nn(joined, table_ref[:, pl.ds(start, CHUNK)])
@@ -250,7 +250,7 @@
 def near_kernel(scale_ref, joined_ref, edge_ref, ensemble_ref, table_ref, last_ref, direct_ref, mirrored_ref):
     band = lax.axis_index("band")
     refs = (last_ref, ensemble_ref, table_ref, scale_ref)
-    joined, edge = joined_ref[...], edge_ref[...]
+    joined, edge = joined_ref[...], edge_ref[...].astype(jnp.float32)
     mirrored_ref[...] = chunk_field(BANDS - 1 - band, joined, edge, *refs)
     direct_ref[...] = chunk_field(band ^ 1, joined, edge, *refs).astype(direct_ref.dtype)
 
@@ -258,7 +258,7 @@
 def own_field_kernel(scale_ref, joined_ref, edge_ref, ensemble_ref, table_ref, last_ref, own_ref):
     band = lax.axis_index("band")
     own_ref[...] = chunk_field(
-        band, joined_ref[...], edge_ref[...], last_ref, ensemble_ref, table_ref, scale_ref
+        band, joined_ref[...], edge_ref[...].astype(jnp.float32), last_ref, ensemble_ref, table_ref, scale_ref
     )
 
 
@@ -301,7 +301,7 @@
         far_kernel,
         out_shape=[
             jax.ShapeDtypeStruct((ROWS * M, KX), jnp.bfloat16),
-            jax.ShapeDtypeStruct((ROWS * M, 256), jnp.float32),
+            jax.ShapeDtypeStruct((ROWS * M, 256), jnp.bfloat16),
             sent,
         ],
         in_specs=whole(12),

time: 59.5 us -> 59.5 us (level)
  no operation moved by 1% of the time
where the time goes in v7:
time: 59.5 us; the launch traced here: 58.9 us
  blocking collectives  32.8 us (55%)
  starting transfers between devices  10.9 us (18%)
  Pallas kernels  6.41 us (11%)
  local copies, waits for them, and re-layouts  4.42 us (7%)
  waiting for transfers between devices  3.57 us (6%)
  other arithmetic  0.65 us (1%)
    all_to_all x1, blocking collectives, body(): lax.all_to_all(rows, ('gx', 'gy'), split_axis=0, concat_axis=0, tiled=True)  32.8 us
    ppermute x3, starting transfers between devices, ahead(): return lax.ppermute(piece, 'band', [(i, i ^ step) for i in range(BANDS)])  5.5 us
    ppermute x1, starting transfers between devices, body(): lax.ppermute(own[:, HALF * MEMBERS:], 'gx', [(i, GX - 1 - i) for i in ran...  5.38 us
    unnamed x32, local copies, waits for them, and re-layouts  3.39 us
    ppermute x1, waiting for transfers between devices, body(): lax.ppermute(own[:, HALF * MEMBERS:], 'gx', [(i, GX - 1 - i) for i in ran...  2.33 us
    pallas_call x1, Pallas kernels, body(): pl.pallas_call(far_kernel, out_shape=[jax.ShapeDtypeStruct((ROWS * M, KX)...  1.68 us
    pallas_call x1, Pallas kernels, body(): pl.pallas_call(near_kernel, out_shape=[sent, piece], in_specs=whole(6), o...  1.56 us
    pallas_call x1, Pallas kernels, body(): pl.pallas_call(rows_kernel, out_shape=jax.ShapeDtypeStruct((DESTS * PAD,...  1.31 us
  transfers between devices with their start and end apart: 4, of which 3 were waited for; matrix products, arithmetic and copies ran while one was open for 0% of the time, Pallas kernels for 6%

profile of v7, /device:TPU:2, one launch (start us, length us, event | category | flops | bytes accessed | tf_op | source)
XLA Modules:
  0.0 58.9 jit_solution(6025646696822874006)
XLA Ops:
  0.0 1.0 %reshape_squeeze.3.own_ref = bf16[2,256,256]{2,1,0:T(8,128)(2,1)S(1)} reshape(bf16[1,2,64,4,256]{4,3,2,1,0:T(4,128)(2,1)} %param.17) | data formatting | bytes 524288 | tf_op jit(solution)/shard_map/reshape;squeeze | solution.py:270
  1.0 5.4 %collective-permute-start = (bf16[2,128,256]{2,1,0:T(8,128)(2,1)S(1)}, bf16[2,128,256]{2,1,0:T(8,128)(2,1)S(1)}, u32[]{:S(2)}, u32[]{:S(2)}) collective-permute-start(bf16[2,128,256]{2,1,0:T(8,128)(2,1)S(1)} %slice.4), channel_id=1, source_target_pairs={{0,60},{4,56},{8,52},{12,48},{16,44},{20,40},{24,36},{28,32},{32,2... | collective-permute-start | bytes 393224 | tf_op jit(solution)/shard_map/ppermute | solution.py:271
  6.4 0.7 %copy-done.1 = s32[4]{0:T(128)S(1)} copy-done((s32[4]{0:T(128)S(1)}, s32[4]{0:T(128)}, u32[]{:S(2)}) %copy-start.1) | copy-done | bytes 40
  7.1 1.0 %copy-done.3 = bf16[2,256,384]{2,1,0:T(8,128)(2,1)S(1)} copy-done((bf16[2,256,384]{2,1,0:T(8,128)(2,1)S(1)}, bf16[2,256,384]{2,1,0:T(8,128)(2,1)}, u32[]{:S(2)}) %copy-start.3) | copy-done | bytes 393240
  8.1 0.8 %copy-done.12 = f32[2,32,256]{2,1,0:T(8,128)S(1)} copy-done((f32[2,32,256]{2,1,0:T(8,128)S(1)}, f32[2,32,256]{2,1,0:T(8,128)}, u32[]{:S(2)}) %copy-start.12) | copy-done | bytes 65560
  8.9 0.8 %copy-done.13 = bf16[64,512]{1,0:T(8,128)(2,1)S(1)} copy-done((bf16[64,512]{1,0:T(8,128)(2,1)S(1)}, bf16[64,512]{1,0:T(8,128)(2,1)}, u32[]{:S(2)}) %copy-start.13) | copy-done | bytes 65560
  9.8 1.0 %own_kernel.1 = (f32[2,256,256]{2,1,0:T(8,128)S(1)}, f32[64,256]{1,0:T(8,128)S(1)}, f32[8,128]{1,0:T(8,128)S(1)}) custom-call(s32[4]{0:T(128)S(1)} %copy-done.1, bf16[2,256,256]{2,1,0:T(8,128)(2,1)S(1)} %reshape_squeeze.3.own_ref, bf16[2,256,384]{2,1,0:T(8,128)(2,1)S(1)} %copy-done.3, bf16[64,512]{1,0:T(8,128)(2,1)S(1)} %copy-done.13, ...), custom_call_target="tpu_custom_call" | custom-call | flops 10000000000 | bytes 1048576 | tf_op jit(solution)/shard_map/own_kernel/pallas_call | solution.py:274
  10.8 2.3 %collective-permute-done.mirror_ref = bf16[2,128,256]{2,1,0:T(8,128)(2,1)S(1)} collective-permute-done((bf16[2,128,256]{2,1,0:T(8,128)(2,1)S(1)}, bf16[2,128,256]{2,1,0:T(8,128)(2,1)S(1)}, u32[]{:S(2)}, u32[]{:S(2)}) %collective-permute-start) | collective-permute-done | bytes 131104 | tf_op jit(solution)/shard_map/ppermute | solution.py:271
  13.1 0.0 copy-done.2
  13.1 0.0 copy-start.5
  13.1 0.0 copy-start.6
  13.2 0.0 copy-start.7
  13.2 0.0 copy-start.8
  13.2 0.0 copy-start.9
  13.2 0.0 copy-start.10
  13.2 0.0 copy-start.11
  13.2 1.3 %rows_kernel.1 = bf16[1536,256]{1,0:T(8,128)(2,1)S(1)} custom-call(s32[4]{0:T(128)S(1)} %copy-done.1, f32[2,256,256]{2,1,0:T(8,128)S(1)} %get-tuple-element.16.folded_ref, f32[64,256]{1,0:T(8,128)S(1)} %get-tuple-element.17.extra_ref, bf16[2,128,256]{2,1,0:T(8,128)(2,1)S(1)} %collective-permute-done.mirror_ref, bf16[2,256,384]{2,1,0:T(8,128)(2,1)S(1)} %copy-done.3, ...), custom_call_target="tpu_custom_call" | custom-call | flops 20000000000 | bytes 4194304 | tf_op jit(solution)/shard_map/rows_kernel/pallas_call | solution.py:287
  14.5 32.8 %all_to_all.11 = bf16[64,24,256]{2,1,0:T(8,128)(2,1)S(1)} all-to-all(bf16[64,24,256]{2,1,0:T(8,128)(2,1)S(1)} %bitcast.6), channel_id=1, replica_groups=mesh['band'=4,'gx'=16,'gy'=4] {'gx','gy'}, dimensions={0} | all-to-all | bytes 1572864 | tf_op jit(solution)/shard_map/all_to_all | solution.py:296
  47.3 0.0 slice-done
  47.3 0.0 copy-done
  47.3 0.0 slice-done.1
  47.3 0.0 copy-done.4
  47.4 1.7 %far_kernel.1 = (bf16[352,1024]{1,0:T(8,128)(2,1)S(1)}, bf16[352,256]{1,0:T(8,128)(2,1)S(1)}, bf16[22,640]{1,0:T(8,128)(2,1)S(1)}) custom-call(f32[8,128]{1,0:T(8,128)S(1)} %get-tuple-element.15.scale_ref, bf16[1536,256]{1,0:T(8,128)(2,1)S(1)} %bitcast.5, bf16[22,16,2560]{2,1,0:T(8,128)(2,1)S(1)} %bitcast.7, bf16[1024,2560]{1,0:T(8,128)(2,1)S(1)} %bitcast.11, ...), custom_call_target="tpu_custom_call" | custom-call | flops 3221225472 | bytes 8388608 | tf_op jit(solution)/shard_map/far_kernel/pallas_call | solution.py:300
  49.1 1.7 %collective-permute-start.1 = (bf16[22,640]{1,0:T(8,128)(2,1)S(1)}, bf16[22,640]{1,0:T(8,128)(2,1)S(1)}, u32[]{:S(2)}, u32[]{:S(2)}) collective-permute-start(bf16[22,640]{1,0:T(8,128)(2,1)S(1)} %get-tuple-element.21), channel_id=1, source_target_pairs={{0,64},{64,0},{128,192},{192,128},{1,65},{65,1},{129,193},{193,129... | collective-permute-start | bytes 84488 | tf_op jit(solution)/shard_map/ppermute | solution.py:340
  50.8 1.6 %near_kernel.1 = (bf16[22,640]{1,0:T(8,128)(2,1)S(1)}, f32[22,640]{1,0:T(8,128)S(1)}) custom-call(f32[8,128]{1,0:T(8,128)S(1)} %get-tuple-element.15.scale_ref, bf16[352,1024]{1,0:T(8,128)(2,1)S(1)} %get-tuple-element.22.joined_ref, bf16[352,256]{1,0:T(8,128)(2,1)S(1)} %get-tuple-element.19.edge_ref, bf16[22,16,2560]{2,1,0:T(8,128)(2,1)S(1)} %bitcast.8, ...), custom_call_target="tpu_custom_call" | custom-call | flops 10000000000 | bytes 4194304 | tf_op jit(solution)/shard_map/near_kernel/pallas_call | solution.py:314
  52.4 0.5 collective-permute-start.2
  52.9 0.2 collective-permute-done.1
  53.1 3.3 %collective-permute-start.3 = (bf16[22,640]{1,0:T(8,128)(2,1)S(1)}, bf16[22,640]{1,0:T(8,128)(2,1)S(1)}, u32[]{:S(2)}, u32[]{:S(2)}) collective-permute-start(bf16[22,640]{1,0:T(8,128)(2,1)S(1)} %add_convert_fusion), channel_id=1, source_target_pairs={{0,192},{64,128},{128,64},{192,0},{1,193},{65,129},{129,65},{193,1... | collective-permute-start | bytes 84488 | tf_op jit(solution)/shard_map/ppermute | solution.py:340
  56.4 0.8 %own_field_kernel.1 = f32[22,640]{1,0:T(8,128)S(1)} custom-call(f32[8,128]{1,0:T(8,128)S(1)} %get-tuple-element.15.scale_ref, bf16[352,1024]{1,0:T(8,128)(2,1)S(1)} %get-tuple-element.22.joined_ref, bf16[352,256]{1,0:T(8,128)(2,1)S(1)} %get-tuple-element.19.edge_ref, bf16[22,16,2560]{2,1,0:T(8,128)(2,1)S(1)} %bitcast.9, bf16[1024,2560]{1,0:T(8,128)(2,1)S(1)} %bitcast.11, ...), custom_call_target="tpu_custom_call" | custom-call | flops 10000000000 | bytes 4194304 | tf_op jit(solution)/shard_map/own_field_kernel/pallas_call | solution.py:327
  57.2 0.0 collective-permute-done.2
  57.3 1.0 %collective-permute-done.3 = bf16[22,640]{1,0:T(8,128)(2,1)S(1)} collective-permute-done((bf16[22,640]{1,0:T(8,128)(2,1)S(1)}, bf16[22,640]{1,0:T(8,128)(2,1)S(1)}, u32[]{:S(2)}, u32[]{:S(2)}) %collective-permute-start.3) | collective-permute-done | bytes 28192 | tf_op jit(solution)/shard_map/ppermute | solution.py:340
  58.3 0.6 %convert_add_fusion = f32[22,640]{1,0:T(8,128)} fusion(bf16[22,640]{1,0:T(8,128)(2,1)S(1)} %collective-permute-done.3, f32[22,640]{1,0:T(8,128)S(1)} %own_field_kernel.1, bf16[22,640]{1,0:T(8,128)(2,1)S(1)} %collective-permute-done.2), kind=kLoop, calls=%fused_computation | loop fusion | flops 56320 | bytes 168960 | tf_op jit(solution)/shard_map/add | solution.py:336
  (19 shorter events, 0.0 us)
Async XLA Ops:
  1.0 12.1 %collective-permute-start = (bf16[2,128,256]{2,1,0:T(8,128)(2,1)S(1)}, bf16[2,128,256]{2,1,0:T(8,128)(2,1)S(1)}, u32[]{:S(2)}, u32[]{:S(2)}) collective-permute-start(bf16[2,128,256]{2,1,0:T(8,128)(2,1)S(1)} %slice.4), channel_id=1, source_target_pairs={{0,60},{4,56},{8,52},{12,48},{16,44},{20,40},{24,36},{28,32},{32,2... | collective-permute-start | bytes 393224 | tf_op jit(solution)/shard_map/ppermute | solution.py:271
  6.4 0.7 %copy-start.1 = (s32[4]{0:T(128)S(1)}, s32[4]{0:T(128)}, u32[]{:S(2)}) copy-start(s32[4]{0:T(128)} %cut_ref.3) | copy-start | bytes 52
  7.1 1.0 %copy-start.3 = (bf16[2,256,384]{2,1,0:T(8,128)(2,1)S(1)}, bf16[2,256,384]{2,1,0:T(8,128)(2,1)}, u32[]{:S(2)}) copy-start(bf16[2,256,384]{2,1,0:T(8,128)(2,1)} %constant.26.clone.fold_ref) | copy-start | bytes 1179652
  8.1 0.8 %copy-start.12 = (f32[2,32,256]{2,1,0:T(8,128)S(1)}, f32[2,32,256]{2,1,0:T(8,128)}, u32[]{:S(2)}) copy-start(f32[2,32,256]{2,1,0:T(8,128)} %constant.28.clone.fine_ref) | copy-start | bytes 196612
  8.9 0.8 %copy-start.13 = (bf16[64,512]{1,0:T(8,128)(2,1)S(1)}, bf16[64,512]{1,0:T(8,128)(2,1)}, u32[]{:S(2)}) copy-start(bf16[64,512]{1,0:T(8,128)(2,1)} %constant.27.clone.coarse_ref) | copy-start | bytes 196612
  9.8 3.4 %copy-start.2 = (bf16[1536,512]{1,0:T(8,128)(2,1)S(1)}, bf16[1536,512]{1,0:T(8,128)(2,1)}, u32[]{:S(2)}) copy-start(bf16[1536,512]{1,0:T(8,128)(2,1)} %constant.29.clone.table_ref) | copy-start | bytes 4718596
  9.8 37.6 %slice-start = ((s8[5242880]{0:T(1024)(128)(4,1)}), s8[4194304]{0:T(1024)(128)(4,1)S(1)}, s32[]{:S(2)}) async-start(s8[5242880]{0:T(1024)(128)(4,1)} %bitcast.10), calls=%async_computation.1 | async-start | bytes 8388608
  13.1 34.2 %copy-start = (bf16[1,16,22,2560]{3,1,2,0:T(8,128)(2,1)S(1)}, bf16[1,16,22,2560]{3,1,2,0:T(8,128)(2,1)}, u32[]{:S(2)}) copy-start(bf16[1,16,22,2560]{3,1,2,0:T(8,128)(2,1)} %param.16) | copy-start | bytes 5406724
  13.1 34.2 %slice-start.1 = ((s8[5242880]{0:T(1024)(128)(4,1)}), s8[1048576]{0:T(1024)(128)(4,1)S(1)}, s32[]{:S(2)}) async-start(s8[5242880]{0:T(1024)(128)(4,1)} %bitcast.10), calls=%async_computation.2 | async-start | bytes 2097152
  13.1 34.2 %copy-start.4 = (bf16[352,384]{1,0:T(8,128)(2,1)S(1)}, bf16[352,384]{1,0:T(8,128)(2,1)}, u32[]{:S(2)}) copy-start(bf16[352,384]{1,0:T(8,128)(2,1)} %constant.31.clone.row_ref) | copy-start | bytes 811012
  13.1 34.2 %copy-start.5 = (bf16[128,1024]{1,0:T(8,128)(2,1)S(1)}, bf16[128,1024]{1,0:T(8,128)(2,1)}, u32[]{:S(2)}) copy-start(bf16[128,1024]{1,0:T(8,128)(2,1)} %constant.36.clone.join_ref) | copy-start | bytes 786436
  13.1 34.2 %copy-start.6 = (bf16[128,768]{1,0:T(8,128)(2,1)S(1)}, bf16[128,768]{1,0:T(8,128)(2,1)}, u32[]{:S(2)}) copy-start(bf16[128,768]{1,0:T(8,128)(2,1)} %constant.34.clone.gather_ref) | copy-start | bytes 589828
  13.2 34.2 %copy-start.7 = (f32[352,128]{1,0:T(8,128)S(1)}, f32[352,128]{1,0:T(8,128)}, u32[]{:S(2)}) copy-start(f32[352,128]{1,0:T(8,128)} %constant.33.clone.same_ref) | copy-start | bytes 540676
  13.2 34.2 %copy-start.8 = (bf16[352,256]{1,0:T(8,128)(2,1)S(1)}, bf16[352,256]{1,0:T(8,128)(2,1)}, u32[]{:S(2)}) copy-start(bf16[352,256]{1,0:T(8,128)(2,1)} %constant.32.clone.pick_ref) | copy-start | bytes 540676
  13.2 34.2 %copy-start.9 = (f32[128,256]{1,0:T(8,128)S(1)}, f32[128,256]{1,0:T(8,128)}, u32[]{:S(2)}) copy-start(f32[128,256]{1,0:T(8,128)} %constant.35.clone.part_ref) | copy-start | bytes 393220
  13.2 34.2 %copy-start.10 = (f32[8,2560]{1,0:T(8,128)S(1)}, f32[8,2560]{1,0:T(8,128)}, u32[]{:S(2)}) copy-start(f32[8,2560]{1,0:T(8,128)} %constant.38.clone.last_ref) | copy-start | bytes 245764
  13.2 34.2 %copy-start.11 = (bf16[128,256]{1,0:T(8,128)(2,1)S(1)}, bf16[128,256]{1,0:T(8,128)(2,1)}, u32[]{:S(2)}) copy-start(bf16[128,256]{1,0:T(8,128)(2,1)} %constant.37.clone.spread_ref) | copy-start | bytes 196612
  49.1 4.0 %collective-permute-start.1 = (bf16[22,640]{1,0:T(8,128)(2,1)S(1)}, bf16[22,640]{1,0:T(8,128)(2,1)S(1)}, u32[]{:S(2)}, u32[]{:S(2)}) collective-permute-start(bf16[22,640]{1,0:T(8,128)(2,1)S(1)} %get-tuple-element.21), channel_id=1, source_target_pairs={{0,64},{64,0},{128,192},{192,128},{1,65},{65,1},{129,193},{193,129... | collective-permute-start | bytes 84488 | tf_op jit(solution)/shard_map/ppermute | solution.py:340
  52.4 4.9 %collective-permute-start.2 = (bf16[22,640]{1,0:T(8,128)(2,1)S(1)}, bf16[22,640]{1,0:T(8,128)(2,1)S(1)}, u32[]{:S(2)}, u32[]{:S(2)}) collective-permute-start(bf16[22,640]{1,0:T(8,128)(2,1)S(1)} %get-tuple-element.23), channel_id=1, source_target_pairs={{0,64},{64,0},{128,192},{192,128},{1,65},{65,1},{129,193},{193,129... | collective-permute-start | bytes 84488 | tf_op jit(solution)/shard_map/ppermute | solution.py:340
  53.1 5.2 %collective-permute-start.3 = (bf16[22,640]{1,0:T(8,128)(2,1)S(1)}, bf16[22,640]{1,0:T(8,128)(2,1)S(1)}, u32[]{:S(2)}, u32[]{:S(2)}) collective-permute-start(bf16[22,640]{1,0:T(8,128)(2,1)S(1)} %add_convert_fusion), channel_id=1, source_target_pairs={{0,192},{64,128},{128,64},{192,0},{1,193},{65,129},{129,65},{193,1... | collective-permute-start | bytes 84488 | tf_op jit(solution)/shard_map/ppermute | solution.py:340

commit v8 on v6

--- a/solution.py
+++ b/solution.py
@@ -268,7 +268,8 @@
 
 def body(ensemble, spectral, band_cut):
     own = spectral[0].reshape(2, WAVES * MEMBERS, KY)
-    mirror = lax.ppermute(own[:, HALF * MEMBERS :], "gx", [(i, GX - 1 - i) for i in range(GX)])
+    mirror = lax.ppermute(spectral[0, :, HALF:], "gx", [(i, GX - 1 - i) for i in range(GX)])
+    mirror = mirror.reshape(2, HALF * MEMBERS, KY)
     table_y, coarse, fine = row_tables()
     smem = pl.BlockSpec(memory_space=pltpu.SMEM)
     folded, extra, scale = pl.pallas_call(

time: 59.5 us -> 59.8 us (level)
  waiting for transfers between devices: 3.58 us -> 2.55 us
  local copies, waits for them, and re-layouts: 4.42 us -> 5.4 us
    ppermute x1, waiting for transfers between devices: 2.33 us -> 1.3 us  [body(): lax.ppermute(spectral[0, :, HALF:], 'gx', [(i, GX - 1 - i) for i in range...]
    squeeze x0 -> x1, local copies, waits for them, and re-layouts: none -> 0.95 us  [body(): spectral[0, :, HALF:]]
    unnamed x32 -> x34, local copies, waits for them, and re-layouts: 3.39 us -> 3.4 us
  transfers between devices with their start and end apart: 4 -> 4, of which waited for: 3 -> 3; matrix products, arithmetic and copies ran while one was open for 0% -> 2% of each run, Pallas kernels for 6% -> 6%
where the time goes in v8:
time: 59.8 us; the launch traced here: 59.2 us
  blocking collectives  33.1 us (55%)
  starting transfers between devices  10.9 us (18%)
  Pallas kernels  6.39 us (11%)
  local copies, waits for them, and re-layouts  5.4 us (9%)
  waiting for transfers between devices  2.55 us (4%)
  other arithmetic  0.65 us (1%)
    all_to_all x1, blocking collectives, body(): lax.all_to_all(rows, ('gx', 'gy'), split_axis=0, concat_axis=0, tiled=True)  33.1 us
    ppermute x3, starting transfers between devices, ahead(): return lax.ppermute(piece, 'band', [(i, i ^ step) for i in range(BANDS)])  5.55 us
    ppermute x1, starting transfers between devices, body(): lax.ppermute(spectral[0, :, HALF:], 'gx', [(i, GX - 1 - i) for i in range...  5.38 us
    unnamed x34, local copies, waits for them, and re-layouts  3.4 us
    pallas_call x1, Pallas kernels, body(): pl.pallas_call(far_kernel, out_shape=[jax.ShapeDtypeStruct((ROWS * M, KX)...  1.68 us
    pallas_call x1, Pallas kernels, body(): pl.pallas_call(near_kernel, out_shape=[sent, piece], in_specs=whole(6), o...  1.56 us
    pallas_call x1, Pallas kernels, body(): pl.pallas_call(rows_kernel, out_shape=jax.ShapeDtypeStruct((DESTS * PAD,...  1.3 us
    ppermute x1, waiting for transfers between devices, body(): lax.ppermute(spectral[0, :, HALF:], 'gx', [(i, GX - 1 - i) for i in range...  1.3 us
  transfers between devices with their start and end apart: 4, of which 3 were waited for; matrix products, arithmetic and copies ran while one was open for 2% of the time, Pallas kernels for 6%

profile of v8, /device:TPU:2, one launch (start us, length us, event | category | flops | bytes accessed | tf_op | source)
XLA Modules:
  0.0 59.2 jit_solution(16821505405675500419)
XLA Ops:
  0.0 1.0 %slice_bitcast_fusion = bf16[2,32,4,256]{3,2,1,0:T(4,128)(2,1)S(1)} fusion(bf16[1,2,64,4,256]{4,3,2,1,0:T(4,128)(2,1)} %param.17), kind=kLoop, calls=%fused_computation | loop fusion | bytes 262144 | tf_op jit(solution)/shard_map/squeeze | solution.py:271
  1.0 5.4 %collective-permute-start = (bf16[2,32,4,256]{3,2,1,0:T(4,128)(2,1)S(1)}, bf16[2,32,4,256]{3,2,1,0:T(4,128)(2,1)S(1)}, u32[]{:S(2)}, u32[]{:S(2)}) collective-permute-start(bf16[2,32,4,256]{3,2,1,0:T(4,128)(2,1)S(1)} %slice_bitcast_fusion), channel_id=1, source_target_pairs={{0,60},{4,56},{8,52},{12,48},{16,44},{20,40},{24,36},{28,32},{32,2... | collective-permute-start | bytes 393224 | tf_op jit(solution)/shard_map/ppermute | solution.py:271
  6.3 1.0 %reshape_squeeze.3.own_ref = bf16[2,256,256]{2,1,0:T(8,128)(2,1)S(1)} reshape(bf16[1,2,64,4,256]{4,3,2,1,0:T(4,128)(2,1)} %param.17) | data formatting | bytes 524288 | tf_op jit(solution)/shard_map/reshape;squeeze | solution.py:270
  7.4 0.0 copy-start.1
  7.4 0.6 %copy-done.1 = s32[4]{0:T(128)S(1)} copy-done((s32[4]{0:T(128)S(1)}, s32[4]{0:T(128)}, u32[]{:S(2)}) %copy-start.1) | copy-done | bytes 40
  8.0 1.0 %copy-done.5 = bf16[2,256,384]{2,1,0:T(8,128)(2,1)S(1)} copy-done((bf16[2,256,384]{2,1,0:T(8,128)(2,1)S(1)}, bf16[2,256,384]{2,1,0:T(8,128)(2,1)}, u32[]{:S(2)}) %copy-start.5) | copy-done | bytes 393240
  9.0 0.8 %copy-done.15 = f32[2,32,256]{2,1,0:T(8,128)S(1)} copy-done((f32[2,32,256]{2,1,0:T(8,128)S(1)}, f32[2,32,256]{2,1,0:T(8,128)}, u32[]{:S(2)}) %copy-start.15) | copy-done | bytes 65560
  9.9 0.8 %copy-done.16 = bf16[64,512]{1,0:T(8,128)(2,1)S(1)} copy-done((bf16[64,512]{1,0:T(8,128)(2,1)S(1)}, bf16[64,512]{1,0:T(8,128)(2,1)}, u32[]{:S(2)}) %copy-start.16) | copy-done | bytes 65560
  10.7 1.0 %own_kernel.1 = (f32[2,256,256]{2,1,0:T(8,128)S(1)}, f32[64,256]{1,0:T(8,128)S(1)}, f32[8,128]{1,0:T(8,128)S(1)}) custom-call(s32[4]{0:T(128)S(1)} %copy-done.1, bf16[2,256,256]{2,1,0:T(8,128)(2,1)S(1)} %reshape_squeeze.3.own_ref, bf16[2,256,384]{2,1,0:T(8,128)(2,1)S(1)} %copy-done.5, bf16[64,512]{1,0:T(8,128)(2,1)S(1)} %copy-done.16, ...), custom_call_target="tpu_custom_call" | custom-call | flops 10000000000 | bytes 1048576 | tf_op jit(solution)/shard_map/own_kernel/pallas_call | solution.py:275
  11.7 1.3 %collective-permute-done = bf16[2,32,4,256]{3,2,1,0:T(4,128)(2,1)S(1)} collective-permute-done((bf16[2,32,4,256]{3,2,1,0:T(4,128)(2,1)S(1)}, bf16[2,32,4,256]{3,2,1,0:T(4,128)(2,1)S(1)}, u32[]{:S(2)}, u32[]{:S(2)}) %collective-permute-start) | collective-permute-done | bytes 131104 | tf_op jit(solution)/shard_map/ppermute | solution.py:271
  13.1 0.0 copy-start
  13.1 0.0 copy-start.3
  13.1 0.0 copy-start.7
  13.1 0.0 copy-start.8
  13.2 0.0 copy-start.9
  13.2 0.0 copy-start.10
  13.2 0.0 copy-start.11
  13.2 0.0 copy-start.12
  13.2 0.0 copy-start.13
  13.2 0.0 copy-start.14
  13.2 1.3 %rows_kernel.1 = bf16[1536,256]{1,0:T(8,128)(2,1)S(1)} custom-call(s32[4]{0:T(128)S(1)} %copy-done.2, f32[2,256,256]{2,1,0:T(8,128)S(1)} %get-tuple-element.16.folded_ref, f32[64,256]{1,0:T(8,128)S(1)} %get-tuple-element.17.extra_ref, bf16[2,128,256]{2,1,0:T(8,128)(2,1)S(1)} %reshape.5.mirror_ref, bf16[2,256,384]{2,1,0:T(8,128)(2,1)S(1)} %copy-done.6, ...), custom_call_target="tpu_custom_call" | custom-call | flops 20000000000 | bytes 4194304 | tf_op jit(solution)/shard_map/rows_kernel/pallas_call | solution.py:288
  14.5 33.1 %all_to_all.11 = bf16[64,24,256]{2,1,0:T(8,128)(2,1)S(1)} all-to-all(bf16[64,24,256]{2,1,0:T(8,128)(2,1)S(1)} %bitcast.8), channel_id=1, replica_groups=mesh['band'=4,'gx'=16,'gy'=4] {'gx','gy'}, dimensions={0} | all-to-all | bytes 1572864 | tf_op jit(solution)/shard_map/all_to_all | solution.py:297
  47.7 1.7 %far_kernel.1 = (bf16[352,1024]{1,0:T(8,128)(2,1)S(1)}, f32[352,256]{1,0:T(8,128)S(1)}, bf16[22,640]{1,0:T(8,128)(2,1)S(1)}) custom-call(f32[8,128]{1,0:T(8,128)S(1)} %get-tuple-element.15.scale_ref, bf16[1536,256]{1,0:T(8,128)(2,1)S(1)} %bitcast.7, bf16[22,16,2560]{2,1,0:T(8,128)(2,1)S(1)} %bitcast.9, bf16[1024,2560]{1,0:T(8,128)(2,1)S(1)} %copy-done.3, ...), custom_call_target="tpu_custom_call" | custom-call | flops 3221225472 | bytes 8388608 | tf_op jit(solution)/shard_map/far_kernel/pallas_call | solution.py:301
  49.4 1.7 %collective-permute-start.1 = (bf16[22,640]{1,0:T(8,128)(2,1)S(1)}, bf16[22,640]{1,0:T(8,128)(2,1)S(1)}, u32[]{:S(2)}, u32[]{:S(2)}) collective-permute-start(bf16[22,640]{1,0:T(8,128)(2,1)S(1)} %get-tuple-element.21), channel_id=1, source_target_pairs={{0,64},{64,0},{128,192},{192,128},{1,65},{65,1},{129,193},{193,129... | collective-permute-start | bytes 84488 | tf_op jit(solution)/shard_map/ppermute | solution.py:341
  51.0 1.6 %near_kernel.1 = (bf16[22,640]{1,0:T(8,128)(2,1)S(1)}, f32[22,640]{1,0:T(8,128)S(1)}) custom-call(f32[8,128]{1,0:T(8,128)S(1)} %get-tuple-element.15.scale_ref, bf16[352,1024]{1,0:T(8,128)(2,1)S(1)} %get-tuple-element.22.joined_ref, f32[352,256]{1,0:T(8,128)S(1)} %get-tuple-element.19.edge_ref, bf16[22,16,2560]{2,1,0:T(8,128)(2,1)S(1)} %bitcast.10, ...), custom_call_target="tpu_custom_call" | custom-call | flops 10000000000 | bytes 4194304 | tf_op jit(solution)/shard_map/near_kernel/pallas_call | solution.py:315
  52.6 0.5 collective-permute-start.2
  53.1 0.2 collective-permute-done.1
  53.4 3.3 %collective-permute-start.3 = (bf16[22,640]{1,0:T(8,128)(2,1)S(1)}, bf16[22,640]{1,0:T(8,128)(2,1)S(1)}, u32[]{:S(2)}, u32[]{:S(2)}) collective-permute-start(bf16[22,640]{1,0:T(8,128)(2,1)S(1)} %add_convert_fusion), channel_id=1, source_target_pairs={{0,192},{64,128},{128,64},{192,0},{1,193},{65,129},{129,65},{193,1... | collective-permute-start | bytes 84488 | tf_op jit(solution)/shard_map/ppermute | solution.py:341
  56.7 0.8 %own_field_kernel.1 = f32[22,640]{1,0:T(8,128)S(1)} custom-call(f32[8,128]{1,0:T(8,128)S(1)} %get-tuple-element.15.scale_ref, bf16[352,1024]{1,0:T(8,128)(2,1)S(1)} %get-tuple-element.22.joined_ref, f32[352,256]{1,0:T(8,128)S(1)} %get-tuple-element.19.edge_ref, bf16[22,16,2560]{2,1,0:T(8,128)(2,1)S(1)} %bitcast.11, bf16[1024,2560]{1,0:T(8,128)(2,1)S(1)} %copy-done.3, ...), custom_call_target="tpu_custom_call" | custom-call | flops 10000000000 | bytes 4194304 | tf_op jit(solution)/shard_map/own_field_kernel/pallas_call | solution.py:328
  57.5 0.0 collective-permute-done.2
  57.5 1.0 %collective-permute-done.3 = bf16[22,640]{1,0:T(8,128)(2,1)S(1)} collective-permute-done((bf16[22,640]{1,0:T(8,128)(2,1)S(1)}, bf16[22,640]{1,0:T(8,128)(2,1)S(1)}, u32[]{:S(2)}, u32[]{:S(2)}) %collective-permute-start.3) | collective-permute-done | bytes 28192 | tf_op jit(solution)/shard_map/ppermute | solution.py:341
  58.6 0.6 %convert_add_fusion = f32[22,640]{1,0:T(8,128)} fusion(bf16[22,640]{1,0:T(8,128)(2,1)S(1)} %collective-permute-done.3, f32[22,640]{1,0:T(8,128)S(1)} %own_field_kernel.1, bf16[22,640]{1,0:T(8,128)(2,1)S(1)} %collective-permute-done.2), kind=kLoop, calls=%fused_computation.1 | loop fusion | flops 56320 | bytes 168960 | tf_op jit(solution)/shard_map/add | solution.py:337
  (21 shorter events, 0.1 us)
Async XLA Ops:
  1.0 12.1 %collective-permute-start = (bf16[2,32,4,256]{3,2,1,0:T(4,128)(2,1)S(1)}, bf16[2,32,4,256]{3,2,1,0:T(4,128)(2,1)S(1)}, u32[]{:S(2)}, u32[]{:S(2)}) collective-permute-start(bf16[2,32,4,256]{3,2,1,0:T(4,128)(2,1)S(1)} %slice_bitcast_fusion), channel_id=1, source_target_pairs={{0,60},{4,56},{8,52},{12,48},{16,44},{20,40},{24,36},{28,32},{32,2... | collective-permute-start | bytes 393224 | tf_op jit(solution)/shard_map/ppermute | solution.py:271
  7.4 0.7 %copy-start.1 = (s32[4]{0:T(128)S(1)}, s32[4]{0:T(128)}, u32[]{:S(2)}) copy-start(s32[4]{0:T(128)} %cut_ref.3) | copy-start | bytes 52
  8.0 1.0 %copy-start.5 = (bf16[2,256,384]{2,1,0:T(8,128)(2,1)S(1)}, bf16[2,256,384]{2,1,0:T(8,128)(2,1)}, u32[]{:S(2)}) copy-start(bf16[2,256,384]{2,1,0:T(8,128)(2,1)} %constant.26.clone.fold_ref) | copy-start | bytes 1179652
  9.0 0.8 %copy-start.15 = (f32[2,32,256]{2,1,0:T(8,128)S(1)}, f32[2,32,256]{2,1,0:T(8,128)}, u32[]{:S(2)}) copy-start(f32[2,32,256]{2,1,0:T(8,128)} %constant.28.clone.fine_ref) | copy-start | bytes 196612
  9.8 0.8 %copy-start.16 = (bf16[64,512]{1,0:T(8,128)(2,1)S(1)}, bf16[64,512]{1,0:T(8,128)(2,1)}, u32[]{:S(2)}) copy-start(bf16[64,512]{1,0:T(8,128)(2,1)} %constant.27.clone.coarse_ref) | copy-start | bytes 196612
  10.7 2.4 %copy-start.2 = (s32[4]{0:T(128)S(1)}, s32[4]{0:T(128)}, u32[]{:S(2)}) copy-start(s32[4]{0:T(128)} %cut_ref.3) | copy-start | bytes 52
  10.7 2.4 %copy-start.4 = (bf16[1536,512]{1,0:T(8,128)(2,1)S(1)}, bf16[1536,512]{1,0:T(8,128)(2,1)}, u32[]{:S(2)}) copy-start(bf16[1536,512]{1,0:T(8,128)(2,1)} %constant.29.clone.table_ref) | copy-start | bytes 4718596
  10.7 2.4 %copy-start.6 = (bf16[2,256,384]{2,1,0:T(8,128)(2,1)S(1)}, bf16[2,256,384]{2,1,0:T(8,128)(2,1)}, u32[]{:S(2)}) copy-start(bf16[2,256,384]{2,1,0:T(8,128)(2,1)} %constant.26.clone.fold_ref) | copy-start | bytes 1179652
  13.1 34.5 %copy-start = (bf16[1,16,22,2560]{3,1,2,0:T(8,128)(2,1)S(1)}, bf16[1,16,22,2560]{3,1,2,0:T(8,128)(2,1)}, u32[]{:S(2)}) copy-start(bf16[1,16,22,2560]{3,1,2,0:T(8,128)(2,1)} %param.16) | copy-start | bytes 5406724
  13.1 34.5 %copy-start.3 = (bf16[1024,2560]{1,0:T(8,128)(2,1)S(1)}, bf16[1024,2560]{1,0:T(8,128)(2,1)}, u32[]{:S(2)}) copy-start(bf16[1024,2560]{1,0:T(8,128)(2,1)} %constant.30.clone.table_ref) | copy-start | bytes 15728644
  13.1 34.5 %copy-start.7 = (bf16[352,384]{1,0:T(8,128)(2,1)S(1)}, bf16[352,384]{1,0:T(8,128)(2,1)}, u32[]{:S(2)}) copy-start(bf16[352,384]{1,0:T(8,128)(2,1)} %constant.31.clone.row_ref) | copy-start | bytes 811012
  13.1 34.5 %copy-start.8 = (bf16[128,1024]{1,0:T(8,128)(2,1)S(1)}, bf16[128,1024]{1,0:T(8,128)(2,1)}, u32[]{:S(2)}) copy-start(bf16[128,1024]{1,0:T(8,128)(2,1)} %constant.36.clone.join_ref) | copy-start | bytes 786436
  13.2 34.5 %copy-start.9 = (bf16[128,768]{1,0:T(8,128)(2,1)S(1)}, bf16[128,768]{1,0:T(8,128)(2,1)}, u32[]{:S(2)}) copy-start(bf16[128,768]{1,0:T(8,128)(2,1)} %constant.34.clone.gather_ref) | copy-start | bytes 589828
  13.2 34.5 %copy-start.10 = (f32[352,128]{1,0:T(8,128)S(1)}, f32[352,128]{1,0:T(8,128)}, u32[]{:S(2)}) copy-start(f32[352,128]{1,0:T(8,128)} %constant.33.clone.same_ref) | copy-start | bytes 540676
  13.2 34.5 %copy-start.11 = (bf16[352,256]{1,0:T(8,128)(2,1)S(1)}, bf16[352,256]{1,0:T(8,128)(2,1)}, u32[]{:S(2)}) copy-start(bf16[352,256]{1,0:T(8,128)(2,1)} %constant.32.clone.pick_ref) | copy-start | bytes 540676
  13.2 34.5 %copy-start.12 = (f32[128,256]{1,0:T(8,128)S(1)}, f32[128,256]{1,0:T(8,128)}, u32[]{:S(2)}) copy-start(f32[128,256]{1,0:T(8,128)} %constant.35.clone.part_ref) | copy-start | bytes 393220
  13.2 34.5 %copy-start.13 = (f32[8,2560]{1,0:T(8,128)S(1)}, f32[8,2560]{1,0:T(8,128)}, u32[]{:S(2)}) copy-start(f32[8,2560]{1,0:T(8,128)} %constant.38.clone.last_ref) | copy-start | bytes 245764
  13.2 34.4 %copy-start.14 = (bf16[128,256]{1,0:T(8,128)(2,1)S(1)}, bf16[128,256]{1,0:T(8,128)(2,1)}, u32[]{:S(2)}) copy-start(bf16[128,256]{1,0:T(8,128)(2,1)} %constant.37.clone.spread_ref) | copy-start | bytes 196612
  49.4 4.0 %collective-permute-start.1 = (bf16[22,640]{1,0:T(8,128)(2,1)S(1)}, bf16[22,640]{1,0:T(8,128)(2,1)S(1)}, u32[]{:S(2)}, u32[]{:S(2)}) collective-permute-start(bf16[22,640]{1,0:T(8,128)(2,1)S(1)} %get-tuple-element.21), channel_id=1, source_target_pairs={{0,64},{64,0},{128,192},{192,128},{1,65},{65,1},{129,193},{193,129... | collective-permute-start | bytes 84488 | tf_op jit(solution)/shard_map/ppermute | solution.py:341
  52.6 4.9 %collective-permute-start.2 = (bf16[22,640]{1,0:T(8,128)(2,1)S(1)}, bf16[22,640]{1,0:T(8,128)(2,1)S(1)}, u32[]{:S(2)}, u32[]{:S(2)}) collective-permute-start(bf16[22,640]{1,0:T(8,128)(2,1)S(1)} %get-tuple-element.23), channel_id=1, source_target_pairs={{0,64},{64,0},{128,192},{192,128},{1,65},{65,1},{129,193},{193,129... | collective-permute-start | bytes 84488 | tf_op jit(solution)/shard_map/ppermute | solution.py:341
  53.4 5.2 %collective-permute-start.3 = (bf16[22,640]{1,0:T(8,128)(2,1)S(1)}, bf16[22,640]{1,0:T(8,128)(2,1)S(1)}, u32[]{:S(2)}, u32[]{:S(2)}) collective-permute-start(bf16[22,640]{1,0:T(8,128)(2,1)S(1)} %add_convert_fusion), channel_id=1, source_target_pairs={{0,192},{64,128},{128,64},{192,0},{1,193},{65,129},{129,65},{193,1... | collective-permute-start | bytes 84488 | tf_op jit(solution)/shard_map/ppermute | solution.py:341
